TPU v7x, 256 devices: a whole 4x4x8 slice. The times are simulated.
256 devices in a mesh: dp: 128 (over z, x, y_lo, core), mp: 2 (over y_hi).
Axes of the slice: x: 4, y: 4 (y_hi: 2, y_lo: 2; y = y_hi * 2 + y_lo), z: 8, core: 2. Of those that a mesh axis runs over, the one named last changes fastest.
Arguments:
- images: bfloat16 [16384, 1152], P('dp', 'mp'), may hold values from -0.1796875 to 0.1796875
- text_feats: bfloat16 [16384, 1152], P('dp', 'mp'), may hold values from -0.1796875 to 0.1796875
- projection: bfloat16 [1152, 1152], P('mp'), may hold values from -0.1875 to 0.1875
- ranks: int32 [16384], P('dp'), may hold values from 0 to 16383, each once
Outputs:
- grad_image: float32 [16384, 1152], P('dp', 'mp')
- grad_text: float32 [16384, 1152], P('dp', 'mp')
- grad_weight: float32 [1152, 1152], P('mp')
Inputs may be any that keep to these rules, and one draw needn't show every extreme that they name: `ranks`: each of 0 to 16383 appears once.
All inputs are finite; a program needn't handle non-finite values.
Results may differ from a plain program's by a relative error of at most 0.015.
Values may be sent and summed in bfloat16 or wider, within the bound.
No kernel may reach another device: no remote copies, remote signals or barrier semaphores. Data moves between devices by JAX's collectives and lax.ppermute only.
A program may use at most 192 MiB of HBM per device.

v0:
```python
import jax
import jax.numpy as jnp
from jax import lax
from jax.sharding import PartitionSpec as P


def inner_rows(left, right):
    return lax.dot_general(
        left, right, (((1,), (1,)), ((), ())), preferred_element_type=jnp.float32
    )


def inner_cols(left, right):
    return lax.dot_general(
        left, right, (((0,), (0,)), ((), ())), preferred_element_type=jnp.float32
    )


def pair_coef(logits, own_weight, all_weight, offset, column_ids):
    rows_here = offset + jnp.arange(logits.shape[0], dtype=jnp.int32)
    diag = (rows_here[:, None] == column_ids[None, :]).astype(jnp.float32)
    scaled = own_weight.astype(jnp.float32)[:, None] * all_weight.astype(jnp.float32)[None, :]
    return (scaled * 10.0 * (jax.nn.sigmoid(logits) - diag)).astype(jnp.bfloat16)


def on_device(images, text_feats, projection, ranks):
    rows = images.shape[0]
    batch = rows * lax.axis_size("dp")
    weight = (0.5 + 1.5 * ranks.astype(jnp.float32) / (batch - 1)).astype(jnp.bfloat16)
    offset = lax.axis_index("dp") * rows
    partial_value = jnp.dot(text_feats, projection, preferred_element_type=jnp.float32)
    text_out = lax.psum_scatter(partial_value, "mp", scatter_dimension=1, tiled=True)
    img32 = images.astype(jnp.float32)
    img_sq, txt_sq = lax.psum(
        (jnp.sum(img32 * img32, axis=1), jnp.sum(text_out * text_out, axis=1)), "mp"
    )
    inv_img = lax.rsqrt(img_sq + 1e-06)
    inv_txt = lax.rsqrt(txt_sq + 1e-06)
    unit_img = img32 * inv_img[:, None]
    unit_txt = text_out * inv_txt[:, None]
    img_b = unit_img.astype(jnp.bfloat16)
    txt_b = unit_txt.astype(jnp.bfloat16)
    all_txt, all_weight = (
        lax.all_gather(txt_b, "dp", axis=0, tiled=True),
        lax.all_gather(weight, "dp", axis=0, tiled=True),
    )
    every_id = jnp.arange(all_txt.shape[0], dtype=jnp.int32)
    logits = (
        10.0 * lax.psum(inner_rows(img_b, all_txt).astype(jnp.bfloat16), "mp").astype(jnp.float32)
        - 2.0
    )
    coef = pair_coef(logits, weight, all_weight, offset, every_id)
    grad_uimg = jnp.dot(coef, all_txt, preferred_element_type=jnp.float32)
    grad_utxt = lax.psum_scatter(inner_cols(coef, img_b), "dp", scatter_dimension=0, tiled=True)
    img_dot, txt_dot = lax.psum(
        (jnp.sum(unit_img * grad_uimg, axis=1), jnp.sum(unit_txt * grad_utxt, axis=1)), "mp"
    )
    grad_image = (grad_uimg - unit_img * img_dot[:, None]) * inv_img[:, None]
    grad_out = ((grad_utxt - unit_txt * txt_dot[:, None]) * inv_txt[:, None]).astype(jnp.bfloat16)
    grad_full = lax.all_gather(grad_out, "mp", axis=1, tiled=True)
    grad_text = inner_rows(grad_full, projection)
    weight_part = inner_cols(text_feats, grad_full)
    grad_weight = lax.psum(weight_part, "dp")
    return (grad_image, grad_text, grad_weight)


def solution(mesh):
    return jax.shard_map(
        on_device,
        mesh=mesh,
        in_specs=(P("dp", "mp"), P("dp", "mp"), P("mp", None), P("dp")),
        out_specs=(P("dp", "mp"), P("dp", "mp"), P("mp", None)),
        check_vma=False,
    )
```

profile of v0, /device:TPU:1, one launch (start us, length us, event | category | flops | bytes accessed | tf_op | source)
XLA Modules:
  0.0 2210.0 jit_solution(16805450341812855556)
XLA Ops:
  7.2 0.0 reduce-scatter.3.cloned.1.call-start
  7.2 1.3 copy-done
  8.5 2.4 fusion.11
  10.9 0.0 reduce-scatter.3.cloned.1.call-update
  10.9 0.0 all-gather.3.cloned.1.call-start
  11.0 1.0 fusion.6
  12.0 24.8 %reduce-scatter.3.cloned.1.call-done = f32[128,576]{0,1:T(8,128)} async-done(((f32[128,1152]{0,1:T(8,128)}), f32[128,576]{0,1:T(8,128)}) %reduce-scatter.3.cloned.1.call-update) | async-done | bytes 294928 | tf_op jit(solution)/shard_map/reduce_scatter | solution.py:32
  36.8 1.1 multiply_reduce_fusion.1
  37.9 5.3 all-reduce.1
  43.2 1.6 multiply_convert_fusion.2
  44.8 0.0 all-gather.3.cloned.1.call-update
  44.8 0.0 all-reduce.5.cloned.1.call-start
  44.9 261.4 %all-gather.3.cloned.1.call-done = bf16[16384,576]{0,1:T(8,128)(2,1)} async-done(((bf16[128,576]{0,1:T(8,128)(2,1)}), bf16[16384,576]{0,1:T(8,128)(2,1)}) %all-gather.3.cloned.1.call-update) | async-done | bytes 18874384 | tf_op jit(solution)/shard_map/all_gather | solution.py:44
  306.4 12.0 convolution_convert_fusion
  318.3 0.0 all-reduce.5.cloned.1.call-update
  318.3 0.0 reduce-scatter.5.cloned.1.call-start
  318.4 154.3 %all-gather = bf16[128,1,128]{2,1,0:T(2,128)(2,1)S(1)} all-gather(bf16[1,1,128]{2,1,0:T(2,128)(2,1)S(1)} %get-tuple-element.8), channel_id=1, replica_groups=mesh['dp'=128,'mp'=2] {'dp'}, dimensions={0}, use_global_device_ids=true | all-gather | bytes 33024 | tf_op jit(solution)/shard_map/all_gather | solution.py:45
  472.7 0.1 convert_element_type.48
  472.8 0.0 all-reduce.5.cloned.1.call-done
  472.8 16.5 fusion.7
  489.4 0.2 all-reduce.7.cloned.1.call-start
  489.6 13.3 fusion.3
  502.9 609.7 %reduce-scatter.5.cloned.1.call-done = f32[128,576]{0,1:T(8,128)} async-done(((f32[16384,576]{0,1:T(8,128)}), f32[128,576]{0,1:T(8,128)}) %reduce-scatter.5.cloned.1.call-update) | async-done | bytes 294928 | tf_op jit(solution)/shard_map/reduce_scatter | solution.py:54
  1112.6 1.1 multiply_reduce_fusion
  1113.6 5.3 all-reduce
  1118.9 1.0 multiply_convert_fusion.1
  1120.0 6.2 all_gather.11
  1126.1 2.0 convolution_bitcast_fusion
  1128.2 0.8 fusion.5
  1128.9 1.2 fusion.12
  1130.2 1069.9 %all-reduce.7.cloned.1.call-done = f32[576,1152]{1,0:T(8,128)} async-done(((f32[576,1152]{1,0:T(8,128)}), f32[576,1152]{1,0:T(8,128)}) %all-reduce.7.cloned.1.call-update) | async-done | bytes 2654224 | tf_op jit(solution)/shard_map/psum | solution.py:63
  2200.0 3.4 copy.9
  (15 shorter events, 0.1 us)
Async XLA Ops:
  7.2 1.3 copy-start
  7.2 29.6 %reduce-scatter.3.cloned.1.call-start = ((), (), s32[]{:S(2)}) async-start(), calls=%async_computation.2 | async-start | bytes 884736 | tf_op jit(solution)/shard_map/reduce_scatter | solution.py:32
  10.9 295.4 %all-gather.3.cloned.1.call-start = ((), (), s32[]{:S(2)}) async-start(), calls=%async_computation.3 | async-start | bytes 19021824 | tf_op jit(solution)/shard_map/all_gather | solution.py:44
  44.8 428.0 %all-reduce.5.cloned.1.call-start = ((), (), s32[]{:S(2)}) async-start(), calls=%async_computation.4 | async-start | bytes 8388608 | tf_op jit(solution)/shard_map/psum | solution.py:49
  44.9 273.5 %copy-start.4 = (s32[128]{0:T(128)S(1)}, s32[128]{0:T(128)}, u32[]{:S(2)}) copy-start(s32[128]{0:T(128)} %param.7) | copy-start | bytes 1540
  44.9 427.9 %copy-start.2 = (bf16[128,576]{0,1:T(8,128)(2,1)S(1)}, bf16[128,576]{0,1:T(8,128)(2,1)}, u32[]{:S(2)}) copy-start(bf16[128,576]{0,1:T(8,128)(2,1)} %param.4) | copy-start | bytes 442372
  318.3 794.3 %reduce-scatter.5.cloned.1.call-start = ((), (), s32[]{:S(2)}) async-start(), calls=%async_computation.5 | async-start | bytes 38043648 | tf_op jit(solution)/shard_map/reduce_scatter | solution.py:54
  489.4 623.2 %copy-start.1 = (f32[128,576]{0,1:T(8,128)S(1)}, f32[128,576]{0,1:T(8,128)}, u32[]{:S(2)}) copy-start(f32[128,576]{0,1:T(8,128)} %reduce-scatter.3.cloned.1.call-done) | copy-start | bytes 884740
  489.4 636.7 %copy-start.3 = (bf16[128,576]{0,1:T(8,128)(2,1)S(1)}, bf16[128,576]{0,1:T(8,128)(2,1)}, u32[]{:S(2)}) copy-start(bf16[128,576]{0,1:T(8,128)(2,1)} %param.5) | copy-start | bytes 442372
  489.4 1710.6 %all-reduce.7.cloned.1.call-start = ((), (), s32[]{:S(2)}) async-start(), calls=%async_computation.6 | async-start | bytes 5308416 | tf_op jit(solution)/shard_map/psum | solution.py:63
Sparse Core Ops, SparseCore 0:
  11.1 25.6 reduce-scatter.2
  45.0 261.3 all-gather.2
  318.5 119.4 all-reduce.4
  489.5 623.0 reduce-scatter.4
  1128.3 1071.6 all-reduce.6
where the time goes:
time: 2210 us
  waiting for transfers between devices  1970 us (89%)
  blocking collectives  171 us (8%)
  matrix products  47.4 us (2%)
    psum x1, waiting for transfers between devices, on_device(): grad_weight = lax.psum(weight_part, 'dp')  1070 us
    reduce_scatter x1, waiting for transfers between devices, on_device(): lax.psum_scatter(inner_cols(coef, img_b), 'dp', scatter_dimension=0, tile...  610 us
    all_gather x1, waiting for transfers between devices, on_device(): lax.all_gather(txt_b, 'dp', axis=0, tiled=True)  261 us
    all_gather x1, blocking collectives, on_device(): lax.all_gather(weight, 'dp', axis=0, tiled=True)  154 us
  transfers between devices with their start and end apart: 5, of which 4 were waited for; matrix products, arithmetic and copies ran while one was open for 1% of the time, Pallas kernels for 0%

commit v1 on v0

v1 whole, which is shorter than its diff:
```python
import jax
import jax.numpy as jnp
from jax import lax
from jax.sharding import Mesh
from jax.sharding import PartitionSpec as P

FINE = ("z", "x", "yl", "c", "yh")
SIZES = (8, 4, 2, 2, 2)
DP = ("z", "x", "yl", "c")
IMG = ("z", "c")
TXT = ("x", "yl", "yh")
SWAP = [(0, 1), (1, 0)]
BF = jnp.bfloat16
F32 = jnp.float32


def contract(left, right, dims):
    return lax.dot_general(left, right, ((dims[:1], dims[1:]), ((), ())), preferred_element_type=F32)


def spread(block, axes, count):
    copies = jnp.broadcast_to(block[None], (count,) + block.shape)
    return lax.all_to_all(copies, axes, 0, 0)


def gather_sum(parts, axes):
    got = lax.all_to_all(parts, axes, 0, 0)
    return jnp.sum(got.astype(F32), axis=0)


def on_device(images, text_feats, projection, ranks):
    rows, half = images.shape
    own = rows // 2
    width = 2 * half
    n_dp = 128
    batch = rows * n_dp
    low = lax.axis_index("yh") == 0

    weight = (0.5 + 1.5 * ranks.astype(F32) / (batch - 1)).astype(BF)
    weight = jnp.where(low, weight[:own], weight[own:])
    partial = jnp.dot(text_feats, projection, preferred_element_type=F32)
    send = jnp.concatenate(
        [
            jnp.where(low, images[own:], images[:own]),
            jnp.where(low, partial[own:], partial[:own]).astype(BF),
        ],
        axis=1,
    )
    got = lax.ppermute(send, "yh", SWAP)
    text_out = jnp.where(low, partial[:own], partial[own:]) + got[:, half:].astype(F32)
    img_own = jnp.where(low, images[:own], images[own:])
    img_got = got[:, :half]
    img32 = jnp.concatenate(
        [jnp.where(low, img_own, img_got), jnp.where(low, img_got, img_own)], axis=1
    ).astype(F32)
    inv_img = lax.rsqrt(jnp.sum(img32 * img32, axis=1, keepdims=True) + 1e-06)
    inv_txt = lax.rsqrt(jnp.sum(text_out * text_out, axis=1, keepdims=True) + 1e-06)
    unit_img = img32 * inv_img
    unit_txt = text_out * inv_txt
    img_b = unit_img.astype(BF)
    txt_b = unit_txt.astype(BF)

    column = jnp.pad(weight[:, None], ((0, 0), (0, 127)))
    all_img = lax.all_gather(jnp.concatenate([img_b, column], axis=1), IMG, axis=0, tiled=True)
    all_txt = spread(jnp.concatenate([txt_b, column], axis=1), TXT, 16).reshape(16 * own, width + 128)

    blk_img, w_img = all_img[:, :width], all_img[:, width:]
    blk_txt, w_txt = all_txt[:, :width], all_txt[:, width:]
    logits = 10.0 * contract(blk_img, blk_txt, (1, 1)) - 2.0
    pair = w_img[:, :1].astype(F32) * w_txt[:, 0].astype(F32)[None, :]
    coef = (pair * 10.0 * jax.nn.sigmoid(logits)).astype(BF)
    part_img = jnp.dot(coef, blk_txt, preferred_element_type=F32).astype(BF)
    part_txt = contract(coef, blk_img, (0, 0)).astype(BF)

    w32 = weight.astype(F32)[:, None]
    diag = 10.0 * w32 * w32
    grad_utxt = gather_sum(part_txt.reshape(16, own, width), TXT) - diag * img_b.astype(F32)
    txt_dot = jnp.sum(unit_txt * grad_utxt, axis=1, keepdims=True)
    grad_out = ((grad_utxt - unit_txt * txt_dot) * inv_txt).astype(BF)
    other = lax.ppermute(grad_out, "yh", SWAP)
    grad_full = jnp.concatenate(
        [jnp.where(low, grad_out, other), jnp.where(low, other, grad_out)], axis=0
    )
    weight_part = contract(text_feats, grad_full, (0, 0)).astype(BF)
    grad_text = contract(grad_full, projection, (1, 1))

    tiles = weight_part.reshape(half // 8, 8, width // 128, 128).transpose(0, 2, 1, 3)
    tiles = tiles.reshape(-1, 8, 128)
    n_tiles = tiles.shape[0]
    share = -(-n_tiles // n_dp)
    tiles = jnp.pad(tiles, ((0, share * n_dp - n_tiles), (0, 0), (0, 0)))
    mine = gather_sum(tiles.reshape(n_dp, share, 8, 128), DP).astype(BF)
    whole = spread(mine, DP, n_dp).reshape(-1, 8, 128)[:n_tiles]
    grad_weight = (
        whole.reshape(half // 8, width // 128, 8, 128).transpose(0, 2, 1, 3).reshape(half, width)
    ).astype(F32)

    grad_uimg = lax.psum_scatter(part_img, IMG, scatter_dimension=0, tiled=True).astype(F32)
    grad_uimg = grad_uimg - diag * txt_b.astype(F32)
    img_dot = jnp.sum(unit_img * grad_uimg, axis=1, keepdims=True)
    grad_img = (grad_uimg - unit_img * img_dot) * inv_img
    left, right = grad_img[:, :half], grad_img[:, half:]
    back = lax.ppermute(jnp.where(low, right, left).astype(BF), "yh", SWAP).astype(F32)
    keep = jnp.where(low, left, right)
    grad_image = jnp.concatenate(
        [jnp.where(low, keep, back), jnp.where(low, back, keep)], axis=0
    )
    return (grad_image, grad_text, grad_weight)


def solution(mesh):
    fine = Mesh(mesh.devices.reshape(SIZES), FINE)
    return jax.shard_map(
        on_device,
        mesh=fine,
        in_specs=(P(DP, "yh"), P(DP, "yh"), P("yh", None), P(DP)),
        out_specs=(P(DP, "yh"), P(DP, "yh"), P("yh", None)),
        check_vma=False,
    )
```

time: 2210 us -> 257 us (0.12)
  waiting for transfers between devices: 1970 us -> 59.3 us
  blocking collectives: 171 us -> 129 us
  matrix products: 47.4 us -> 21.5 us
    psum x2 -> x0, waiting for transfers between devices: 1070 us -> none  [the longest x1 1070 us: on_device(): grad_weight = lax.psum(weight_part, 'dp')]
    reduce_scatter x2 -> x1, waiting for transfers between devices: 635 us -> 14.5 us  [on_device(): lax.psum_scatter(part_img, IMG, scatter_dimension=0, tiled=True).astype(F32)]
    all_gather x1, waiting for transfers between devices: 261 us -> 4.74 us  [on_device(): lax.all_gather(jnp.concatenate([img_b, column], axis=1), IMG, axis=0, til...]
    all_gather x2 -> x0, blocking collectives: 160 us -> none  [the longest x1 154 us: on_device(): lax.all_gather(weight, 'dp', axis=0, tiled=True)]
    all_to_all x0 -> x3, blocking collectives: none -> 129 us  [the longest x2 89.7 us: gather_sum(): got = lax.all_to_all(parts, axes, 0, 0)]
    all_to_all x0 -> x1, waiting for transfers between devices: none -> 28 us  [spread(): return lax.all_to_all(copies, axes, 0, 0)]
    dot_general x6, matrix products: 47.4 us -> 21.5 us  [the longest x4 14.3 us: contract(): lax.dot_general(left, right, ((dims[:1], dims[1:]), ((), ())), preferred_...]
  transfers between devices with their start and end apart: 5 -> 6, of which waited for: 4 -> 6; matrix products, arithmetic and copies ran while one was open for 1% -> 4% of each run, Pallas kernels for 0% -> 0%
where the time goes in v1:
time: 257 us; the launch traced here: 256 us
  blocking collectives  129 us (50%)
  waiting for transfers between devices  59.3 us (23%)
  matrix products  21.5 us (8%)
  starting transfers between devices  17.1 us (7%)
  between operations  14.2 us (6%)
  other arithmetic  8.35 us (3%)
  local copies, waits for them, and re-layouts  6.73 us (3%)
    all_to_all x2, blocking collectives, gather_sum(): got = lax.all_to_all(parts, axes, 0, 0)  89.7 us
    all_to_all x1, blocking collectives, spread(): return lax.all_to_all(copies, axes, 0, 0)  39 us
    all_to_all x1, waiting for transfers between devices, spread(): return lax.all_to_all(copies, axes, 0, 0)  28 us
    reduce_scatter x1, waiting for transfers between devices, on_device(): lax.psum_scatter(part_img, IMG, scatter_dimension=0, tiled=True).astype(F32)  14.5 us
    dot_general x4, matrix products, contract(): lax.dot_general(left, right, ((dims[:1], dims[1:]), ((), ())), preferred_...  14.3 us
    all_to_all x1, starting transfers between devices, spread(): return lax.all_to_all(copies, axes, 0, 0)  7.8 us
    dot_general x1, matrix products, on_device(): part_img = jnp.dot(coef, blk_txt, preferred_element_type=F32).astype(BF)  5.87 us
  transfers between devices with their start and end apart: 6, of which 6 were waited for; matrix products, arithmetic and copies ran while one was open for 4% of the time, Pallas kernels for 0%

profile of v1, /device:TPU:1, one launch (start us, length us, event | category | flops | bytes accessed | tf_op | source)
XLA Modules:
  0.0 255.9 jit_solution(15985526926018484129)
XLA Ops:
  7.2 1.2 fusion.17
  8.7 1.4 fusion.18
  10.3 3.8 %collective-permute-start = (bf16[64,1728]{1,0:T(8,128)(2,1)S(1)}, bf16[64,1728]{1,0:T(8,128)(2,1)S(1)}, u32[]{:S(2)}, u32[]{:S(2)}) collective-permute-start(bf16[64,1728]{1,0:T(8,128)(2,1)S(1)} %pad_maximum_fusion.2), channel_id=1, source_target_pairs={{0,1},{1,0},{2,3},{3,2},{4,5},{5,4},{6,7},{7,6},{8,9},{9,8},{10,11... | collective-permute-start | bytes 663560 | tf_op jit(solution)/shard_map/ppermute | solution.py:49
  14.3 4.1 %collective-permute-done = bf16[64,1728]{1,0:T(8,128)(2,1)S(1)} collective-permute-done((bf16[64,1728]{1,0:T(8,128)(2,1)S(1)}, bf16[64,1728]{1,0:T(8,128)(2,1)S(1)}, u32[]{:S(2)}, u32[]{:S(2)}) %collective-permute-start) | collective-permute-done | bytes 221216 | tf_op jit(solution)/shard_map/ppermute | solution.py:49
  19.0 0.7 fusion.13
  19.7 0.2 broadcast_in_dim.7
  20.0 39.0 %all_to_all.20 = bf16[16,64,1280]{2,1,0:T(8,128)(2,1)S(1)} all-to-all(bf16[16,64,1280]{2,1,0:T(8,128)(2,1)S(1)} %broadcast_in_dim.7), channel_id=1, replica_groups=mesh['z'=8,'x'=4,'yl'=2,'c'=2,'yh'=2] {'x','yl','yh'}, dimensions={0} | all-to-all | bytes 5242880 | tf_op jit(solution)/shard_map/all_to_all | solution.py:23
  59.0 1.5 copy-done.1
  60.6 4.7 %all-gather.2.cloned.1.call-done = bf16[1024,1280]{1,0:T(8,128)(2,1)} async-done(((bf16[64,1280]{1,0:T(8,128)(2,1)}), bf16[1024,1280]{1,0:T(8,128)(2,1)}) %all-gather.2.cloned.1.call-update) | async-done | bytes 2621456 | tf_op jit(solution)/shard_map/all_gather | solution.py:64
  65.3 1.1 convert_reduce_fusion.2
  66.5 7.3 %multiply_convert_fusion = bf16[1024,1024]{1,0:T(8,128)(2,1)} fusion(f32[1024]{0:T(1024)S(1)} %convert_reduce_fusion.1, f32[1024]{0:T(1024)S(1)} %convert_reduce_fusion.2, bf16[1024,1280]{1,0:T(8,128)(2,1)} %bitcast.27, bf16[1024,1280]{1,0:T(8,128)(2,1)} %all-gather.2.cloned.1.call-done), kind=kOutput, calls=%fused_computation.1 | convolution fusion | flops 2425356288 | bytes 6823936 | tf_op jit(solution)/shard_map/dot_general | solution.py:18
  73.8 5.9 %convolution_convert_fusion.1 = bf16[1024,1152]{1,0:T(8,128)(2,1)} fusion(bf16[1024,1024]{1,0:T(8,128)(2,1)} %multiply_convert_fusion, bf16[1024,1280]{1,0:T(8,128)(2,1)S(1)} %bitcast.28), kind=kOutput, calls=%fused_computation.3 | convolution fusion | flops 2417098752 | bytes 6815744 | tf_op jit(solution)/shard_map/dot_general | solution.py:72
  79.7 5.2 %convolution_convert_fusion = bf16[1024,1152]{1,0:T(8,128)(2,1)S(1)} fusion(bf16[1024,1024]{1,0:T(8,128)(2,1)} %multiply_convert_fusion, bf16[1024,1280]{1,0:T(8,128)(2,1)} %all-gather.2.cloned.1.call-done), kind=kOutput, calls=%fused_computation.2 | convolution fusion | flops 2417098752 | bytes 6815744 | tf_op jit(solution)/shard_map/dot_general | solution.py:18
  84.9 36.9 %all_to_all.21 = bf16[16,64,1152]{2,1,0:T(8,128)(2,1)S(1)} all-to-all(bf16[16,64,1152]{2,1,0:T(8,128)(2,1)S(1)} %bitcast.29), channel_id=1, replica_groups=mesh['z'=8,'x'=4,'yl'=2,'c'=2,'yh'=2] {'x','yl','yh'}, dimensions={0} | all-to-all | bytes 4718592 | tf_op jit(solution)/shard_map/all_to_all | solution.py:27
  121.8 0.3 convert_reduce_fusion
  122.1 14.5 %reduce-scatter.2.cloned.1.call-done = bf16[64,1152]{1,0:T(8,128)(2,1)} async-done(((bf16[1024,1152]{1,0:T(8,128)(2,1)}), bf16[64,1152]{1,0:T(8,128)(2,1)}) %reduce-scatter.2.cloned.1.call-update) | async-done | bytes 147472 | tf_op jit(solution)/shard_map/reduce_scatter | solution.py:98
  136.6 1.2 multiply_reduce_fusion
  137.9 1.1 multiply_convert_fusion.1
  139.0 2.8 %collective-permute-start.2 = (bf16[64,1152]{1,0:T(8,128)(2,1)S(1)}, bf16[64,1152]{1,0:T(8,128)(2,1)S(1)}, u32[]{:S(2)}, u32[]{:S(2)}) collective-permute-start(bf16[64,1152]{1,0:T(8,128)(2,1)S(1)} %get-tuple-element.28), channel_id=1, source_target_pairs={{0,1},{1,0},{2,3},{3,2},{4,5},{5,4},{6,7},{7,6},{8,9},{9,8},{10,11... | collective-permute-start | bytes 442376 | tf_op jit(solution)/shard_map/ppermute | solution.py:80
  141.8 2.9 %collective-permute-done.2 = bf16[64,1152]{1,0:T(8,128)(2,1)S(1)} collective-permute-done((bf16[64,1152]{1,0:T(8,128)(2,1)S(1)}, bf16[64,1152]{1,0:T(8,128)(2,1)S(1)}, u32[]{:S(2)}, u32[]{:S(2)}) %collective-permute-start.2) | collective-permute-done | bytes 147488 | tf_op jit(solution)/shard_map/ppermute | solution.py:80
  144.8 0.5 convolution_convert_fusion.2
  145.4 52.9 %all_to_all.22 = bf16[128,6,8,128]{3,2,1,0:T(8,128)(2,1)S(1)} all-to-all(bf16[128,6,8,128]{3,2,1,0:T(8,128)(2,1)S(1)} %bitcast.23), channel_id=1, replica_groups=mesh['z'=8,'x'=4,'yl'=2,'c'=2,'yh'=2] {'z','x','yl','c'}, dimensions={0} | all-to-all | bytes 3145728 | tf_op jit(solution)/shard_map/all_to_all | solution.py:27
  198.3 0.3 reduce_sum.62
  198.6 1.3 broadcast_in_dim.8
  199.9 7.8 %all-to-all-start.3 = ((bf16[128,6,8,128]{3,2,1,0:T(8,128)(2,1)}), bf16[128,6,8,128]{3,2,1,0:T(8,128)(2,1)S(1)}, u32[]{:S(2)}, u32[]{:S(2)}) async-start(bf16[128,6,8,128]{3,2,1,0:T(8,128)(2,1)} %broadcast_in_dim.8), calls=%async_computation.4 | async-start | bytes 3145728 | tf_op jit(solution)/shard_map/all_to_all | solution.py:23
  207.8 2.6 %collective-permute-start.1 = (bf16[64,576]{1,0:T(8,128)(2,1)S(1)}, bf16[64,576]{1,0:T(8,128)(2,1)S(1)}, u32[]{:S(2)}, u32[]{:S(2)}) collective-permute-start(bf16[64,576]{1,0:T(8,128)(2,1)S(1)} %select_convert_fusion.1), channel_id=1, source_target_pairs={{0,1},{1,0},{2,3},{3,2},{4,5},{5,4},{6,7},{7,6},{8,9},{9,8},{10,11... | collective-permute-start | bytes 221192 | tf_op jit(solution)/shard_map/ppermute | solution.py:103
  210.4 5.0 %collective-permute-done.1 = bf16[64,576]{1,0:T(8,128)(2,1)S(1)} collective-permute-done((bf16[64,576]{1,0:T(8,128)(2,1)S(1)}, bf16[64,576]{1,0:T(8,128)(2,1)S(1)}, u32[]{:S(2)}, u32[]{:S(2)}) %collective-permute-start.1) | collective-permute-done | bytes 73760 | tf_op jit(solution)/shard_map/ppermute | solution.py:103
  215.5 0.7 pad_maximum_fusion
  216.3 1.8 copy.19
  218.1 1.2 fusion.12
  219.3 28.0 %all-to-all-done.3 = bf16[128,6,8,128]{3,2,1,0:T(8,128)(2,1)S(1)} async-done(((bf16[128,6,8,128]{3,2,1,0:T(8,128)(2,1)}), bf16[128,6,8,128]{3,2,1,0:T(8,128)(2,1)S(1)}, u32[]{:S(2)}, u32[]{:S(2)}) %all-to-all-start.3) | async-done | bytes 1572896 | tf_op jit(solution)/shard_map/all_to_all | solution.py:23
  247.4 1.7 convert_bitcast_fusion
  (33 shorter events, 1.9 us)
Async XLA Ops:
  7.2 1.6 copy-start
  7.2 6.9 %copy-start.4 = (s32[128]{0:T(128)S(1)}, s32[128]{0:T(128)}, u32[]{:S(2)}) copy-start(s32[128]{0:T(128)} %param.7) | copy-start | bytes 1540
  7.2 58.2 %all-gather.2.cloned.1.call-start = ((), (), s32[]{:S(2)}) async-start(), calls=%async_computation.5 | async-start | bytes 2785280 | tf_op jit(solution)/shard_map/all_gather | solution.py:64
  10.3 8.1 %collective-permute-start = (bf16[64,1728]{1,0:T(8,128)(2,1)S(1)}, bf16[64,1728]{1,0:T(8,128)(2,1)S(1)}, u32[]{:S(2)}, u32[]{:S(2)}) collective-permute-start(bf16[64,1728]{1,0:T(8,128)(2,1)S(1)} %pad_maximum_fusion.2), channel_id=1, source_target_pairs={{0,1},{1,0},{2,3},{3,2},{4,5},{5,4},{6,7},{7,6},{8,9},{9,8},{10,11... | collective-permute-start | bytes 663560 | tf_op jit(solution)/shard_map/ppermute | solution.py:49
  19.7 117.0 %reduce-scatter.2.cloned.1.call-start = ((), (), s32[]{:S(2)}) async-start(), calls=%async_computation.6 | async-start | bytes 2506752 | tf_op jit(solution)/shard_map/reduce_scatter | solution.py:98
  59.0 1.5 copy-start.1
  66.4 7.3 %copy-start.2 = (bf16[16,64,1280]{2,1,0:T(8,128)(2,1)S(1)}, bf16[16,64,1280]{2,1,0:T(8,128)(2,1)}, u32[]{:S(2)}) copy-start(bf16[16,64,1280]{2,1,0:T(8,128)(2,1)} %copy-done.1) | copy-start | bytes 7864324
  122.1 22.7 %copy-start.3 = (bf16[128,576]{0,1:T(8,128)(2,1)S(1)}, bf16[128,576]{0,1:T(8,128)(2,1)}, u32[]{:S(2)}) copy-start(bf16[128,576]{0,1:T(8,128)(2,1)} %param.5) | copy-start | bytes 442372
  139.0 5.8 %collective-permute-start.2 = (bf16[64,1152]{1,0:T(8,128)(2,1)S(1)}, bf16[64,1152]{1,0:T(8,128)(2,1)S(1)}, u32[]{:S(2)}, u32[]{:S(2)}) collective-permute-start(bf16[64,1152]{1,0:T(8,128)(2,1)S(1)} %get-tuple-element.28), channel_id=1, source_target_pairs={{0,1},{1,0},{2,3},{3,2},{4,5},{5,4},{6,7},{7,6},{8,9},{9,8},{10,11... | collective-permute-start | bytes 442376 | tf_op jit(solution)/shard_map/ppermute | solution.py:80
  199.9 47.4 %all-to-all-start.3 = ((bf16[128,6,8,128]{3,2,1,0:T(8,128)(2,1)}), bf16[128,6,8,128]{3,2,1,0:T(8,128)(2,1)S(1)}, u32[]{:S(2)}, u32[]{:S(2)}) async-start(bf16[128,6,8,128]{3,2,1,0:T(8,128)(2,1)} %broadcast_in_dim.8), calls=%async_computation.4 | async-start | bytes 3145728 | tf_op jit(solution)/shard_map/all_to_all | solution.py:23
  207.8 7.6 %collective-permute-start.1 = (bf16[64,576]{1,0:T(8,128)(2,1)S(1)}, bf16[64,576]{1,0:T(8,128)(2,1)S(1)}, u32[]{:S(2)}, u32[]{:S(2)}) collective-permute-start(bf16[64,576]{1,0:T(8,128)(2,1)S(1)} %select_convert_fusion.1), channel_id=1, source_target_pairs={{0,1},{1,0},{2,3},{3,2},{4,5},{5,4},{6,7},{7,6},{8,9},{9,8},{10,11... | collective-permute-start | bytes 221192 | tf_op jit(solution)/shard_map/ppermute | solution.py:103
Sparse Core Ops, SparseCore 0:
  19.8 45.5 all-gather.1
  79.8 56.7 reduce-scatter.1

commit v2 on v1

v2 whole, which is shorter than its diff:
```python
import jax
import jax.numpy as jnp
from jax import lax
from jax.sharding import Mesh
from jax.sharding import PartitionSpec as P

FINE = ("z", "x", "yl", "c", "yh")
SIZES = (8, 4, 2, 2, 2)
DP = ("z", "x", "yl", "c")
NEAR = ("x", "yl")
SWAP = [(0, 1), (1, 0)]
BF = jnp.bfloat16
F32 = jnp.float32


def contract(left, right, dims):
    return lax.dot_general(left, right, ((dims[:1], dims[1:]), ((), ())), preferred_element_type=F32)


def spread(block, axes, count):
    copies = jnp.broadcast_to(block[None], (count,) + block.shape)
    return lax.all_to_all(copies, axes, 0, 0)


def summed(got):
    return jnp.sum(got.astype(F32), axis=0)


def z_ring(block):
    n = SIZES[0]
    up = [(i, (i + 1) % n) for i in range(n)]
    down = [(i, (i - 1) % n) for i in range(n)]
    held = [None] * n
    held[0] = fro = to = block
    for step in range(1, n // 2):
        fro = held[n - step] = lax.ppermute(fro, "z", up)
        to = held[step] = lax.ppermute(to, "z", down)
    cut = block.shape[0] // 16 * 8
    held[n // 2] = jnp.concatenate(
        [lax.ppermute(fro[:cut], "z", up), lax.ppermute(to[cut:], "z", down)], axis=0
    )
    return held


def weight_row(weight, width):
    return jnp.pad(weight[None], ((0, 7), (0, width - weight.shape[0])))


def on_device(images, text_feats, projection, ranks):
    rows, half = images.shape
    own = rows // 2
    width = 2 * half
    batch = rows * 128
    nz, near = 8, 8
    yh = lax.axis_index("yh")
    low = yh == 0
    first = lax.axis_index("c") == 0
    place = lax.axis_index("x") * 2 + lax.axis_index("yl")

    def side(array):
        return jnp.where(low, array[:own], array[own:])

    weight = (0.5 + 1.5 * ranks.astype(F32) / (batch - 1)).astype(BF)

    img_other = lax.ppermute(images, "yh", SWAP)
    partial = jnp.dot(text_feats, projection, preferred_element_type=F32)
    got = lax.ppermute(
        jnp.where(low, partial[own:], partial[:own]).astype(BF), "yh", SWAP
    )
    img32 = jnp.concatenate(
        [jnp.where(low, images, img_other), jnp.where(low, img_other, images)], axis=1
    ).astype(F32)
    inv_img = lax.rsqrt(jnp.sum(img32 * img32, axis=1, keepdims=True) + 1e-06)
    img_b = (img32 * inv_img).astype(BF)
    held = z_ring(jnp.concatenate([img_b, weight_row(weight, width)], axis=0))

    text_out = side(partial) + got.astype(F32)
    inv_txt = lax.rsqrt(jnp.sum(text_out * text_out, axis=1, keepdims=True) + 1e-06)
    unit_txt = text_out * inv_txt
    txt_block = jnp.concatenate([unit_txt.astype(BF), weight_row(side(weight), width)], axis=0)
    txt_mine = spread(txt_block, NEAR, near)
    txt_theirs = lax.ppermute(txt_mine, "c", SWAP)

    all_img = jnp.concatenate([h[:rows] for h in held], axis=0)
    w_img = jnp.concatenate([h[rows, :rows] for h in held], axis=0).astype(F32)

    def pairs(txt, diagonal):
        blk = txt[:, :own].reshape(near * own, width)
        w_txt = txt[:, own, :own].reshape(near * own).astype(F32)
        logits = 10.0 * contract(all_img, blk, (1, 1)) - 2.0
        sig = jax.nn.sigmoid(logits)
        if diagonal:
            i = lax.broadcasted_iota(jnp.int32, sig.shape, 0) - yh * own
            j = lax.broadcasted_iota(jnp.int32, sig.shape, 1) - place * own
            sig = sig - ((i == j) & (i >= 0) & (i < own)).astype(F32)
        coef = (w_img[:, None] * w_txt[None, :] * 10.0 * sig).astype(BF)
        return blk, coef, contract(coef, all_img, (0, 0))

    blk_t, coef_t, part_t = pairs(txt_theirs, False)
    from_c = lax.ppermute(part_t.astype(BF), "c", SWAP)
    blk_m, coef_m, part_m = pairs(txt_mine, True)
    part_txt = (part_m + from_c.astype(F32)).astype(BF).reshape(near, own, width)
    grad_utxt = summed(lax.all_to_all(part_txt, NEAR, 0, 0))

    part_img = (
        jnp.dot(coef_m, blk_m, preferred_element_type=F32)
        + jnp.dot(coef_t, blk_t, preferred_element_type=F32)
    ).astype(BF)
    part_img = jnp.roll(part_img.reshape(nz, rows, width), lax.axis_index("z"), axis=0)
    sum_img = lax.psum_scatter(
        part_img.reshape(nz * rows, width), "z", scatter_dimension=0, tiled=True
    )

    txt_dot = jnp.sum(unit_txt * grad_utxt, axis=1, keepdims=True)
    grad_out = ((grad_utxt - unit_txt * txt_dot) * inv_txt).astype(BF)
    other = lax.ppermute(grad_out, "yh", SWAP)
    grad_full = jnp.concatenate(
        [jnp.where(low, grad_out, other), jnp.where(low, other, grad_out)], axis=0
    )
    grad_text = contract(grad_full, projection, (1, 1))

    weight_part = contract(text_feats, grad_full, (0, 0))
    top, bottom = weight_part[: half // 2], weight_part[half // 2 :]
    from_c = lax.ppermute(jnp.where(first, bottom, top).astype(BF), "c", SWAP)
    mine = (jnp.where(first, top, bottom) + from_c.astype(F32)).astype(BF)
    mine = mine.reshape(near, half // 2 // near, width)
    mine = summed(lax.all_to_all(mine, NEAR, 0, 0)).astype(BF)
    mine = summed(spread(mine, "z", nz)).astype(BF)
    mine, sum_img = lax.optimization_barrier((mine, sum_img))
    mine = spread(mine, NEAR, near).reshape(half // 2, width)
    theirs = lax.ppermute(mine, "c", SWAP)
    grad_weight = jnp.concatenate(
        [jnp.where(first, mine, theirs), jnp.where(first, theirs, mine)], axis=0
    ).astype(F32)

    left, right = sum_img[:, :half], sum_img[:, half:]
    from_yh = lax.ppermute(jnp.where(low, right, left), "yh", SWAP)
    grad_uimg = jnp.where(low, left, right).astype(F32) + from_yh.astype(F32)
    unit_img = images.astype(F32) * inv_img
    dot = jnp.sum(unit_img * grad_uimg, axis=1)
    dot = (dot + lax.ppermute(dot, "yh", SWAP))[:, None]
    grad_image = (grad_uimg - unit_img * dot) * inv_img
    return (grad_image, grad_text, grad_weight)


def solution(mesh):
    fine = Mesh(mesh.devices.reshape(SIZES), FINE)
    return jax.shard_map(
        on_device,
        mesh=fine,
        in_specs=(P(DP, "yh"), P(DP, "yh"), P("yh", None), P(DP)),
        out_specs=(P(DP, "yh"), P(DP, "yh"), P("yh", None)),
        check_vma=False,
    )
```

time: 257 us -> 199 us (0.77)
  blocking collectives: 129 us -> 13.6 us
  starting transfers between devices: 17.1 us -> 58.9 us
  local copies, waits for them, and re-layouts: 6.73 us -> 25.9 us
  waiting for transfers between devices: 59.3 us -> 51.6 us
  other arithmetic: 8.35 us -> 14 us
  matrix products: 21.5 us -> 18.6 us
    all_to_all x3 -> x1, blocking collectives: 129 us -> 13.6 us  [on_device(): mine = summed(lax.all_to_all(mine, NEAR, 0, 0)).astype(BF)]
    ppermute x2 -> x16, starting transfers between devices: 6.4 us -> 32.5 us  [the longest x3 9.35 us: z_ring(): to = held[step] = lax.ppermute(to, 'z', down)]
    reduce_scatter x1 -> x0, waiting for transfers between devices: 14.5 us -> none  [on_device(): lax.psum_scatter(part_img, IMG, scatter_dimension=0, tiled=True).astype(F32)]
    unnamed x13 -> x54, local copies, waits for them, and re-layouts: 3.64 us -> 14.2 us
    all_to_all x0 -> x1, waiting for transfers between devices: none -> 10.6 us  [on_device(): grad_utxt = summed(lax.all_to_all(part_txt, NEAR, 0, 0))]
    all_to_all x1 -> x3, starting transfers between devices: 7.8 us -> 17.3 us  [spread(): return lax.all_to_all(copies, axes, 0, 0)]
    all_to_all x0 -> x1, starting transfers between devices: none -> 5.14 us  [on_device(): grad_utxt = summed(lax.all_to_all(part_txt, NEAR, 0, 0))]
    all_gather x1 -> x0, waiting for transfers between devices: 4.74 us -> none  [on_device(): lax.all_gather(jnp.concatenate([img_b, column], axis=1), IMG, axis=0, til...]
  transfers between devices with their start and end apart: 6 -> 22, of which waited for: 6 -> 11; matrix products, arithmetic and copies ran while one was open for 4% -> 20% of each run, Pallas kernels for 0% -> 0%
where the time goes in v2:
time: 199 us; the launch traced here: 197 us
  starting transfers between devices  58.9 us (30%)
  waiting for transfers between devices  51.6 us (26%)
  local copies, waits for them, and re-layouts  25.9 us (13%)
  matrix products  18.6 us (9%)
  between operations  14.4 us (7%)
  other arithmetic  14 us (7%)
  blocking collectives  13.6 us (7%)
    all_to_all x3, waiting for transfers between devices, spread(): return lax.all_to_all(copies, axes, 0, 0)  26.3 us
    all_to_all x3, starting transfers between devices, spread(): return lax.all_to_all(copies, axes, 0, 0)  17.3 us
    unnamed x54, local copies, waits for them, and re-layouts  14.2 us
    all_to_all x1, blocking collectives, on_device(): mine = summed(lax.all_to_all(mine, NEAR, 0, 0)).astype(BF)  13.6 us
    dot_general x6, matrix products, contract(): lax.dot_general(left, right, ((dims[:1], dims[1:]), ((), ())), preferred_...  12.7 us
    all_to_all x1, waiting for transfers between devices, on_device(): grad_utxt = summed(lax.all_to_all(part_txt, NEAR, 0, 0))  10.6 us
    ppermute x3, starting transfers between devices, z_ring(): to = held[step] = lax.ppermute(to, 'z', down)  9.35 us
    all_to_all x1, starting transfers between devices, on_device(): grad_utxt = summed(lax.all_to_all(part_txt, NEAR, 0, 0))  5.14 us
  transfers between devices with their start and end apart: 22, of which 11 were waited for; matrix products, arithmetic and copies ran while one was open for 20% of the time, Pallas kernels for 0%

profile of v2, /device:TPU:1, one launch (start us, length us, event | category | flops | bytes accessed | tf_op | source)
XLA Modules:
  0.0 197.1 jit_solution(8047454741564351330)
XLA Ops:
  8.4 3.8 %collective-permute-start = (bf16[128,576]{1,0:T(8,128)(2,1)S(1)}, bf16[128,576]{1,0:T(8,128)(2,1)S(1)}, u32[]{:S(2)}, u32[]{:S(2)}) collective-permute-start(bf16[128,576]{1,0:T(8,128)(2,1)S(1)} %copy.28), channel_id=1, source_target_pairs={{0,1},{1,0},{2,3},{3,2},{4,5},{5,4},{6,7},{7,6},{8,9},{9,8},{10,11... | collective-permute-start | bytes 442376 | tf_op jit(solution)/shard_map/ppermute | solution.py:65
  16.2 2.5 %collective-permute-start.5 = (bf16[136,1152]{1,0:T(8,128)(2,1)S(1)}, bf16[136,1152]{1,0:T(8,128)(2,1)S(1)}, u32[]{:S(2)}, u32[]{:S(2)}) collective-permute-start(bf16[136,1152]{1,0:T(8,128)(2,1)S(1)} %fusion.7), channel_id=1, source_target_pairs={{0,32},{32,64},{64,96},{96,128},{128,160},{160,192},{192,224},{224... | collective-permute-start | bytes 940040 | tf_op jit(solution)/shard_map/ppermute | solution.py:36
  18.7 4.0 %collective-permute-start.1 = (bf16[136,1152]{1,0:T(8,128)(2,1)S(1)}, bf16[136,1152]{1,0:T(8,128)(2,1)}, u32[]{:S(2)}, u32[]{:S(2)}) collective-permute-start(bf16[136,1152]{1,0:T(8,128)(2,1)S(1)} %fusion.7), channel_id=1, source_target_pairs={{0,224},{32,0},{64,32},{96,64},{128,96},{160,128},{192,160},{224,1... | collective-permute-start | bytes 940040 | tf_op jit(solution)/shard_map/ppermute | solution.py:37
  24.9 5.0 %all-to-all-start = ((bf16[8,72,1152]{2,1,0:T(8,128)(2,1)}), bf16[8,72,1152]{2,1,0:T(8,128)(2,1)S(1)}, u32[]{:S(2)}, u32[]{:S(2)}) async-start(bf16[8,72,1152]{2,1,0:T(8,128)(2,1)} %broadcast_in_dim.12), calls=%async_computation | async-start | bytes 2654208 | tf_op jit(solution)/shard_map/all_to_all | solution.py:22
  30.0 2.7 %collective-permute-start.2 = (bf16[136,1152]{1,0:T(8,128)(2,1)}, bf16[136,1152]{1,0:T(8,128)(2,1)}, u32[]{:S(2)}, u32[]{:S(2)}) collective-permute-start(bf16[136,1152]{1,0:T(8,128)(2,1)} %collective-permute-done.1), channel_id=1, source_target_pairs={{0,224},{32,0},{64,32},{96,64},{128,96},{160,128},{192,160},{224,1... | collective-permute-start | bytes 940040 | tf_op jit(solution)/shard_map/ppermute | solution.py:37
  32.7 1.7 slice_dynamic-update-slice_fusion.5
  35.3 2.8 %collective-permute-done.6 = bf16[136,1152]{1,0:T(8,128)(2,1)} collective-permute-done((bf16[136,1152]{1,0:T(8,128)(2,1)S(1)}, bf16[136,1152]{1,0:T(8,128)(2,1)}, u32[]{:S(2)}, u32[]{:S(2)}) %collective-permute-start.6) | collective-permute-done | bytes 313376 | tf_op jit(solution)/shard_map/ppermute | solution.py:36
  38.1 2.7 %collective-permute-start.3 = (bf16[136,1152]{1,0:T(8,128)(2,1)}, bf16[136,1152]{1,0:T(8,128)(2,1)S(1)}, u32[]{:S(2)}, u32[]{:S(2)}) collective-permute-start(bf16[136,1152]{1,0:T(8,128)(2,1)} %collective-permute-done.2), channel_id=1, source_target_pairs={{0,224},{32,0},{64,32},{96,64},{128,96},{160,128},{192,160},{224,1... | collective-permute-start | bytes 940040 | tf_op jit(solution)/shard_map/ppermute | solution.py:37
  40.8 1.7 slice_dynamic-update-slice_fusion.4
  46.3 2.7 %collective-permute-start.4 = (bf16[72,1152]{1,0:T(8,128)(2,1)S(1)}, bf16[72,1152]{1,0:T(8,128)(2,1)}, u32[]{:S(2)}, u32[]{:S(2)}) collective-permute-start(bf16[72,1152]{1,0:T(8,128)(2,1)S(1)} %slice.118), channel_id=1, source_target_pairs={{0,224},{32,0},{64,32},{96,64},{128,96},{160,128},{192,160},{224,1... | collective-permute-start | bytes 497672 | tf_op jit(solution)/shard_map/ppermute | solution.py:40
  54.5 5.0 %collective-permute-start.10 = (bf16[8,72,1152]{2,1,0:T(8,128)(2,1)S(1)}, bf16[8,72,1152]{2,1,0:T(8,128)(2,1)S(1)}, u32[]{:S(2)}, u32[]{:S(2)}) collective-permute-start(bf16[8,72,1152]{2,1,0:T(8,128)(2,1)S(1)} %all-to-all-done), channel_id=1, source_target_pairs={{0,2},{2,0},{1,3},{3,1},{4,6},{6,4},{5,7},{7,5},{8,10},{10,8},{9,1... | collective-permute-start | bytes 3981320 | tf_op jit(solution)/shard_map/ppermute | solution.py:82
  66.8 1.9 multiply_convert_fusion
  68.8 2.6 %convolution_convert_fusion = bf16[512,1152]{1,0:T(8,128)(2,1)} fusion(bf16[1024,512]{1,0:T(8,128)(2,1)S(1)} %multiply_convert_fusion, bf16[1024,1152]{1,0:T(8,128)(2,1)S(1)} %copy-done.1), kind=kOutput, calls=%fused_computation.7 | convolution fusion | flops 1208549376 | bytes 4587520 | tf_op jit(solution)/shard_map/dot_general | solution.py:17
  71.7 1.9 copy-done.2
  73.6 2.7 %multiply_convert_fusion.1 = bf16[1024,512]{1,0:T(8,128)(2,1)S(1)} fusion(bf16[1024,1152]{1,0:T(8,128)(2,1)S(1)} %copy-done.2, bf16[512,1152]{1,0:T(8,128)(2,1)S(1)} %bitcast.46, s32[512]{0:T(512)S(1)} %iota_subtract_fusion.1, f32[512]{0:T(512)S(1)} %reshape.130, f32[1024]{0:T(1024)S(1)} %convert_element_type.108, s32[1024]{0:T(1024)S(1)} %iota_subtract_fusion, ...), kind=kOutput, calls=%fused_computation.11 | convolution fusion | flops 1215299584 | bytes 4601856 | tf_op jit(solution)/shard_map/dot_general | solution.py:17
  76.3 3.9 %fusion.1 = bf16[512,1152]{1,0:T(8,128)(2,1)} fusion(bf16[1024,512]{1,0:T(8,128)(2,1)S(1)} %multiply_convert_fusion.1, bf16[1024,1152]{1,0:T(8,128)(2,1)S(1)} %copy-done.2, bf16[512,1152]{1,0:T(8,128)(2,1)} %collective-permute-done.11), kind=kOutput, calls=%fused_computation.6 | convolution fusion | flops 1209729024 | bytes 5767168 | tf_op jit(solution)/shard_map/dot_general | solution.py:17
  80.2 5.1 %all-to-all-start.1 = ((bf16[8,64,1152]{2,1,0:T(8,128)(2,1)}), bf16[8,64,1152]{2,1,0:T(8,128)(2,1)}, u32[]{:S(2)}, u32[]{:S(2)}) async-start(bf16[8,64,1152]{2,1,0:T(8,128)(2,1)} %bitcast.11), calls=%async_computation.1 | async-start | bytes 2359296 | tf_op jit(solution)/shard_map/all_to_all | solution.py:103
  85.4 2.9 %fusion.21 = f32[1024,1152]{1,0:T(8,128)S(1)} fusion(bf16[1024,512]{1,0:T(8,128)(2,1)S(1)} %multiply_convert_fusion.1, bf16[512,1152]{1,0:T(8,128)(2,1)} %bitcast.47), kind=kOutput, calls=%fused_computation.79 | convolution fusion | flops 1207959552 | bytes 6946816 | tf_op jit(solution)/shard_map/dot_general | solution.py:106
  89.9 2.4 %fusion.2 = bf16[8,128,1152]{2,1,0:T(8,128)(2,1)} fusion(s32[]{:T(128)S(6)} %select_n.99, bf16[8,128,1152]{2,1,0:T(8,128)(2,1)S(1)} %bitcast.42), kind=kLoop, calls=%fused_computation.8 | loop fusion | flops 1179648 | bytes 4718596 | tf_op jit(solution)/shard_map/jit(_roll_dynamic)/concatenate | solution.py:109
  92.3 10.6 %all-to-all-done.1 = bf16[8,64,1152]{2,1,0:T(8,128)(2,1)} async-done(((bf16[8,64,1152]{2,1,0:T(8,128)(2,1)}), bf16[8,64,1152]{2,1,0:T(8,128)(2,1)}, u32[]{:S(2)}, u32[]{:S(2)}) %all-to-all-start.1) | async-done | bytes 1179680 | tf_op jit(solution)/shard_map/all_to_all | solution.py:103
  104.7 3.9 %collective-permute-start.12 = (bf16[64,1152]{1,0:T(8,128)(2,1)S(1)}, bf16[64,1152]{1,0:T(8,128)(2,1)S(1)}, u32[]{:S(2)}, u32[]{:S(2)}) collective-permute-start(bf16[64,1152]{1,0:T(8,128)(2,1)S(1)} %multiply_convert_fusion.2), channel_id=1, source_target_pairs={{0,1},{1,0},{2,3},{3,2},{4,5},{5,4},{6,7},{7,6},{8,9},{9,8},{10,11... | collective-permute-start | bytes 442376 | tf_op jit(solution)/shard_map/ppermute | solution.py:116
  108.6 2.5 %collective-permute-done.12 = bf16[64,1152]{1,0:T(8,128)(2,1)S(1)} collective-permute-done((bf16[64,1152]{1,0:T(8,128)(2,1)S(1)}, bf16[64,1152]{1,0:T(8,128)(2,1)S(1)}, u32[]{:S(2)}, u32[]{:S(2)}) %collective-permute-start.12) | collective-permute-done | bytes 147488 | tf_op jit(solution)/shard_map/ppermute | solution.py:116
  111.8 2.5 %collective-permute-start.13 = (bf16[288,1152]{1,0:T(8,128)(2,1)S(1)}, bf16[288,1152]{1,0:T(8,128)(2,1)S(1)}, u32[]{:S(2)}, u32[]{:S(2)}) collective-permute-start(bf16[288,1152]{1,0:T(8,128)(2,1)S(1)} %select_convert_fusion), channel_id=1, source_target_pairs={{0,2},{2,0},{1,3},{3,1},{4,6},{6,4},{5,7},{7,5},{8,10},{10,8},{9,1... | collective-permute-start | bytes 1990664 | tf_op jit(solution)/shard_map/ppermute | solution.py:124
  114.3 1.7 collective-permute-done.13
  116.4 13.6 %all_to_all.25 = bf16[8,36,1152]{2,1,0:T(8,128)(2,1)S(1)} all-to-all(bf16[8,36,1152]{2,1,0:T(8,128)(2,1)S(1)} %reshape.126), channel_id=1, replica_groups=mesh['z'=8,'x'=4,'yl'=2,'c'=2,'yh'=2] {'x','yl'}, dimensions={0} | all-to-all | bytes 1327104 | tf_op jit(solution)/shard_map/all_to_all | solution.py:127
  131.0 7.4 %all-to-all-start.3 = ((bf16[8,36,1152]{2,1,0:T(8,128)(2,1)}), bf16[8,36,1152]{2,1,0:T(8,128)(2,1)S(1)}, u32[]{:S(2)}, u32[]{:S(2)}) async-start(bf16[8,36,1152]{2,1,0:T(8,128)(2,1)} %broadcast_in_dim.13), calls=%async_computation.3 | async-start | bytes 1474560 | tf_op jit(solution)/shard_map/all_to_all | solution.py:22
  139.6 19.5 %all-to-all-done.3 = bf16[8,36,1152]{2,1,0:T(8,128)(2,1)S(1)} async-done(((bf16[8,36,1152]{2,1,0:T(8,128)(2,1)}), bf16[8,36,1152]{2,1,0:T(8,128)(2,1)S(1)}, u32[]{:S(2)}, u32[]{:S(2)}) %all-to-all-start.3) | async-done | bytes 663584 | tf_op jit(solution)/shard_map/all_to_all | solution.py:22
  160.1 5.0 %all-to-all-start.4 = ((bf16[8,36,1152]{2,1,0:T(8,128)(2,1)}), bf16[8,36,1152]{2,1,0:T(8,128)(2,1)S(1)}, u32[]{:S(2)}, u32[]{:S(2)}) async-start(bf16[8,36,1152]{2,1,0:T(8,128)(2,1)} %broadcast_in_dim.14), calls=%async_computation.4 | async-start | bytes 1474560 | tf_op jit(solution)/shard_map/all_to_all | solution.py:22
  166.1 3.2 %collective-permute-start.14 = (bf16[128,576]{1,0:T(8,128)(2,1)}, bf16[128,576]{1,0:T(8,128)(2,1)}, u32[]{:S(2)}, u32[]{:S(2)}) collective-permute-start(bf16[128,576]{1,0:T(8,128)(2,1)} %broadcast_select_fusion.2), channel_id=1, source_target_pairs={{0,1},{1,0},{2,3},{3,2},{4,5},{5,4},{6,7},{7,6},{8,9},{9,8},{10,11... | collective-permute-start | bytes 442376 | tf_op jit(solution)/shard_map/ppermute | solution.py:137
  169.3 6.8 %all-to-all-done.4 = bf16[8,36,1152]{2,1,0:T(8,128)(2,1)S(1)} async-done(((bf16[8,36,1152]{2,1,0:T(8,128)(2,1)}), bf16[8,36,1152]{2,1,0:T(8,128)(2,1)S(1)}, u32[]{:S(2)}, u32[]{:S(2)}) %all-to-all-start.4) | async-done | bytes 663584 | tf_op jit(solution)/shard_map/all_to_all | solution.py:22
  176.3 1.8 collective-permute-start.16
  178.0 2.1 %collective-permute-done.14 = bf16[128,576]{1,0:T(8,128)(2,1)} collective-permute-done((bf16[128,576]{1,0:T(8,128)(2,1)}, bf16[128,576]{1,0:T(8,128)(2,1)}, u32[]{:S(2)}, u32[]{:S(2)}) %collective-permute-start.14) | collective-permute-done | bytes 147488 | tf_op jit(solution)/shard_map/ppermute | solution.py:137
  (134 shorter events, 43.8 us)
Async XLA Ops:
  7.2 5.0 %copy-start = (bf16[576,1152]{1,0:T(8,128)(2,1)S(1)}, bf16[576,1152]{1,0:T(8,128)(2,1)}, u32[]{:S(2)}) copy-start(bf16[576,1152]{1,0:T(8,128)(2,1)} %param.6) | copy-start | bytes 3981316
  7.2 6.6 %copy-start.19 = (s32[128]{0:T(128)S(1)}, s32[128]{0:T(128)}, u32[]{:S(2)}) copy-start(s32[128]{0:T(128)} %param.7) | copy-start | bytes 1540
  8.4 7.8 %copy-start.10 = (bf16[128,576]{1,0:T(8,128)(2,1)}, bf16[128,576]{1,0:T(8,128)(2,1)S(1)}, u32[]{:S(2)}) copy-start(bf16[128,576]{1,0:T(8,128)(2,1)S(1)} %copy.28) | copy-start | bytes 442372
  8.4 6.7 %collective-permute-start = (bf16[128,576]{1,0:T(8,128)(2,1)S(1)}, bf16[128,576]{1,0:T(8,128)(2,1)S(1)}, u32[]{:S(2)}, u32[]{:S(2)}) collective-permute-start(bf16[128,576]{1,0:T(8,128)(2,1)S(1)} %copy.28), channel_id=1, source_target_pairs={{0,1},{1,0},{2,3},{3,2},{4,5},{5,4},{6,7},{7,6},{8,9},{9,8},{10,11... | collective-permute-start | bytes 442376 | tf_op jit(solution)/shard_map/ppermute | solution.py:65
  13.6 9.1 %collective-permute-start.8 = (bf16[64,1152]{1,0:T(8,128)(2,1)S(1)}, bf16[64,1152]{1,0:T(8,128)(2,1)S(1)}, u32[]{:S(2)}, u32[]{:S(2)}) collective-permute-start(bf16[64,1152]{1,0:T(8,128)(2,1)S(1)} %select_convert_fusion.1), channel_id=1, source_target_pairs={{0,1},{1,0},{2,3},{3,2},{4,5},{5,4},{6,7},{7,6},{8,9},{9,8},{10,11... | collective-permute-start | bytes 442376 | tf_op jit(solution)/shard_map/ppermute | solution.py:67
  15.3 9.6 %copy-start.15 = (f32[128]{0:T(128)}, f32[128]{0:T(128)S(1)}, u32[]{:S(2)}) copy-start(f32[128]{0:T(128)S(1)} %add_rsqrt_fusion.1) | copy-start | bytes 1540
  16.2 13.7 %collective-permute-start.5 = (bf16[136,1152]{1,0:T(8,128)(2,1)S(1)}, bf16[136,1152]{1,0:T(8,128)(2,1)S(1)}, u32[]{:S(2)}, u32[]{:S(2)}) collective-permute-start(bf16[136,1152]{1,0:T(8,128)(2,1)S(1)} %fusion.7), channel_id=1, source_target_pairs={{0,32},{32,64},{64,96},{96,128},{128,160},{160,192},{192,224},{224... | collective-permute-start | bytes 940040 | tf_op jit(solution)/shard_map/ppermute | solution.py:36
  18.7 11.3 %collective-permute-start.1 = (bf16[136,1152]{1,0:T(8,128)(2,1)S(1)}, bf16[136,1152]{1,0:T(8,128)(2,1)}, u32[]{:S(2)}, u32[]{:S(2)}) collective-permute-start(bf16[136,1152]{1,0:T(8,128)(2,1)S(1)} %fusion.7), channel_id=1, source_target_pairs={{0,224},{32,0},{64,32},{96,64},{128,96},{160,128},{192,160},{224,1... | collective-permute-start | bytes 940040 | tf_op jit(solution)/shard_map/ppermute | solution.py:37
  24.9 29.6 %all-to-all-start = ((bf16[8,72,1152]{2,1,0:T(8,128)(2,1)}), bf16[8,72,1152]{2,1,0:T(8,128)(2,1)S(1)}, u32[]{:S(2)}, u32[]{:S(2)}) async-start(bf16[8,72,1152]{2,1,0:T(8,128)(2,1)} %broadcast_in_dim.12), calls=%async_computation | async-start | bytes 2654208 | tf_op jit(solution)/shard_map/all_to_all | solution.py:22
  29.9 8.2 %copy-start.14 = (bf16[136,1152]{1,0:T(8,128)(2,1)}, bf16[136,1152]{1,0:T(8,128)(2,1)S(1)}, u32[]{:S(2)}) copy-start(bf16[136,1152]{1,0:T(8,128)(2,1)S(1)} %collective-permute-done.5) | copy-start | bytes 940036
  29.9 8.2 %collective-permute-start.6 = (bf16[136,1152]{1,0:T(8,128)(2,1)S(1)}, bf16[136,1152]{1,0:T(8,128)(2,1)}, u32[]{:S(2)}, u32[]{:S(2)}) collective-permute-start(bf16[136,1152]{1,0:T(8,128)(2,1)S(1)} %collective-permute-done.5), channel_id=1, source_target_pairs={{0,32},{32,64},{64,96},{96,128},{128,160},{160,192},{192,224},{224... | collective-permute-start | bytes 940040 | tf_op jit(solution)/shard_map/ppermute | solution.py:36
  30.0 8.1 %collective-permute-start.2 = (bf16[136,1152]{1,0:T(8,128)(2,1)}, bf16[136,1152]{1,0:T(8,128)(2,1)}, u32[]{:S(2)}, u32[]{:S(2)}) collective-permute-start(bf16[136,1152]{1,0:T(8,128)(2,1)} %collective-permute-done.1), channel_id=1, source_target_pairs={{0,224},{32,0},{64,32},{96,64},{128,96},{160,128},{192,160},{224,1... | collective-permute-start | bytes 940040 | tf_op jit(solution)/shard_map/ppermute | solution.py:37
  38.1 7.5 %collective-permute-start.7 = (bf16[136,1152]{1,0:T(8,128)(2,1)}, bf16[136,1152]{1,0:T(8,128)(2,1)S(1)}, u32[]{:S(2)}, u32[]{:S(2)}) collective-permute-start(bf16[136,1152]{1,0:T(8,128)(2,1)} %collective-permute-done.6), channel_id=1, source_target_pairs={{0,32},{32,64},{64,96},{96,128},{128,160},{160,192},{192,224},{224... | collective-permute-start | bytes 940040 | tf_op jit(solution)/shard_map/ppermute | solution.py:36
  38.1 8.1 %collective-permute-start.3 = (bf16[136,1152]{1,0:T(8,128)(2,1)}, bf16[136,1152]{1,0:T(8,128)(2,1)S(1)}, u32[]{:S(2)}, u32[]{:S(2)}) collective-permute-start(bf16[136,1152]{1,0:T(8,128)(2,1)} %collective-permute-done.2), channel_id=1, source_target_pairs={{0,224},{32,0},{64,32},{96,64},{128,96},{160,128},{192,160},{224,1... | collective-permute-start | bytes 940040 | tf_op jit(solution)/shard_map/ppermute | solution.py:37
  46.3 6.5 %collective-permute-start.9 = (bf16[64,1152]{1,0:T(8,128)(2,1)}, bf16[64,1152]{1,0:T(8,128)(2,1)}, u32[]{:S(2)}, u32[]{:S(2)}) collective-permute-start(bf16[64,1152]{1,0:T(8,128)(2,1)} %slice.129), channel_id=1, source_target_pairs={{0,32},{32,64},{64,96},{96,128},{128,160},{160,192},{192,224},{224... | collective-permute-start | bytes 442376 | tf_op jit(solution)/shard_map/ppermute | solution.py:40
  46.3 5.0 %collective-permute-start.4 = (bf16[72,1152]{1,0:T(8,128)(2,1)S(1)}, bf16[72,1152]{1,0:T(8,128)(2,1)}, u32[]{:S(2)}, u32[]{:S(2)}) collective-permute-start(bf16[72,1152]{1,0:T(8,128)(2,1)S(1)} %slice.118), channel_id=1, source_target_pairs={{0,224},{32,0},{64,32},{96,64},{128,96},{160,128},{192,160},{224,1... | collective-permute-start | bytes 497672 | tf_op jit(solution)/shard_map/ppermute | solution.py:40
  54.5 9.2 %collective-permute-start.10 = (bf16[8,72,1152]{2,1,0:T(8,128)(2,1)S(1)}, bf16[8,72,1152]{2,1,0:T(8,128)(2,1)S(1)}, u32[]{:S(2)}, u32[]{:S(2)}) collective-permute-start(bf16[8,72,1152]{2,1,0:T(8,128)(2,1)S(1)} %all-to-all-done), channel_id=1, source_target_pairs={{0,2},{2,0},{1,3},{3,1},{4,6},{6,4},{5,7},{7,5},{8,10},{10,8},{9,1... | collective-permute-start | bytes 3981320 | tf_op jit(solution)/shard_map/ppermute | solution.py:82
  71.4 4.9 %collective-permute-start.11 = (bf16[512,1152]{1,0:T(8,128)(2,1)}, bf16[512,1152]{1,0:T(8,128)(2,1)}, u32[]{:S(2)}, u32[]{:S(2)}) collective-permute-start(bf16[512,1152]{1,0:T(8,128)(2,1)} %convolution_convert_fusion), channel_id=1, source_target_pairs={{0,2},{2,0},{1,3},{3,1},{4,6},{6,4},{5,7},{7,5},{8,10},{10,8},{9,1... | collective-permute-start | bytes 3538952 | tf_op jit(solution)/shard_map/ppermute | solution.py:100
  80.2 22.8 %all-to-all-start.1 = ((bf16[8,64,1152]{2,1,0:T(8,128)(2,1)}), bf16[8,64,1152]{2,1,0:T(8,128)(2,1)}, u32[]{:S(2)}, u32[]{:S(2)}) async-start(bf16[8,64,1152]{2,1,0:T(8,128)(2,1)} %bitcast.11), calls=%async_computation.1 | async-start | bytes 2359296 | tf_op jit(solution)/shard_map/all_to_all | solution.py:103
  85.3 53.1 %reduce-scatter.4.cloned.1.call-start = ((), (), s32[]{:S(2)}) async-start(), calls=%async_computation.6 | async-start | bytes 2654208
  92.3 12.1 %copy-start.6 = (f32[64,1152]{1,0:T(8,128)S(1)}, f32[64,1152]{1,0:T(8,128)}, u32[]{:S(2)}) copy-start(f32[64,1152]{1,0:T(8,128)} %copy-done.5) | copy-start | bytes 884740
  92.3 12.1 %copy-start.18 = (f32[64]{0:T(128)S(1)}, f32[64]{0:T(128)}, u32[]{:S(2)}) copy-start(f32[64]{0:T(128)} %copy-done.17) | copy-start | bytes 772
  92.3 18.9 %copy-start.13 = (bf16[128,576]{0,1:T(8,128)(2,1)S(1)}, bf16[128,576]{0,1:T(8,128)(2,1)}, u32[]{:S(2)}) copy-start(bf16[128,576]{0,1:T(8,128)(2,1)} %param.5) | copy-start | bytes 442372
  104.7 6.4 %collective-permute-start.12 = (bf16[64,1152]{1,0:T(8,128)(2,1)S(1)}, bf16[64,1152]{1,0:T(8,128)(2,1)S(1)}, u32[]{:S(2)}, u32[]{:S(2)}) collective-permute-start(bf16[64,1152]{1,0:T(8,128)(2,1)S(1)} %multiply_convert_fusion.2), channel_id=1, source_target_pairs={{0,1},{1,0},{2,3},{3,2},{4,5},{5,4},{6,7},{7,6},{8,9},{9,8},{10,11... | collective-permute-start | bytes 442376 | tf_op jit(solution)/shard_map/ppermute | solution.py:116
  111.8 4.2 %collective-permute-start.13 = (bf16[288,1152]{1,0:T(8,128)(2,1)S(1)}, bf16[288,1152]{1,0:T(8,128)(2,1)S(1)}, u32[]{:S(2)}, u32[]{:S(2)}) collective-permute-start(bf16[288,1152]{1,0:T(8,128)(2,1)S(1)} %select_convert_fusion), channel_id=1, source_target_pairs={{0,2},{2,0},{1,3},{3,1},{4,6},{6,4},{5,7},{7,5},{8,10},{10,8},{9,1... | collective-permute-start | bytes 1990664 | tf_op jit(solution)/shard_map/ppermute | solution.py:124
  131.0 28.1 %all-to-all-start.3 = ((bf16[8,36,1152]{2,1,0:T(8,128)(2,1)}), bf16[8,36,1152]{2,1,0:T(8,128)(2,1)S(1)}, u32[]{:S(2)}, u32[]{:S(2)}) async-start(bf16[8,36,1152]{2,1,0:T(8,128)(2,1)} %broadcast_in_dim.13), calls=%async_computation.3 | async-start | bytes 1474560 | tf_op jit(solution)/shard_map/all_to_all | solution.py:22
  160.1 20.0 %copy-start.11 = (bf16[128,576]{1,0:T(8,128)(2,1)S(1)}, bf16[128,576]{1,0:T(8,128)(2,1)}, u32[]{:S(2)}) copy-start(bf16[128,576]{1,0:T(8,128)(2,1)} %copy-done.10) | copy-start | bytes 442372
  160.1 20.0 %copy-start.16 = (f32[128]{0:T(128)S(1)}, f32[128]{0:T(128)}, u32[]{:S(2)}) copy-start(f32[128]{0:T(128)} %copy-done.15) | copy-start | bytes 1540
  160.1 16.0 %all-to-all-start.4 = ((bf16[8,36,1152]{2,1,0:T(8,128)(2,1)}), bf16[8,36,1152]{2,1,0:T(8,128)(2,1)S(1)}, u32[]{:S(2)}, u32[]{:S(2)}) async-start(bf16[8,36,1152]{2,1,0:T(8,128)(2,1)} %broadcast_in_dim.14), calls=%async_computation.4 | async-start | bytes 1474560 | tf_op jit(solution)/shard_map/all_to_all | solution.py:22
  166.1 14.0 %collective-permute-start.14 = (bf16[128,576]{1,0:T(8,128)(2,1)}, bf16[128,576]{1,0:T(8,128)(2,1)}, u32[]{:S(2)}, u32[]{:S(2)}) collective-permute-start(bf16[128,576]{1,0:T(8,128)(2,1)} %broadcast_select_fusion.2), channel_id=1, source_target_pairs={{0,1},{1,0},{2,3},{3,2},{4,5},{5,4},{6,7},{7,6},{8,9},{9,8},{10,11... | collective-permute-start | bytes 442376 | tf_op jit(solution)/shard_map/ppermute | solution.py:137
  176.3 11.0 %collective-permute-start.16 = (bf16[288,1152]{1,0:T(8,128)(2,1)S(1)}, bf16[288,1152]{1,0:T(8,128)(2,1)}, u32[]{:S(2)}, u32[]{:S(2)}) collective-permute-start(bf16[288,1152]{1,0:T(8,128)(2,1)S(1)} %reshape.129), channel_id=1, source_target_pairs={{0,2},{2,0},{1,3},{3,1},{4,6},{6,4},{5,7},{7,5},{8,10},{10,8},{9,1... | collective-permute-start | bytes 1990664 | tf_op jit(solution)/shard_map/ppermute | solution.py:131
  181.3 4.0 %collective-permute-start.15 = (f32[128]{0:T(128)S(1)}, f32[128]{0:T(128)S(1)}, u32[]{:S(2)}, u32[]{:S(2)}) collective-permute-start(f32[128]{0:T(128)S(1)} %multiply_reduce_fusion), channel_id=1, source_target_pairs={{0,1},{1,0},{2,3},{3,2},{4,5},{5,4},{6,7},{7,6},{8,9},{9,8},{10,11... | collective-permute-start | bytes 1544 | tf_op jit(solution)/shard_map/ppermute | solution.py:141
  (10 other events, 23.5 us)
Sparse Core Ops, SparseCore 0:
  92.4 42.6 reduce-scatter.3

commit v3 on v2

--- a/solution.py
+++ b/solution.py
@@ -1,6 +1,9 @@
 import jax
 import jax.numpy as jnp
+import numpy as np
 from jax import lax
+from jax.experimental import pallas as pl
+from jax.experimental.pallas import tpu as pltpu
 from jax.sharding import Mesh
 from jax.sharding import PartitionSpec as P
 
@@ -9,6 +12,8 @@
 DP = ("z", "x", "yl", "c")
 NEAR = ("x", "yl")
 SWAP = [(0, 1), (1, 0)]
+LANES = 128
+CHUNK = 256
 BF = jnp.bfloat16
 F32 = jnp.float32
 
@@ -35,15 +40,88 @@
     for step in range(1, n // 2):
         fro = held[n - step] = lax.ppermute(fro, "z", up)
         to = held[step] = lax.ppermute(to, "z", down)
-    cut = block.shape[0] // 16 * 8
-    held[n // 2] = jnp.concatenate(
-        [lax.ppermute(fro[:cut], "z", up), lax.ppermute(to[cut:], "z", down)], axis=0
-    )
+    cut = block.shape[0] // 2
+    held[n // 2] = (lax.ppermute(fro[:cut], "z", up), lax.ppermute(to[cut:], "z", down))
     return held
 
 
-def weight_row(weight, width):
-    return jnp.pad(weight[None], ((0, 7), (0, width - weight.shape[0])))
+def with_column(block, weight):
+    return jnp.concatenate([block, jnp.pad(weight[:, None], ((0, 0), (0, LANES - 1)))], axis=1)
+
+
+def coefficients(txt, img, w_img, shift, out):
+    width = img.shape[1]
+    dots = contract(txt[:, :width], img[...], (1, 1))
+    sig = 1.0 / (1.0 + jnp.exp(2.0 - 10.0 * dots))
+    if shift is not None:
+        row0, col0, own = shift
+        i = lax.broadcasted_iota(jnp.int32, (1, dots.shape[1]), 1) - col0
+        j = lax.broadcasted_iota(jnp.int32, (dots.shape[0], 1), 0) - row0
+        i = jnp.where((i >= 0) & (i < own), i, -batch_far)
+        sig = jnp.where(j == i, sig - 1.0, sig)
+    w_txt = txt[:, width : width + 1].astype(F32) * 10.0
+    coef = (w_txt * w_img * sig).astype(BF)
+    out[...] = coef
+    return coef
+
+
+batch_far = 1 << 20
+
+
+def theirs_kernel(*refs):
+    blocks, (txt, img, w_img, coef, part) = refs[:-5], refs[-5:]
+    width = img.shape[1]
+    at = 0
+    for block in blocks:
+        n = block.shape[0]
+        img[at : at + n] = block[:, :width]
+        at += n
+    pick = (lax.broadcasted_iota(jnp.int32, (8, LANES), 1) == 0).astype(BF)
+    at = 0
+    for block in blocks:
+        n = block.shape[0]
+        w_img[:, at : at + n] = contract(pick, block[:, width:], (1, 1))
+        at += n
+    for k in range(0, txt.shape[0], CHUNK):
+        c = coefficients(txt.at[k : k + CHUNK], img, w_img[:1], None, coef.at[k : k + CHUNK])
+        part[k : k + CHUNK] = jnp.dot(c, img[...], preferred_element_type=F32).astype(BF)
+
+
+def mine_kernel(where, txt, img, w_img, coef, part):
+    own = where[2]
+    for k in range(0, txt.shape[0], CHUNK):
+        shift = (where[0] * own - k, where[1] * own, own)
+        c = coefficients(txt.at[k : k + CHUNK], img, w_img[:1], shift, coef.at[k : k + CHUNK])
+        part[k : k + CHUNK] = jnp.dot(c, img[...], preferred_element_type=F32)
+
+
+def image_kernel(where, coef_m, coef_t, txt_m, txt_t, part):
+    n, width = part.shape[0], part.shape[2]
+    rows = part.shape[1]
+    per = CHUNK // rows
+    for r in range(0, n, per):
+        cols = slice(r * rows, (r + per) * rows)
+        got = contract(coef_m[:, cols], txt_m[:, :width], (0, 0)) + contract(
+            coef_t[:, cols], txt_t[:, :width], (0, 0)
+        )
+        for e in range(per):
+            part[lax.rem(where[0] + r + e, n)] = got[e * rows : (e + 1) * rows].astype(BF)
+
+
+def call(kernel, outs, scalars, *args):
+    flops = 0
+    for o in outs:
+        flops += 2 * int(np.prod(o[0])) * 1024
+    smem = [pl.BlockSpec(memory_space=pltpu.SMEM)] * (scalars is not None)
+    lead = [scalars] * (scalars is not None)
+    return pl.pallas_call(
+        kernel,
+        out_shape=[jax.ShapeDtypeStruct(*o) for o in outs],
+        in_specs=smem + [pl.BlockSpec(memory_space=pltpu.VMEM)] * len(args),
+        out_specs=[pl.BlockSpec(memory_space=pltpu.VMEM)] * len(outs),
+        compiler_params=pltpu.CompilerParams(vmem_limit_bytes=28 << 20),
+        cost_estimate=pl.CostEstimate(flops=flops, bytes_accessed=8 << 20, transcendentals=0),
+    )(*lead, *args)
 
 
 def on_device(images, text_feats, projection, ranks):
@@ -72,41 +150,42 @@
     ).astype(F32)
     inv_img = lax.rsqrt(jnp.sum(img32 * img32, axis=1, keepdims=True) + 1e-06)
     img_b = (img32 * inv_img).astype(BF)
-    held = z_ring(jnp.concatenate([img_b, weight_row(weight, width)], axis=0))
+    held = z_ring(with_column(img_b, weight))
 
     text_out = side(partial) + got.astype(F32)
     inv_txt = lax.rsqrt(jnp.sum(text_out * text_out, axis=1, keepdims=True) + 1e-06)
     unit_txt = text_out * inv_txt
-    txt_block = jnp.concatenate([unit_txt.astype(BF), weight_row(side(weight), width)], axis=0)
-    txt_mine = spread(txt_block, NEAR, near)
+    txt_mine = spread(with_column(unit_txt.astype(BF), side(weight)), NEAR, near)
+    txt_mine = txt_mine.reshape(near * own, width + LANES)
     txt_theirs = lax.ppermute(txt_mine, "c", SWAP)
 
-    all_img = jnp.concatenate([h[:rows] for h in held], axis=0)
-    w_img = jnp.concatenate([h[rows, :rows] for h in held], axis=0).astype(F32)
-
-    def pairs(txt, diagonal):
-        blk = txt[:, :own].reshape(near * own, width)
-        w_txt = txt[:, own, :own].reshape(near * own).astype(F32)
-        logits = 10.0 * contract(all_img, blk, (1, 1)) - 2.0
-        sig = jax.nn.sigmoid(logits)
-        if diagonal:
-            i = lax.broadcasted_iota(jnp.int32, sig.shape, 0) - yh * own
-            j = lax.broadcasted_iota(jnp.int32, sig.shape, 1) - place * own
-            sig = sig - ((i == j) & (i >= 0) & (i < own)).astype(F32)
-        coef = (w_img[:, None] * w_txt[None, :] * 10.0 * sig).astype(BF)
-        return blk, coef, contract(coef, all_img, (0, 0))
-
-    blk_t, coef_t, part_t = pairs(txt_theirs, False)
-    from_c = lax.ppermute(part_t.astype(BF), "c", SWAP)
-    blk_m, coef_m, part_m = pairs(txt_mine, True)
+    blocks = jax.tree.leaves(held)
+    n_img, n_txt = nz * rows, near * own
+    coef_like = ((n_txt, n_img), BF)
+    all_img, w_img, coef_t, part_t = call(
+        theirs_kernel,
+        [((n_img, width), BF), ((8, n_img), F32), coef_like, ((n_txt, width), BF)],
+        None,
+        *blocks,
+        txt_theirs,
+    )
+    from_c = lax.ppermute(part_t, "c", SWAP)
+    where = jnp.stack([place, yh, jnp.full_like(yh, own)]).astype(jnp.int32)
+    coef_m, part_m = call(
+        mine_kernel, [coef_like, ((n_txt, width), F32)], where, txt_mine, all_img, w_img
+    )
     part_txt = (part_m + from_c.astype(F32)).astype(BF).reshape(near, own, width)
     grad_utxt = summed(lax.all_to_all(part_txt, NEAR, 0, 0))
 
-    part_img = (
-        jnp.dot(coef_m, blk_m, preferred_element_type=F32)
-        + jnp.dot(coef_t, blk_t, preferred_element_type=F32)
-    ).astype(BF)
-    part_img = jnp.roll(part_img.reshape(nz, rows, width), lax.axis_index("z"), axis=0)
+    (part_img,) = call(
+        image_kernel,
+        [((nz, rows, width), BF)],
+        lax.axis_index("z")[None].astype(jnp.int32),
+        coef_m,
+        coef_t,
+        txt_mine,
+        txt_theirs,
+    )
     sum_img = lax.psum_scatter(
         part_img.reshape(nz * rows, width), "z", scatter_dimension=0, tiled=True
     )
@@ -125,8 +204,8 @@
     mine = (jnp.where(first, top, bottom) + from_c.astype(F32)).astype(BF)
     mine = mine.reshape(near, half // 2 // near, width)
     mine = summed(lax.all_to_all(mine, NEAR, 0, 0)).astype(BF)
+    mine, sum_img = lax.optimization_barrier((mine, sum_img))
     mine = summed(spread(mine, "z", nz)).astype(BF)
-    mine, sum_img = lax.optimization_barrier((mine, sum_img))
     mine = spread(mine, NEAR, near).reshape(half // 2, width)
     theirs = lax.ppermute(mine, "c", SWAP)
     grad_weight = jnp.concatenate(

time: 199 us -> 217 us (1.090)
  blocking collectives: 13.6 us -> 36.1 us
  matrix products: 18.6 us -> 3.07 us
  waiting for transfers between devices: 51.6 us -> 65.3 us
  local copies, waits for them, and re-layouts: 25.9 us -> 14.2 us
  Pallas kernels: 0 us -> 11 us
    all_to_all x0 -> x1, blocking collectives: none -> 22.5 us  [spread(): return lax.all_to_all(copies, axes, 0, 0)]
    all_to_all x3 -> x2, waiting for transfers between devices: 26.3 us -> 4.13 us  [spread(): return lax.all_to_all(copies, axes, 0, 0)]
    ppermute x3, waiting for transfers between devices: 4.42 us -> 21.4 us  [z_ring(): fro = held[n - step] = lax.ppermute(fro, 'z', up)]
    ppermute x1, waiting for transfers between devices: 0.95 us -> 17.3 us  [on_device(): img_other = lax.ppermute(images, 'yh', SWAP)]
    dot_general x6 -> x2, matrix products: 12.7 us -> 1.72 us  [contract(): lax.dot_general(left, right, ((dims[:1], dims[1:]), ((), ())), preferred_...]
    pallas_call x0 -> x3, Pallas kernels: none -> 11 us  [call(): pl.pallas_call(kernel, out_shape=[jax.ShapeDtypeStruct(*o) for o in outs]...]
    all_to_all x3 -> x2, starting transfers between devices: 17.3 us -> 10.4 us  [spread(): return lax.all_to_all(copies, axes, 0, 0)]
    ppermute x1, starting transfers between devices: 1.77 us -> 7.51 us  [on_device(): theirs = lax.ppermute(mine, 'c', SWAP)]
  transfers between devices with their start and end apart: 22 -> 21, of which waited for: 11 -> 11; matrix products, arithmetic and copies ran while one was open for 20% -> 4% of each run, Pallas kernels for 0% -> 3%
where the time goes in v3:
time: 217 us; the launch traced here: 215 us
  waiting for transfers between devices  65.3 us (30%)
  starting transfers between devices  58.5 us (27%)
  blocking collectives  36.1 us (17%)
  between operations  14.3 us (7%)
  local copies, waits for them, and re-layouts  14.2 us (7%)
  other arithmetic  12.1 us (6%)
  Pallas kernels  11 us (5%)
  matrix products  3.07 us (1%)
    all_to_all x1, blocking collectives, spread(): return lax.all_to_all(copies, axes, 0, 0)  22.5 us
    ppermute x3, waiting for transfers between devices, z_ring(): fro = held[n - step] = lax.ppermute(fro, 'z', up)  21.4 us
    ppermute x1, waiting for transfers between devices, on_device(): img_other = lax.ppermute(images, 'yh', SWAP)  17.3 us
    all_to_all x1, blocking collectives, on_device(): mine = summed(lax.all_to_all(mine, NEAR, 0, 0)).astype(BF)  13.6 us
    unnamed x30, local copies, waits for them, and re-layouts  11.6 us
    pallas_call x3, Pallas kernels, call(): pl.pallas_call(kernel, out_shape=[jax.ShapeDtypeStruct(*o) for o in outs]...  11 us
    all_to_all x2, starting transfers between devices, spread(): return lax.all_to_all(copies, axes, 0, 0)  10.4 us
    all_to_all x1, waiting for transfers between devices, on_device(): grad_utxt = summed(lax.all_to_all(part_txt, NEAR, 0, 0))  10.4 us
  transfers between devices with their start and end apart: 21, of which 11 were waited for; matrix products, arithmetic and copies ran while one was open for 4% of the time, Pallas kernels for 3%

profile of v3, /device:TPU:1, one launch (start us, length us, event | category | flops | bytes accessed | tf_op | source)
XLA Modules:
  0.0 214.6 jit_solution(14275563627348631406)
XLA Ops:
  9.9 3.8 %collective-permute-start = (bf16[64,1152]{1,0:T(8,128)(2,1)S(1)}, bf16[64,1152]{1,0:T(8,128)(2,1)S(1)}, u32[]{:S(2)}, u32[]{:S(2)}) collective-permute-start(bf16[64,1152]{1,0:T(8,128)(2,1)S(1)} %select_convert_fusion.1), channel_id=1, source_target_pairs={{0,1},{1,0},{2,3},{3,2},{4,5},{5,4},{6,7},{7,6},{8,9},{9,8},{10,11... | collective-permute-start | bytes 442376 | tf_op jit(solution)/shard_map/ppermute | solution.py:145
  13.9 2.3 %collective-permute-done = bf16[64,1152]{1,0:T(8,128)(2,1)S(1)} collective-permute-done((bf16[64,1152]{1,0:T(8,128)(2,1)S(1)}, bf16[64,1152]{1,0:T(8,128)(2,1)S(1)}, u32[]{:S(2)}, u32[]{:S(2)}) %collective-permute-start) | collective-permute-done | bytes 147488 | tf_op jit(solution)/shard_map/ppermute | solution.py:145
  17.7 5.9 %all-to-all-start = ((bf16[8,64,1280]{2,1,0:T(8,128)(2,1)}), bf16[8,64,1280]{2,1,0:T(8,128)(2,1)S(1)}, u32[]{:S(2)}, u32[]{:S(2)}) async-start(bf16[8,64,1280]{2,1,0:T(8,128)(2,1)} %broadcast_in_dim.13), calls=%async_computation | async-start | bytes 2621440 | tf_op jit(solution)/shard_map/all_to_all | solution.py:27
  23.8 2.7 %collective-permute-start.1 = (bf16[128,576]{1,0:T(8,128)(2,1)S(1)}, bf16[128,576]{1,0:T(8,128)(2,1)S(1)}, u32[]{:S(2)}, u32[]{:S(2)}) collective-permute-start(bf16[128,576]{1,0:T(8,128)(2,1)S(1)} %copy.30), channel_id=1, source_target_pairs={{0,1},{1,0},{2,3},{3,2},{4,5},{5,4},{6,7},{7,6},{8,9},{9,8},{10,11... | collective-permute-start | bytes 442376 | tf_op jit(solution)/shard_map/ppermute | solution.py:143
  26.6 17.3 %collective-permute-done.1 = bf16[128,576]{1,0:T(8,128)(2,1)S(1)} collective-permute-done((bf16[128,576]{1,0:T(8,128)(2,1)S(1)}, bf16[128,576]{1,0:T(8,128)(2,1)S(1)}, u32[]{:S(2)}, u32[]{:S(2)}) %collective-permute-start.1) | collective-permute-done | bytes 147488 | tf_op jit(solution)/shard_map/ppermute | solution.py:143
  44.3 1.8 collective-permute-start.10
  46.2 1.7 collective-permute-start.5
  47.9 4.0 %collective-permute-start.2 = (bf16[128,1280]{1,0:T(8,128)(2,1)S(1)}, bf16[128,1280]{1,0:T(8,128)(2,1)S(1)}, u32[]{:S(2)}, u32[]{:S(2)}) collective-permute-start(bf16[128,1280]{1,0:T(8,128)(2,1)S(1)} %fusion.3.refs_0_), channel_id=1, source_target_pairs={{0,224},{32,0},{64,32},{96,64},{128,96},{160,128},{192,160},{224,1... | collective-permute-start | bytes 983048 | tf_op jit(solution)/shard_map/ppermute | solution.py:42
  51.9 8.0 %collective-permute-done.5.refs_8_ = bf16[128,1280]{1,0:T(8,128)(2,1)S(1)} collective-permute-done((bf16[128,1280]{1,0:T(8,128)(2,1)S(1)}, bf16[128,1280]{1,0:T(8,128)(2,1)S(1)}, u32[]{:S(2)}, u32[]{:S(2)}) %collective-permute-start.5) | collective-permute-done | bytes 327712 | tf_op jit(solution)/shard_map/ppermute | solution.py:41
  59.9 2.7 %collective-permute-start.3 = (bf16[128,1280]{1,0:T(8,128)(2,1)S(1)}, bf16[128,1280]{1,0:T(8,128)(2,1)S(1)}, u32[]{:S(2)}, u32[]{:S(2)}) collective-permute-start(bf16[128,1280]{1,0:T(8,128)(2,1)S(1)} %collective-permute-done.2.refs_1_), channel_id=1, source_target_pairs={{0,224},{32,0},{64,32},{96,64},{128,96},{160,128},{192,160},{224,1... | collective-permute-start | bytes 983048 | tf_op jit(solution)/shard_map/ppermute | solution.py:42
  62.6 7.2 %collective-permute-done.6.refs_7_ = bf16[128,1280]{1,0:T(8,128)(2,1)S(1)} collective-permute-done((bf16[128,1280]{1,0:T(8,128)(2,1)S(1)}, bf16[128,1280]{1,0:T(8,128)(2,1)S(1)}, u32[]{:S(2)}, u32[]{:S(2)}) %collective-permute-start.6) | collective-permute-done | bytes 327712 | tf_op jit(solution)/shard_map/ppermute | solution.py:41
  69.8 2.7 %collective-permute-start.4 = (bf16[128,1280]{1,0:T(8,128)(2,1)S(1)}, bf16[128,1280]{1,0:T(8,128)(2,1)S(1)}, u32[]{:S(2)}, u32[]{:S(2)}) collective-permute-start(bf16[128,1280]{1,0:T(8,128)(2,1)S(1)} %collective-permute-done.3.refs_2_), channel_id=1, source_target_pairs={{0,224},{32,0},{64,32},{96,64},{128,96},{160,128},{192,160},{224,1... | collective-permute-start | bytes 983048 | tf_op jit(solution)/shard_map/ppermute | solution.py:42
  72.4 6.3 %collective-permute-done.7.refs_6_ = bf16[128,1280]{1,0:T(8,128)(2,1)S(1)} collective-permute-done((bf16[128,1280]{1,0:T(8,128)(2,1)S(1)}, bf16[128,1280]{1,0:T(8,128)(2,1)S(1)}, u32[]{:S(2)}, u32[]{:S(2)}) %collective-permute-start.7) | collective-permute-done | bytes 327712 | tf_op jit(solution)/shard_map/ppermute | solution.py:41
  78.9 2.9 %collective-permute-start.9 = (bf16[64,1280]{1,0:T(8,128)(2,1)S(1)}, bf16[64,1280]{1,0:T(8,128)(2,1)S(1)}, u32[]{:S(2)}, u32[]{:S(2)}) collective-permute-start(bf16[64,1280]{1,0:T(8,128)(2,1)S(1)} %slice.45), channel_id=1, source_target_pairs={{0,224},{32,0},{64,32},{96,64},{128,96},{160,128},{192,160},{224,1... | collective-permute-start | bytes 491528 | tf_op jit(solution)/shard_map/ppermute | solution.py:44
  81.8 2.4 %collective-permute-done.8.refs_4_ = bf16[64,1280]{1,0:T(8,128)(2,1)S(1)} collective-permute-done((bf16[64,1280]{1,0:T(8,128)(2,1)S(1)}, bf16[64,1280]{1,0:T(8,128)(2,1)S(1)}, u32[]{:S(2)}, u32[]{:S(2)}) %collective-permute-start.8) | collective-permute-done | bytes 163872 | tf_op jit(solution)/shard_map/ppermute | solution.py:44
  84.2 4.3 %shard_map.67 = (bf16[1024,1152]{1,0:T(8,128)(2,1)S(1)}, f32[8,1024]{1,0:T(8,128)S(1)}, bf16[512,1024]{1,0:T(8,128)(2,1)S(1)}, bf16[512,1152]{1,0:T(8,128)(2,1)}) custom-call(bf16[128,1280]{1,0:T(8,128)(2,1)S(1)} %fusion.3.refs_0_, bf16[128,1280]{1,0:T(8,128)(2,1)S(1)} %collective-permute-done.2.refs_1_, ...), custom_call_target="tpu_custom_call" | custom-call | flops 4714397696 | bytes 8388608 | tf_op jit(solution)/shard_map/pallas_call | solution.py:117
  90.9 3.5 %collective-permute-start.11 = (bf16[512,1152]{1,0:T(8,128)(2,1)}, bf16[512,1152]{1,0:T(8,128)(2,1)}, u32[]{:S(2)}, u32[]{:S(2)}) collective-permute-start(bf16[512,1152]{1,0:T(8,128)(2,1)} %get-tuple-element.14), channel_id=1, source_target_pairs={{0,2},{2,0},{1,3},{3,1},{4,6},{6,4},{5,7},{7,5},{8,10},{10,8},{9,1... | collective-permute-start | bytes 3538952 | tf_op jit(solution)/shard_map/ppermute | solution.py:172
  96.2 3.7 %shard_map.68 = (bf16[512,1024]{1,0:T(8,128)(2,1)S(1)}, f32[512,1152]{1,0:T(8,128)S(1)}) custom-call(s32[3]{0:T(128)S(1)} %pad_add_fusion.where, bf16[512,1280]{1,0:T(8,128)(2,1)S(1)} %bitcast.18, bf16[1024,1152]{1,0:T(8,128)(2,1)S(1)} %copy-done.9, f32[8,1024]{1,0:T(8,128)S(1)} %get-tuple-element.12.w_img), custom_call_target="tpu_custom_call" | custom-call | flops 2281701376 | bytes 8388608 | tf_op jit(solution)/shard_map/pallas_call | solution.py:117
  100.0 2.9 %add_convert_fusion = bf16[512,1152]{1,0:T(8,128)(2,1)} fusion(f32[512,1152]{1,0:T(8,128)S(1)} %get-tuple-element.13, bf16[512,1152]{1,0:T(8,128)(2,1)} %collective-permute-done.11), kind=kLoop, calls=%fused_computation.2 | loop fusion | flops 1769472 | bytes 4718592 | tf_op jit(solution)/shard_map/convert_element_type | solution.py:177
  102.8 4.5 %all-to-all-start.1 = ((bf16[8,64,1152]{2,1,0:T(8,128)(2,1)}), bf16[8,64,1152]{2,1,0:T(8,128)(2,1)}, u32[]{:S(2)}, u32[]{:S(2)}) async-start(bf16[8,64,1152]{2,1,0:T(8,128)(2,1)} %bitcast.20), calls=%async_computation.1 | async-start | bytes 2359296 | tf_op jit(solution)/shard_map/all_to_all | solution.py:178
  111.2 3.0 %shard_map.69 = bf16[8,128,1152]{2,1,0:T(8,128)(2,1)S(1)} custom-call(s32[1]{0:T(128)} %bitcast.7.where, bf16[512,1024]{1,0:T(8,128)(2,1)S(1)} %copy-done.7, bf16[512,1024]{1,0:T(8,128)(2,1)S(1)} %copy-done.5, bf16[512,1280]{1,0:T(8,128)(2,1)S(1)} %bitcast.19, bf16[512,1280]{1,0:T(8,128)(2,1)S(1)} %copy-done.3), custom_call_target="tpu_custom_call" | custom-call | flops 2415919104 | bytes 8388608 | tf_op jit(solution)/shard_map/pallas_call | solution.py:117
  115.6 10.4 %all-to-all-done.1 = bf16[8,64,1152]{2,1,0:T(8,128)(2,1)} async-done(((bf16[8,64,1152]{2,1,0:T(8,128)(2,1)}), bf16[8,64,1152]{2,1,0:T(8,128)(2,1)}, u32[]{:S(2)}, u32[]{:S(2)}) %all-to-all-start.1) | async-done | bytes 1179680 | tf_op jit(solution)/shard_map/all_to_all | solution.py:178
  129.4 4.0 %collective-permute-done.12 = bf16[64,1152]{1,0:T(8,128)(2,1)S(1)} collective-permute-done((bf16[64,1152]{1,0:T(8,128)(2,1)S(1)}, bf16[64,1152]{1,0:T(8,128)(2,1)S(1)}, u32[]{:S(2)}, u32[]{:S(2)}) %collective-permute-start.12) | collective-permute-done | bytes 147488 | tf_op jit(solution)/shard_map/ppermute | solution.py:195
  134.1 2.3 %collective-permute-start.13 = (bf16[288,1152]{1,0:T(8,128)(2,1)S(1)}, bf16[288,1152]{1,0:T(8,128)(2,1)S(1)}, u32[]{:S(2)}, u32[]{:S(2)}) collective-permute-start(bf16[288,1152]{1,0:T(8,128)(2,1)S(1)} %select_convert_fusion), channel_id=1, source_target_pairs={{0,2},{2,0},{1,3},{3,1},{4,6},{6,4},{5,7},{7,5},{8,10},{10,8},{9,1... | collective-permute-start | bytes 1990664 | tf_op jit(solution)/shard_map/ppermute | solution.py:203
  136.4 1.7 collective-permute-done.13
  138.5 13.6 %all_to_all.25 = bf16[8,36,1152]{2,1,0:T(8,128)(2,1)S(1)} all-to-all(bf16[8,36,1152]{2,1,0:T(8,128)(2,1)S(1)} %reshape.40), channel_id=1, replica_groups=mesh['z'=8,'x'=4,'yl'=2,'c'=2,'yh'=2] {'x','yl'}, dimensions={0} | all-to-all | bytes 1327104 | tf_op jit(solution)/shard_map/all_to_all | solution.py:206
  153.8 22.5 %all_to_all.26 = bf16[8,36,1152]{2,1,0:T(8,128)(2,1)S(1)} all-to-all(bf16[8,36,1152]{2,1,0:T(8,128)(2,1)S(1)} %broadcast_in_dim.16), channel_id=1, replica_groups=mesh['z'=8,'x'=4,'yl'=2,'c'=2,'yh'=2] {'z'}, dimensions={0} | all-to-all | bytes 1327104 | tf_op jit(solution)/shard_map/all_to_all | solution.py:27
  177.3 4.5 %all-to-all-start.4 = ((bf16[8,36,1152]{2,1,0:T(8,128)(2,1)}), bf16[8,36,1152]{2,1,0:T(8,128)(2,1)S(1)}, u32[]{:S(2)}, u32[]{:S(2)}) async-start(bf16[8,36,1152]{2,1,0:T(8,128)(2,1)} %broadcast_in_dim.17), calls=%async_computation.5 | async-start | bytes 1474560 | tf_op jit(solution)/shard_map/all_to_all | solution.py:27
  182.6 3.3 %collective-permute-start.14 = (bf16[128,576]{1,0:T(8,128)(2,1)}, bf16[128,576]{1,0:T(8,128)(2,1)}, u32[]{:S(2)}, u32[]{:S(2)}) collective-permute-start(bf16[128,576]{1,0:T(8,128)(2,1)} %broadcast_select_fusion.2), channel_id=1, source_target_pairs={{0,1},{1,0},{2,3},{3,2},{4,5},{5,4},{6,7},{7,6},{8,9},{9,8},{10,11... | collective-permute-start | bytes 442376 | tf_op jit(solution)/shard_map/ppermute | solution.py:216
  185.8 4.1 %all-to-all-done.4 = bf16[8,36,1152]{2,1,0:T(8,128)(2,1)S(1)} async-done(((bf16[8,36,1152]{2,1,0:T(8,128)(2,1)}), bf16[8,36,1152]{2,1,0:T(8,128)(2,1)S(1)}, u32[]{:S(2)}, u32[]{:S(2)}) %all-to-all-start.4) | async-done | bytes 663584 | tf_op jit(solution)/shard_map/all_to_all | solution.py:27
  190.1 7.5 %collective-permute-start.16 = (bf16[288,1152]{1,0:T(8,128)(2,1)S(1)}, bf16[288,1152]{1,0:T(8,128)(2,1)}, u32[]{:S(2)}, u32[]{:S(2)}) collective-permute-start(bf16[288,1152]{1,0:T(8,128)(2,1)S(1)} %reshape.42), channel_id=1, source_target_pairs={{0,2},{2,0},{1,3},{3,1},{4,6},{6,4},{5,7},{7,5},{8,10},{10,8},{9,1... | collective-permute-start | bytes 1990664 | tf_op jit(solution)/shard_map/ppermute | solution.py:210
  198.8 2.8 %collective-permute-start.15 = (f32[128]{0:T(128)S(1)}, f32[128]{0:T(128)S(1)}, u32[]{:S(2)}, u32[]{:S(2)}) collective-permute-start(f32[128]{0:T(128)S(1)} %multiply_reduce_fusion), channel_id=1, source_target_pairs={{0,1},{1,0},{2,3},{3,2},{4,5},{5,4},{6,7},{7,6},{8,9},{9,8},{10,11... | collective-permute-start | bytes 1544 | tf_op jit(solution)/shard_map/ppermute | solution.py:220
  (86 shorter events, 29.8 us)
Async XLA Ops:
  7.2 1.3 copy-start
  7.2 6.5 %copy-start.13 = (s32[128]{0:T(128)S(1)}, s32[128]{0:T(128)}, u32[]{:S(2)}) copy-start(s32[128]{0:T(128)} %param.7) | copy-start | bytes 1540
  9.9 6.4 %collective-permute-start = (bf16[64,1152]{1,0:T(8,128)(2,1)S(1)}, bf16[64,1152]{1,0:T(8,128)(2,1)S(1)}, u32[]{:S(2)}, u32[]{:S(2)}) collective-permute-start(bf16[64,1152]{1,0:T(8,128)(2,1)S(1)} %select_convert_fusion.1), channel_id=1, source_target_pairs={{0,1},{1,0},{2,3},{3,2},{4,5},{5,4},{6,7},{7,6},{8,9},{9,8},{10,11... | collective-permute-start | bytes 442376 | tf_op jit(solution)/shard_map/ppermute | solution.py:145
  17.7 5.9 %copy-start.12 = (bf16[128,576]{0,1:T(8,128)(2,1)S(1)}, bf16[128,576]{0,1:T(8,128)(2,1)}, u32[]{:S(2)}) copy-start(bf16[128,576]{0,1:T(8,128)(2,1)} %param.4) | copy-start | bytes 442372
  17.7 26.6 %all-to-all-start = ((bf16[8,64,1280]{2,1,0:T(8,128)(2,1)}), bf16[8,64,1280]{2,1,0:T(8,128)(2,1)S(1)}, u32[]{:S(2)}, u32[]{:S(2)}) async-start(bf16[8,64,1280]{2,1,0:T(8,128)(2,1)} %broadcast_in_dim.13), calls=%async_computation | async-start | bytes 2621440 | tf_op jit(solution)/shard_map/all_to_all | solution.py:27
  23.8 20.1 %collective-permute-start.1 = (bf16[128,576]{1,0:T(8,128)(2,1)S(1)}, bf16[128,576]{1,0:T(8,128)(2,1)S(1)}, u32[]{:S(2)}, u32[]{:S(2)}) collective-permute-start(bf16[128,576]{1,0:T(8,128)(2,1)S(1)} %copy.30), channel_id=1, source_target_pairs={{0,1},{1,0},{2,3},{3,2},{4,5},{5,4},{6,7},{7,6},{8,9},{9,8},{10,11... | collective-permute-start | bytes 442376 | tf_op jit(solution)/shard_map/ppermute | solution.py:143
  44.3 39.9 %collective-permute-start.10 = (bf16[512,1280]{1,0:T(8,128)(2,1)S(1)}, bf16[512,1280]{1,0:T(8,128)(2,1)S(1)}, u32[]{:S(2)}, u32[]{:S(2)}) collective-permute-start(bf16[512,1280]{1,0:T(8,128)(2,1)S(1)} %bitcast.17), channel_id=1, source_target_pairs={{0,2},{2,0},{1,3},{3,1},{4,6},{6,4},{5,7},{7,5},{8,10},{10,8},{9,1... | collective-permute-start | bytes 3932168 | tf_op jit(solution)/shard_map/ppermute | solution.py:160
  46.2 13.7 %collective-permute-start.5 = (bf16[128,1280]{1,0:T(8,128)(2,1)S(1)}, bf16[128,1280]{1,0:T(8,128)(2,1)S(1)}, u32[]{:S(2)}, u32[]{:S(2)}) collective-permute-start(bf16[128,1280]{1,0:T(8,128)(2,1)S(1)} %fusion.3.refs_0_), channel_id=1, source_target_pairs={{0,32},{32,64},{64,96},{96,128},{128,160},{160,192},{192,224},{224... | collective-permute-start | bytes 983048 | tf_op jit(solution)/shard_map/ppermute | solution.py:41
  47.9 12.0 %collective-permute-start.2 = (bf16[128,1280]{1,0:T(8,128)(2,1)S(1)}, bf16[128,1280]{1,0:T(8,128)(2,1)S(1)}, u32[]{:S(2)}, u32[]{:S(2)}) collective-permute-start(bf16[128,1280]{1,0:T(8,128)(2,1)S(1)} %fusion.3.refs_0_), channel_id=1, source_target_pairs={{0,224},{32,0},{64,32},{96,64},{128,96},{160,128},{192,160},{224,1... | collective-permute-start | bytes 983048 | tf_op jit(solution)/shard_map/ppermute | solution.py:42
  59.9 9.9 %collective-permute-start.6 = (bf16[128,1280]{1,0:T(8,128)(2,1)S(1)}, bf16[128,1280]{1,0:T(8,128)(2,1)S(1)}, u32[]{:S(2)}, u32[]{:S(2)}) collective-permute-start(bf16[128,1280]{1,0:T(8,128)(2,1)S(1)} %collective-permute-done.5.refs_8_), channel_id=1, source_target_pairs={{0,32},{32,64},{64,96},{96,128},{128,160},{160,192},{192,224},{224... | collective-permute-start | bytes 983048 | tf_op jit(solution)/shard_map/ppermute | solution.py:41
  59.9 9.9 %collective-permute-start.3 = (bf16[128,1280]{1,0:T(8,128)(2,1)S(1)}, bf16[128,1280]{1,0:T(8,128)(2,1)S(1)}, u32[]{:S(2)}, u32[]{:S(2)}) collective-permute-start(bf16[128,1280]{1,0:T(8,128)(2,1)S(1)} %collective-permute-done.2.refs_1_), channel_id=1, source_target_pairs={{0,224},{32,0},{64,32},{96,64},{128,96},{160,128},{192,160},{224,1... | collective-permute-start | bytes 983048 | tf_op jit(solution)/shard_map/ppermute | solution.py:42
  69.8 9.0 %collective-permute-start.7 = (bf16[128,1280]{1,0:T(8,128)(2,1)S(1)}, bf16[128,1280]{1,0:T(8,128)(2,1)S(1)}, u32[]{:S(2)}, u32[]{:S(2)}) collective-permute-start(bf16[128,1280]{1,0:T(8,128)(2,1)S(1)} %collective-permute-done.6.refs_7_), channel_id=1, source_target_pairs={{0,32},{32,64},{64,96},{96,128},{128,160},{160,192},{192,224},{224... | collective-permute-start | bytes 983048 | tf_op jit(solution)/shard_map/ppermute | solution.py:41
  69.8 9.1 %collective-permute-start.4 = (bf16[128,1280]{1,0:T(8,128)(2,1)S(1)}, bf16[128,1280]{1,0:T(8,128)(2,1)S(1)}, u32[]{:S(2)}, u32[]{:S(2)}) collective-permute-start(bf16[128,1280]{1,0:T(8,128)(2,1)S(1)} %collective-permute-done.3.refs_2_), channel_id=1, source_target_pairs={{0,224},{32,0},{64,32},{96,64},{128,96},{160,128},{192,160},{224,1... | collective-permute-start | bytes 983048 | tf_op jit(solution)/shard_map/ppermute | solution.py:42
  78.7 5.5 %collective-permute-start.8 = (bf16[64,1280]{1,0:T(8,128)(2,1)S(1)}, bf16[64,1280]{1,0:T(8,128)(2,1)S(1)}, u32[]{:S(2)}, u32[]{:S(2)}) collective-permute-start(bf16[64,1280]{1,0:T(8,128)(2,1)S(1)} %slice.44), channel_id=1, source_target_pairs={{0,32},{32,64},{64,96},{96,128},{128,160},{160,192},{192,224},{224... | collective-permute-start | bytes 491528 | tf_op jit(solution)/shard_map/ppermute | solution.py:44
  78.9 5.3 %collective-permute-start.9 = (bf16[64,1280]{1,0:T(8,128)(2,1)S(1)}, bf16[64,1280]{1,0:T(8,128)(2,1)S(1)}, u32[]{:S(2)}, u32[]{:S(2)}) collective-permute-start(bf16[64,1280]{1,0:T(8,128)(2,1)S(1)} %slice.45), channel_id=1, source_target_pairs={{0,224},{32,0},{64,32},{96,64},{128,96},{160,128},{192,160},{224,1... | collective-permute-start | bytes 491528 | tf_op jit(solution)/shard_map/ppermute | solution.py:44
  84.2 4.3 %copy-start.2 = (bf16[512,1280]{1,0:T(8,128)(2,1)}, bf16[512,1280]{1,0:T(8,128)(2,1)S(1)}, u32[]{:S(2)}) copy-start(bf16[512,1280]{1,0:T(8,128)(2,1)S(1)} %collective-permute-done.10.refs_9_.txt_t) | copy-start | bytes 3932164
  89.5 1.4 copy-start.8
  90.9 9.0 %collective-permute-start.11 = (bf16[512,1152]{1,0:T(8,128)(2,1)}, bf16[512,1152]{1,0:T(8,128)(2,1)}, u32[]{:S(2)}, u32[]{:S(2)}) collective-permute-start(bf16[512,1152]{1,0:T(8,128)(2,1)} %get-tuple-element.14), channel_id=1, source_target_pairs={{0,2},{2,0},{1,3},{3,1},{4,6},{6,4},{5,7},{7,5},{8,10},{10,8},{9,1... | collective-permute-start | bytes 3538952 | tf_op jit(solution)/shard_map/ppermute | solution.py:172
  94.5 1.7 copy-start.9
  99.9 2.9 %copy-start.6 = (bf16[512,1024]{1,0:T(8,128)(2,1)}, bf16[512,1024]{1,0:T(8,128)(2,1)S(1)}, u32[]{:S(2)}) copy-start(bf16[512,1024]{1,0:T(8,128)(2,1)S(1)} %get-tuple-element.15.coef_m) | copy-start | bytes 3145732
  102.8 23.2 %all-to-all-start.1 = ((bf16[8,64,1152]{2,1,0:T(8,128)(2,1)}), bf16[8,64,1152]{2,1,0:T(8,128)(2,1)}, u32[]{:S(2)}, u32[]{:S(2)}) async-start(bf16[8,64,1152]{2,1,0:T(8,128)(2,1)} %bitcast.20), calls=%async_computation.1 | async-start | bytes 2359296 | tf_op jit(solution)/shard_map/all_to_all | solution.py:178
  107.4 46.4 %reduce-scatter.2.cloned.1.call-start = ((), (), s32[]{:S(2)}) async-start(), calls=%async_computation.6 | async-start | bytes 2654208 | tf_op jit(solution)/shard_map/reduce_scatter | solution.py:189
  107.4 1.3 copy-start.3
  114.2 1.4 copy-start.1
  127.5 6.0 %copy-start.11 = (bf16[128,576]{0,1:T(8,128)(2,1)S(1)}, bf16[128,576]{0,1:T(8,128)(2,1)}, u32[]{:S(2)}) copy-start(bf16[128,576]{0,1:T(8,128)(2,1)} %param.5) | copy-start | bytes 442372
  127.8 5.6 %collective-permute-start.12 = (bf16[64,1152]{1,0:T(8,128)(2,1)S(1)}, bf16[64,1152]{1,0:T(8,128)(2,1)S(1)}, u32[]{:S(2)}, u32[]{:S(2)}) collective-permute-start(bf16[64,1152]{1,0:T(8,128)(2,1)S(1)} %multiply_convert_fusion), channel_id=1, source_target_pairs={{0,1},{1,0},{2,3},{3,2},{4,5},{5,4},{6,7},{7,6},{8,9},{9,8},{10,11... | collective-permute-start | bytes 442376 | tf_op jit(solution)/shard_map/ppermute | solution.py:195
  134.1 4.0 %collective-permute-start.13 = (bf16[288,1152]{1,0:T(8,128)(2,1)S(1)}, bf16[288,1152]{1,0:T(8,128)(2,1)S(1)}, u32[]{:S(2)}, u32[]{:S(2)}) collective-permute-start(bf16[288,1152]{1,0:T(8,128)(2,1)S(1)} %select_convert_fusion), channel_id=1, source_target_pairs={{0,2},{2,0},{1,3},{3,1},{4,6},{6,4},{5,7},{7,5},{8,10},{10,8},{9,1... | collective-permute-start | bytes 1990664 | tf_op jit(solution)/shard_map/ppermute | solution.py:203
  176.4 5.4 %copy-start.10 = (bf16[128,1152]{1,0:T(8,128)(2,1)S(1)}, bf16[128,1152]{1,0:T(8,128)(2,1)}, u32[]{:S(2)}) copy-start(bf16[128,1152]{1,0:T(8,128)(2,1)} %reduce-scatter.2.cloned.1.call-done) | copy-start | bytes 884740
  177.3 12.7 %all-to-all-start.4 = ((bf16[8,36,1152]{2,1,0:T(8,128)(2,1)}), bf16[8,36,1152]{2,1,0:T(8,128)(2,1)S(1)}, u32[]{:S(2)}, u32[]{:S(2)}) async-start(bf16[8,36,1152]{2,1,0:T(8,128)(2,1)} %broadcast_in_dim.17), calls=%async_computation.5 | async-start | bytes 1474560 | tf_op jit(solution)/shard_map/all_to_all | solution.py:27
  182.6 15.0 %collective-permute-start.14 = (bf16[128,576]{1,0:T(8,128)(2,1)}, bf16[128,576]{1,0:T(8,128)(2,1)}, u32[]{:S(2)}, u32[]{:S(2)}) collective-permute-start(bf16[128,576]{1,0:T(8,128)(2,1)} %broadcast_select_fusion.2), channel_id=1, source_target_pairs={{0,1},{1,0},{2,3},{3,2},{4,5},{5,4},{6,7},{7,6},{8,9},{9,8},{10,11... | collective-permute-start | bytes 442376 | tf_op jit(solution)/shard_map/ppermute | solution.py:216
  190.1 14.8 %collective-permute-start.16 = (bf16[288,1152]{1,0:T(8,128)(2,1)S(1)}, bf16[288,1152]{1,0:T(8,128)(2,1)}, u32[]{:S(2)}, u32[]{:S(2)}) collective-permute-start(bf16[288,1152]{1,0:T(8,128)(2,1)S(1)} %reshape.42), channel_id=1, source_target_pairs={{0,2},{2,0},{1,3},{3,1},{4,6},{6,4},{5,7},{7,5},{8,10},{10,8},{9,1... | collective-permute-start | bytes 1990664 | tf_op jit(solution)/shard_map/ppermute | solution.py:210
  198.8 4.1 %collective-permute-start.15 = (f32[128]{0:T(128)S(1)}, f32[128]{0:T(128)S(1)}, u32[]{:S(2)}, u32[]{:S(2)}) collective-permute-start(f32[128]{0:T(128)S(1)} %multiply_reduce_fusion), channel_id=1, source_target_pairs={{0,1},{1,0},{2,3},{3,2},{4,5},{5,4},{6,7},{7,6},{8,9},{9,8},{10,11... | collective-permute-start | bytes 1544 | tf_op jit(solution)/shard_map/ppermute | solution.py:220
  (3 other events, 3.4 us)
Sparse Core Ops, SparseCore 0:
  115.7 37.9 reduce-scatter.1

commit v4 on v2

v4 whole, which is shorter than its diff:
```python
import functools

import jax
import jax.numpy as jnp
import numpy as np
from jax import lax
from jax.experimental import pallas as pl
from jax.experimental.pallas import tpu as pltpu
from jax.sharding import Mesh
from jax.sharding import PartitionSpec as P

FINE = ("z", "x", "yl", "c", "yh")
SIZES = (8, 4, 2, 2, 2)
DP = ("z", "x", "yl", "c")
NEAR = ("x", "yl")
SWAP = [(0, 1), (1, 0)]
LANES = 128
CHUNK = 256
BF = jnp.bfloat16
F32 = jnp.float32


def contract(left, right, dims):
    return lax.dot_general(left, right, ((dims[:1], dims[1:]), ((), ())), preferred_element_type=F32)


def spread(block, axes, count):
    copies = jnp.broadcast_to(block[None], (count,) + block.shape)
    return lax.all_to_all(copies, axes, 0, 0)


def summed(got):
    return jnp.sum(got.astype(F32), axis=0)


def with_column(block, weight):
    return jnp.concatenate([block, jnp.pad(weight[:, None], ((0, 0), (0, LANES - 1)))], axis=1)


def pair_kernel(where, img, txt_theirs, txt_mine, coef, theirs, mine, w_img):
    own, width = theirs.shape[1:]
    pick = (lax.broadcasted_iota(jnp.int32, (8, LANES), 1) == 0).astype(BF)
    w_img[...] = contract(pick, img[:, width:], (1, 1)) * 10.0
    half = txt_mine.shape[0]
    for txt, out, at in ((txt_theirs, theirs, 0), (txt_mine, mine, half)):
        for k in range(0, half, CHUNK):
            dots = contract(txt[k : k + CHUNK, :width], img[:, :width], (1, 1))
            sig = 1.0 / (1.0 + jnp.exp(2.0 - 10.0 * dots))
            if at:
                i = lax.broadcasted_iota(jnp.int32, (1, dots.shape[1]), 1) - where[0]
                j = lax.broadcasted_iota(jnp.int32, (dots.shape[0], 1), 0) - (where[1] - k)
                j = jnp.where((j >= 0) & (j < own), j, -1)
                i = jnp.where(i >= 0, i, -2)
                sig = jnp.where(j == i, sig - 1.0, sig)
            w_txt = txt[k : k + CHUNK, width : width + 1].astype(F32)
            c = (w_txt * w_img[:1] * sig).astype(BF)
            coef[at + k : at + k + CHUNK] = c
            got = jnp.dot(c, img[:, :width], preferred_element_type=F32).astype(BF)
            for e in range(0, CHUNK, own):
                out[(k + e) // own] = got[e : e + own]


def join_kernel(where, mine, theirs, out):
    n = mine.shape[0]
    out[pl.ds(pl.multiple_of(where[0] * n, 8), n)] = mine[...].astype(F32)
    out[pl.ds(pl.multiple_of((1 - where[0]) * n, 8), n)] = theirs[...].astype(F32)


def image_kernel(coef, txt_theirs, txt_mine, part):
    width = part.shape[1]
    half = txt_mine.shape[0]
    for r in range(0, part.shape[0], CHUNK):
        cut = slice(r, r + CHUNK)
        part[cut] = (
            contract(coef[:half, cut], txt_theirs[:, :width], (0, 0))
            + contract(coef[half:, cut], txt_mine[:, :width], (0, 0))
        ).astype(BF)


def call(kernel, outs, scalars, *args, scratch=(), flops=0):
    lead = [] if scalars is None else [jnp.stack(scalars).astype(jnp.int32)]
    return pl.pallas_call(
        kernel,
        out_shape=[jax.ShapeDtypeStruct(*o) for o in outs],
        in_specs=[pl.BlockSpec(memory_space=pltpu.SMEM)] * len(lead)
        + [pl.BlockSpec(memory_space=pltpu.VMEM)] * len(args),
        out_specs=[pl.BlockSpec(memory_space=pltpu.VMEM)] * len(outs),
        scratch_shapes=list(scratch),
        compiler_params=pltpu.CompilerParams(vmem_limit_bytes=16 << 20),
        cost_estimate=pl.CostEstimate(flops=flops, bytes_accessed=8 << 20, transcendentals=0),
    )(*lead, *args)


def on_device(images, text_feats, projection, ranks):
    rows, half = images.shape
    own = rows // 2
    width = 2 * half
    batch = rows * 128
    nz, near = 8, 8
    yh = lax.axis_index("yh")
    low = yh == 0
    first = lax.axis_index("c") == 0

    def side(array):
        return jnp.where(low, array[:own], array[own:])

    weight = (0.5 + 1.5 * ranks.astype(F32) / (batch - 1)).astype(BF)

    img_other = lax.ppermute(images, "yh", SWAP)
    partial = jnp.dot(text_feats, projection, preferred_element_type=F32)
    send = jnp.where(low, partial[own:], partial[:own]).astype(BF)
    send, img_other = lax.optimization_barrier((send, img_other))
    got = lax.ppermute(send, "yh", SWAP)
    img32 = jnp.concatenate(
        [jnp.where(low, images, img_other), jnp.where(low, img_other, images)], axis=1
    ).astype(F32)
    inv_img = lax.rsqrt(jnp.sum(img32 * img32, axis=1, keepdims=True) + 1e-06)
    img_b = (img32 * inv_img).astype(BF)

    text_out = side(partial) + got.astype(F32)
    inv_txt = lax.rsqrt(jnp.sum(text_out * text_out, axis=1, keepdims=True) + 1e-06)
    unit_txt = text_out * inv_txt
    all_img = lax.all_gather(with_column(img_b, weight), "z", axis=0, tiled=True)
    txt_block = with_column(unit_txt.astype(BF), side(weight))
    txt_mine = spread(txt_block, NEAR, near).reshape(near * own, width + LANES)
    txt_theirs = lax.ppermute(txt_mine, "c", SWAP)

    n_img, n_txt = nz * rows, near * own
    flops = 2 * n_img * 2 * n_txt * width
    coef, part_t, part_m = call(
        pair_kernel,
        [((2 * n_txt, n_img), BF), ((near, own, width), BF), ((near, own, width), BF)],
        [
            lax.axis_index("z") * rows + yh * own,
            (lax.axis_index("x") * 2 + lax.axis_index("yl")) * own,
        ],
        all_img,
        txt_theirs,
        txt_mine,
        scratch=[pltpu.VMEM((8, n_img), F32)],
        flops=2 * flops,
    )
    from_c = lax.ppermute(part_t, "c", SWAP)
    part_txt = (part_m.astype(F32) + from_c.astype(F32)).astype(BF)
    grad_utxt = summed(lax.all_to_all(part_txt, NEAR, 0, 0))

    (part_img,) = call(
        image_kernel, [((n_img, width), BF)], None, coef, txt_theirs, txt_mine, flops=flops
    )
    sum_img = lax.psum_scatter(part_img, "z", scatter_dimension=0, tiled=True)

    txt_dot = jnp.sum(unit_txt * grad_utxt, axis=1, keepdims=True)
    grad_out = ((grad_utxt - unit_txt * txt_dot) * inv_txt).astype(BF)
    other = lax.ppermute(grad_out, "yh", SWAP)
    grad_full = jnp.concatenate(
        [jnp.where(low, grad_out, other), jnp.where(low, other, grad_out)], axis=0
    )
    grad_text = contract(grad_full, projection, (1, 1))

    weight_part = contract(text_feats, grad_full, (0, 0))
    top, bottom = weight_part[: half // 2], weight_part[half // 2 :]
    from_c = lax.ppermute(jnp.where(first, bottom, top).astype(BF), "c", SWAP)
    mine = (jnp.where(first, top, bottom) + from_c.astype(F32)).astype(BF)
    mine = mine.reshape(near, half // 2 // near, width)
    mine = summed(lax.all_to_all(mine, NEAR, 0, 0)).astype(BF)
    mine, sum_img = lax.optimization_barrier((mine, sum_img))
    mine = summed(spread(mine, "z", nz)).astype(BF)

    left, right = sum_img[:, :half], sum_img[:, half:]
    from_yh = lax.ppermute(jnp.where(low, right, left), "yh", SWAP)
    grad_uimg = jnp.where(low, left, right).astype(F32) + from_yh.astype(F32)
    unit_img = images.astype(F32) * inv_img
    dot = jnp.sum(unit_img * grad_uimg, axis=1)
    dot_other = lax.ppermute(dot, "yh", SWAP)
    mine, dot_other = lax.optimization_barrier((mine, dot_other))
    grad_image = (grad_uimg - unit_img * (dot + dot_other)[:, None]) * inv_img

    mine = spread(mine, NEAR, near).reshape(half // 2, width)
    mine, grad_image, grad_text = lax.optimization_barrier((mine, grad_image, grad_text))
    theirs = lax.ppermute(mine, "c", SWAP)
    (grad_weight,) = call(
        join_kernel,
        [((half, width), F32)],
        [lax.axis_index("c")],
        mine,
        theirs,
    )
    return (grad_image, grad_text, grad_weight)


def solution(mesh):
    fine = Mesh(mesh.devices.reshape(SIZES), FINE)
    return jax.shard_map(
        on_device,
        mesh=fine,
        in_specs=(P(DP, "yh"), P(DP, "yh"), P("yh", None), P(DP)),
        out_specs=(P(DP, "yh"), P(DP, "yh"), P("yh", None)),
        check_vma=False,
    )
```

time: 199 us -> 185 us (0.930)
  blocking collectives: 13.6 us -> 33.6 us
  matrix products: 18.6 us -> 3.07 us
  local copies, waits for them, and re-layouts: 25.9 us -> 10.5 us
  Pallas kernels: 0 us -> 13.4 us
  starting transfers between devices: 58.9 us -> 46.9 us
  other arithmetic: 14 us -> 5.87 us
  waiting for transfers between devices: 51.6 us -> 56.5 us
    all_to_all x0 -> x1, blocking collectives: none -> 20 us  [spread(): return lax.all_to_all(copies, axes, 0, 0)]
    pallas_call x0 -> x3, Pallas kernels: none -> 13.4 us  [call(): pl.pallas_call(kernel, out_shape=[jax.ShapeDtypeStruct(*o) for o in outs]...]
    dot_general x6 -> x2, matrix products: 12.7 us -> 1.72 us  [contract(): lax.dot_general(left, right, ((dims[:1], dims[1:]), ((), ())), preferred_...]
    all_gather x0 -> x1, waiting for transfers between devices: none -> 10.6 us  [on_device(): lax.all_gather(with_column(img_b, weight), 'z', axis=0, tiled=True)]
    all_to_all x3 -> x2, waiting for transfers between devices: 26.3 us -> 17.1 us  [spread(): return lax.all_to_all(copies, axes, 0, 0)]
    all_to_all x3 -> x2, starting transfers between devices: 17.3 us -> 10.4 us  [spread(): return lax.all_to_all(copies, axes, 0, 0)]
    unnamed x54 -> x18, local copies, waits for them, and re-layouts: 14.2 us -> 8.08 us
    ppermute x11 -> x3, starting transfers between devices: 16.1 us -> 10.4 us  [the longest x1 3.79 us: on_device(): got = lax.ppermute(send, 'yh', SWAP)]
  transfers between devices with their start and end apart: 22 -> 14, of which waited for: 11 -> 13; matrix products, arithmetic and copies ran while one was open for 20% -> 4% of each run, Pallas kernels for 0% -> 2%
where the time goes in v4:
time: 185 us; the launch traced here: 184 us
  waiting for transfers between devices  56.5 us (31%)
  starting transfers between devices  46.9 us (25%)
  blocking collectives  33.6 us (18%)
  between operations  14.3 us (8%)
  Pallas kernels  13.4 us (7%)
  local copies, waits for them, and re-layouts  10.5 us (6%)
  other arithmetic  5.87 us (3%)
  matrix products  3.07 us (2%)
    all_to_all x1, blocking collectives, spread(): return lax.all_to_all(copies, axes, 0, 0)  20 us
    all_to_all x2, waiting for transfers between devices, spread(): return lax.all_to_all(copies, axes, 0, 0)  17.1 us
    all_to_all x1, blocking collectives, on_device(): mine = summed(lax.all_to_all(mine, NEAR, 0, 0)).astype(BF)  13.6 us
    pallas_call x3, Pallas kernels, call(): pl.pallas_call(kernel, out_shape=[jax.ShapeDtypeStruct(*o) for o in outs]...  13.4 us
    all_gather x1, waiting for transfers between devices, on_device(): lax.all_gather(with_column(img_b, weight), 'z', axis=0, tiled=True)  10.6 us
    all_to_all x2, starting transfers between devices, spread(): return lax.all_to_all(copies, axes, 0, 0)  10.4 us
    all_to_all x1, waiting for transfers between devices, on_device(): grad_utxt = summed(lax.all_to_all(part_txt, NEAR, 0, 0))  10.3 us
    unnamed x18, local copies, waits for them, and re-layouts  8.08 us
  transfers between devices with their start and end apart: 14, of which 13 were waited for; matrix products, arithmetic and copies ran while one was open for 4% of the time, Pallas kernels for 2%

profile of v4, /device:TPU:1, one launch (start us, length us, event | category | flops | bytes accessed | tf_op | source)
XLA Modules:
  0.0 184.1 jit_solution(2430283695210547658)
XLA Ops:
  8.4 3.8 %collective-permute-start = (bf16[128,576]{1,0:T(8,128)(2,1)S(1)}, bf16[128,576]{1,0:T(8,128)(2,1)S(1)}, u32[]{:S(2)}, u32[]{:S(2)}) collective-permute-start(bf16[128,576]{1,0:T(8,128)(2,1)S(1)} %copy.29), channel_id=1, source_target_pairs={{0,1},{1,0},{2,3},{3,2},{4,5},{5,4},{6,7},{7,6},{8,9},{9,8},{10,11... | collective-permute-start | bytes 442376 | tf_op jit(solution)/shard_map/ppermute | solution.py:109
  12.2 1.4 fusion.11
  16.3 3.8 %collective-permute-start.1 = (bf16[64,1152]{1,0:T(8,128)(2,1)S(1)}, bf16[64,1152]{1,0:T(8,128)(2,1)S(1)}, u32[]{:S(2)}, u32[]{:S(2)}) collective-permute-start(bf16[64,1152]{1,0:T(8,128)(2,1)S(1)} %select_convert_fusion.1), channel_id=1, source_target_pairs={{0,1},{1,0},{2,3},{3,2},{4,5},{5,4},{6,7},{7,6},{8,9},{9,8},{10,11... | collective-permute-start | bytes 442376 | tf_op jit(solution)/shard_map/ppermute | solution.py:113
  20.2 2.3 %collective-permute-done.1 = bf16[64,1152]{1,0:T(8,128)(2,1)S(1)} collective-permute-done((bf16[64,1152]{1,0:T(8,128)(2,1)S(1)}, bf16[64,1152]{1,0:T(8,128)(2,1)S(1)}, u32[]{:S(2)}, u32[]{:S(2)}) %collective-permute-start.1) | collective-permute-done | bytes 147488 | tf_op jit(solution)/shard_map/ppermute | solution.py:113
  23.0 20.0 %all_to_all.25 = bf16[8,64,1280]{2,1,0:T(8,128)(2,1)S(1)} all-to-all(bf16[8,64,1280]{2,1,0:T(8,128)(2,1)S(1)} %broadcast_in_dim.12), channel_id=1, replica_groups=mesh['z'=8,'x'=4,'yl'=2,'c'=2,'yh'=2] {'x','yl'}, dimensions={0} | all-to-all | bytes 2621440 | tf_op jit(solution)/shard_map/all_to_all | solution.py:29
  43.0 4.0 %collective-permute-start.2 = (bf16[512,1280]{1,0:T(8,128)(2,1)S(1)}, bf16[512,1280]{1,0:T(8,128)(2,1)}, u32[]{:S(2)}, u32[]{:S(2)}) collective-permute-start(bf16[512,1280]{1,0:T(8,128)(2,1)S(1)} %bitcast.14), channel_id=1, source_target_pairs={{0,2},{2,0},{1,3},{3,1},{4,6},{6,4},{5,7},{7,5},{8,10},{10,8},{9,1... | collective-permute-start | bytes 3932168 | tf_op jit(solution)/shard_map/ppermute | solution.py:126
  47.0 2.7 %collective-permute-done.2.txt_theirs = bf16[512,1280]{1,0:T(8,128)(2,1)} collective-permute-done((bf16[512,1280]{1,0:T(8,128)(2,1)S(1)}, bf16[512,1280]{1,0:T(8,128)(2,1)}, u32[]{:S(2)}, u32[]{:S(2)}) %collective-permute-start.2) | collective-permute-done | bytes 1310752 | tf_op jit(solution)/shard_map/ppermute | solution.py:126
  49.8 10.6 %all-gather.2.cloned.1.call-done.img = bf16[1024,1280]{1,0:T(8,128)(2,1)} async-done(((bf16[128,1280]{1,0:T(8,128)(2,1)}), bf16[1024,1280]{1,0:T(8,128)(2,1)}) %all-gather.2.cloned.1.call-update) | async-done | bytes 2621456 | tf_op jit(solution)/shard_map/all_gather | solution.py:123
  60.4 1.7 copy-done.2
  62.1 7.5 %shard_map.67 = (bf16[1024,1024]{1,0:T(8,128)(2,1)S(1)}, bf16[8,64,1152]{2,1,0:T(8,128)(2,1)S(1)}, bf16[8,64,1152]{2,1,0:T(8,128)(2,1)S(1)}) custom-call(s32[2]{0:T(128)S(1)} %pad_add_fusion.where, bf16[1024,1280]{1,0:T(8,128)(2,1)S(1)} %copy-done.2, bf16[512,1280]{1,0:T(8,128)(2,1)} %collective-permute-done.2.txt_theirs, bf16[512,1280]{1,0:T(8,128)(2,1)S(1)} %bitcast.15), custom_call_target="tpu_custom_call" | custom-call | flops 4831838208 | bytes 8388608 | tf_op jit(solution)/shard_map/pallas_call | solution.py:82
  71.0 3.7 %collective-permute-start.3 = (bf16[8,64,1152]{2,1,0:T(8,128)(2,1)S(1)}, bf16[8,64,1152]{2,1,0:T(8,128)(2,1)S(1)}, u32[]{:S(2)}, u32[]{:S(2)}) collective-permute-start(bf16[8,64,1152]{2,1,0:T(8,128)(2,1)S(1)} %get-tuple-element.18), channel_id=1, source_target_pairs={{0,2},{2,0},{1,3},{3,1},{4,6},{6,4},{5,7},{7,5},{8,10},{10,8},{9,1... | collective-permute-start | bytes 3538952 | tf_op jit(solution)/shard_map/ppermute | solution.py:143
  74.7 2.5 %collective-permute-done.3 = bf16[8,64,1152]{2,1,0:T(8,128)(2,1)S(1)} collective-permute-done((bf16[8,64,1152]{2,1,0:T(8,128)(2,1)S(1)}, bf16[8,64,1152]{2,1,0:T(8,128)(2,1)S(1)}, u32[]{:S(2)}, u32[]{:S(2)}) %collective-permute-start.3) | collective-permute-done | bytes 1179680 | tf_op jit(solution)/shard_map/ppermute | solution.py:143
  78.5 4.8 %all-to-all-start.1 = ((bf16[8,64,1152]{2,1,0:T(8,128)(2,1)}), bf16[8,64,1152]{2,1,0:T(8,128)(2,1)}, u32[]{:S(2)}, u32[]{:S(2)}) async-start(bf16[8,64,1152]{2,1,0:T(8,128)(2,1)} %add_convert_fusion), calls=%async_computation.1 | async-start | bytes 2359296 | tf_op jit(solution)/shard_map/all_to_all | solution.py:145
  83.6 1.6 copy-done.4
  85.1 4.2 %shard_map.68 = bf16[1024,1152]{1,0:T(8,128)(2,1)S(1)} custom-call(bf16[1024,1024]{1,0:T(8,128)(2,1)S(1)} %copy-done.4, bf16[512,1280]{1,0:T(8,128)(2,1)} %collective-permute-done.2.txt_theirs, bf16[512,1280]{1,0:T(8,128)(2,1)S(1)} %bitcast.16), custom_call_target="tpu_custom_call" | custom-call | flops 2415919104 | bytes 8388608 | tf_op jit(solution)/shard_map/pallas_call | solution.py:82
  89.4 1.4 copy-done.1
  90.8 10.3 %all-to-all-done.1 = bf16[8,64,1152]{2,1,0:T(8,128)(2,1)} async-done(((bf16[8,64,1152]{2,1,0:T(8,128)(2,1)}), bf16[8,64,1152]{2,1,0:T(8,128)(2,1)}, u32[]{:S(2)}, u32[]{:S(2)}) %all-to-all-start.1) | async-done | bytes 1179680 | tf_op jit(solution)/shard_map/all_to_all | solution.py:145
  101.2 1.5 convert_reduce_fusion
  103.0 2.6 %collective-permute-start.4 = (bf16[64,1152]{1,0:T(8,128)(2,1)S(1)}, bf16[64,1152]{1,0:T(8,128)(2,1)S(1)}, u32[]{:S(2)}, u32[]{:S(2)}) collective-permute-start(bf16[64,1152]{1,0:T(8,128)(2,1)S(1)} %multiply_convert_fusion), channel_id=1, source_target_pairs={{0,1},{1,0},{2,3},{3,2},{4,5},{5,4},{6,7},{7,6},{8,9},{9,8},{10,11... | collective-permute-start | bytes 442376 | tf_op jit(solution)/shard_map/ppermute | solution.py:154
  105.5 3.0 %collective-permute-done.4 = bf16[64,1152]{1,0:T(8,128)(2,1)S(1)} collective-permute-done((bf16[64,1152]{1,0:T(8,128)(2,1)S(1)}, bf16[64,1152]{1,0:T(8,128)(2,1)S(1)}, u32[]{:S(2)}, u32[]{:S(2)}) %collective-permute-start.4) | collective-permute-done | bytes 147488 | tf_op jit(solution)/shard_map/ppermute | solution.py:154
  109.2 2.7 %collective-permute-start.5 = (bf16[288,1152]{1,0:T(8,128)(2,1)S(1)}, bf16[288,1152]{1,0:T(8,128)(2,1)S(1)}, u32[]{:S(2)}, u32[]{:S(2)}) collective-permute-start(bf16[288,1152]{1,0:T(8,128)(2,1)S(1)} %select_convert_fusion), channel_id=1, source_target_pairs={{0,2},{2,0},{1,3},{3,1},{4,6},{6,4},{5,7},{7,5},{8,10},{10,8},{9,1... | collective-permute-start | bytes 1990664 | tf_op jit(solution)/shard_map/ppermute | solution.py:162
  111.9 1.7 collective-permute-done.5
  114.0 13.6 %all_to_all.26 = bf16[8,36,1152]{2,1,0:T(8,128)(2,1)S(1)} all-to-all(bf16[8,36,1152]{2,1,0:T(8,128)(2,1)S(1)} %reshape.33), channel_id=1, replica_groups=mesh['z'=8,'x'=4,'yl'=2,'c'=2,'yh'=2] {'x','yl'}, dimensions={0} | all-to-all | bytes 1327104 | tf_op jit(solution)/shard_map/all_to_all | solution.py:165
  129.6 5.1 %all-to-all-start.3 = ((bf16[8,36,1152]{2,1,0:T(8,128)(2,1)}), bf16[8,36,1152]{2,1,0:T(8,128)(2,1)S(1)}, u32[]{:S(2)}, u32[]{:S(2)}) async-start(bf16[8,36,1152]{2,1,0:T(8,128)(2,1)} %broadcast_in_dim.13), calls=%async_computation.4 | async-start | bytes 1474560 | tf_op jit(solution)/shard_map/all_to_all | solution.py:29
  134.8 2.9 %collective-permute-start.6 = (bf16[128,576]{1,0:T(8,128)(2,1)S(1)}, bf16[128,576]{1,0:T(8,128)(2,1)S(1)}, u32[]{:S(2)}, u32[]{:S(2)}) collective-permute-start(bf16[128,576]{1,0:T(8,128)(2,1)S(1)} %broadcast_select_fusion), channel_id=1, source_target_pairs={{0,1},{1,0},{2,3},{3,2},{4,5},{5,4},{6,7},{7,6},{8,9},{9,8},{10,11... | collective-permute-start | bytes 442376 | tf_op jit(solution)/shard_map/ppermute | solution.py:170
  137.7 2.9 %collective-permute-done.6 = bf16[128,576]{1,0:T(8,128)(2,1)S(1)} collective-permute-done((bf16[128,576]{1,0:T(8,128)(2,1)S(1)}, bf16[128,576]{1,0:T(8,128)(2,1)S(1)}, u32[]{:S(2)}, u32[]{:S(2)}) %collective-permute-start.6) | collective-permute-done | bytes 147488 | tf_op jit(solution)/shard_map/ppermute | solution.py:170
  140.8 2.9 %collective-permute-start.7 = (f32[128]{0:T(128)S(1)}, f32[128]{0:T(128)S(1)}, u32[]{:S(2)}, u32[]{:S(2)}) collective-permute-start(f32[128]{0:T(128)S(1)} %multiply_reduce_fusion), channel_id=1, source_target_pairs={{0,1},{1,0},{2,3},{3,2},{4,5},{5,4},{6,7},{7,6},{8,9},{9,8},{10,11... | collective-permute-start | bytes 1544 | tf_op jit(solution)/shard_map/ppermute | solution.py:174
  143.7 10.4 %all-to-all-done.3 = bf16[8,36,1152]{2,1,0:T(8,128)(2,1)S(1)} async-done(((bf16[8,36,1152]{2,1,0:T(8,128)(2,1)}), bf16[8,36,1152]{2,1,0:T(8,128)(2,1)S(1)}, u32[]{:S(2)}, u32[]{:S(2)}) %all-to-all-start.3) | async-done | bytes 663584 | tf_op jit(solution)/shard_map/all_to_all | solution.py:29
  155.1 5.3 %all-to-all-start.4 = ((bf16[8,36,1152]{2,1,0:T(8,128)(2,1)}), bf16[8,36,1152]{2,1,0:T(8,128)(2,1)S(1)}, u32[]{:S(2)}, u32[]{:S(2)}) async-start(bf16[8,36,1152]{2,1,0:T(8,128)(2,1)} %broadcast_in_dim.14), calls=%async_computation.5 | async-start | bytes 1474560 | tf_op jit(solution)/shard_map/all_to_all | solution.py:29
  161.9 6.7 %all-to-all-done.4 = bf16[8,36,1152]{2,1,0:T(8,128)(2,1)S(1)} async-done(((bf16[8,36,1152]{2,1,0:T(8,128)(2,1)}), bf16[8,36,1152]{2,1,0:T(8,128)(2,1)S(1)}, u32[]{:S(2)}, u32[]{:S(2)}) %all-to-all-start.4) | async-done | bytes 663584 | tf_op jit(solution)/shard_map/all_to_all | solution.py:29
  168.7 5.1 %collective-permute-start.8 = (bf16[288,1152]{1,0:T(8,128)(2,1)S(1)}, bf16[288,1152]{1,0:T(8,128)(2,1)S(1)}, u32[]{:S(2)}, u32[]{:S(2)}) collective-permute-start(bf16[288,1152]{1,0:T(8,128)(2,1)S(1)} %reshape.34.mine), channel_id=1, source_target_pairs={{0,2},{2,0},{1,3},{3,1},{4,6},{6,4},{5,7},{7,5},{8,10},{10,8},{9,1... | collective-permute-start | bytes 1990664 | tf_op jit(solution)/shard_map/ppermute | solution.py:180
  175.6 1.7 shard_map.69
  (57 shorter events, 15.4 us)
Async XLA Ops:
  7.2 5.1 %copy-start = (bf16[576,1152]{1,0:T(8,128)(2,1)S(1)}, bf16[576,1152]{1,0:T(8,128)(2,1)}, u32[]{:S(2)}) copy-start(bf16[576,1152]{1,0:T(8,128)(2,1)} %param.6) | copy-start | bytes 3981316
  7.2 53.2 %all-gather.2.cloned.1.call-start = ((), (), s32[]{:S(2)}) async-start(), calls=%async_computation.6 | async-start | bytes 2949120 | tf_op jit(solution)/shard_map/all_gather | solution.py:123
  8.4 5.2 %copy-start.7 = (s32[128]{0:T(128)S(1)}, s32[128]{0:T(128)}, u32[]{:S(2)}) copy-start(s32[128]{0:T(128)} %param.7) | copy-start | bytes 1540
  8.4 6.7 %collective-permute-start = (bf16[128,576]{1,0:T(8,128)(2,1)S(1)}, bf16[128,576]{1,0:T(8,128)(2,1)S(1)}, u32[]{:S(2)}, u32[]{:S(2)}) collective-permute-start(bf16[128,576]{1,0:T(8,128)(2,1)S(1)} %copy.29), channel_id=1, source_target_pairs={{0,1},{1,0},{2,3},{3,2},{4,5},{5,4},{6,7},{7,6},{8,9},{9,8},{10,11... | collective-permute-start | bytes 442376 | tf_op jit(solution)/shard_map/ppermute | solution.py:109
  16.3 6.3 %collective-permute-start.1 = (bf16[64,1152]{1,0:T(8,128)(2,1)S(1)}, bf16[64,1152]{1,0:T(8,128)(2,1)S(1)}, u32[]{:S(2)}, u32[]{:S(2)}) collective-permute-start(bf16[64,1152]{1,0:T(8,128)(2,1)S(1)} %select_convert_fusion.1), channel_id=1, source_target_pairs={{0,1},{1,0},{2,3},{3,2},{4,5},{5,4},{6,7},{7,6},{8,9},{9,8},{10,11... | collective-permute-start | bytes 442376 | tf_op jit(solution)/shard_map/ppermute | solution.py:113
  43.0 6.8 %collective-permute-start.2 = (bf16[512,1280]{1,0:T(8,128)(2,1)S(1)}, bf16[512,1280]{1,0:T(8,128)(2,1)}, u32[]{:S(2)}, u32[]{:S(2)}) collective-permute-start(bf16[512,1280]{1,0:T(8,128)(2,1)S(1)} %bitcast.14), channel_id=1, source_target_pairs={{0,2},{2,0},{1,3},{3,1},{4,6},{6,4},{5,7},{7,5},{8,10},{10,8},{9,1... | collective-permute-start | bytes 3932168 | tf_op jit(solution)/shard_map/ppermute | solution.py:126
  60.4 1.7 copy-start.2
  69.7 1.3 copy-start.3
  71.0 6.1 %collective-permute-start.3 = (bf16[8,64,1152]{2,1,0:T(8,128)(2,1)S(1)}, bf16[8,64,1152]{2,1,0:T(8,128)(2,1)S(1)}, u32[]{:S(2)}, u32[]{:S(2)}) collective-permute-start(bf16[8,64,1152]{2,1,0:T(8,128)(2,1)S(1)} %get-tuple-element.18), channel_id=1, source_target_pairs={{0,2},{2,0},{1,3},{3,1},{4,6},{6,4},{5,7},{7,5},{8,10},{10,8},{9,1... | collective-permute-start | bytes 3538952 | tf_op jit(solution)/shard_map/ppermute | solution.py:143
  78.5 22.7 %all-to-all-start.1 = ((bf16[8,64,1152]{2,1,0:T(8,128)(2,1)}), bf16[8,64,1152]{2,1,0:T(8,128)(2,1)}, u32[]{:S(2)}, u32[]{:S(2)}) async-start(bf16[8,64,1152]{2,1,0:T(8,128)(2,1)} %add_convert_fusion), calls=%async_computation.1 | async-start | bytes 2359296 | tf_op jit(solution)/shard_map/all_to_all | solution.py:145
  83.3 45.4 %reduce-scatter.2.cloned.1.call-start = ((), (), s32[]{:S(2)}) async-start(), calls=%async_computation.7 | async-start | bytes 2654208 | tf_op jit(solution)/shard_map/reduce_scatter | solution.py:150
  83.5 1.6 copy-start.4
  89.4 1.4 copy-start.1
  102.6 6.0 %copy-start.6 = (bf16[128,576]{0,1:T(8,128)(2,1)S(1)}, bf16[128,576]{0,1:T(8,128)(2,1)}, u32[]{:S(2)}) copy-start(bf16[128,576]{0,1:T(8,128)(2,1)} %param.5) | copy-start | bytes 442372
  103.0 5.6 %collective-permute-start.4 = (bf16[64,1152]{1,0:T(8,128)(2,1)S(1)}, bf16[64,1152]{1,0:T(8,128)(2,1)S(1)}, u32[]{:S(2)}, u32[]{:S(2)}) collective-permute-start(bf16[64,1152]{1,0:T(8,128)(2,1)S(1)} %multiply_convert_fusion), channel_id=1, source_target_pairs={{0,1},{1,0},{2,3},{3,2},{4,5},{5,4},{6,7},{7,6},{8,9},{9,8},{10,11... | collective-permute-start | bytes 442376 | tf_op jit(solution)/shard_map/ppermute | solution.py:154
  109.2 4.4 %collective-permute-start.5 = (bf16[288,1152]{1,0:T(8,128)(2,1)S(1)}, bf16[288,1152]{1,0:T(8,128)(2,1)S(1)}, u32[]{:S(2)}, u32[]{:S(2)}) collective-permute-start(bf16[288,1152]{1,0:T(8,128)(2,1)S(1)} %select_convert_fusion), channel_id=1, source_target_pairs={{0,2},{2,0},{1,3},{3,1},{4,6},{6,4},{5,7},{7,5},{8,10},{10,8},{9,1... | collective-permute-start | bytes 1990664 | tf_op jit(solution)/shard_map/ppermute | solution.py:162
  128.7 6.0 %copy-start.5 = (bf16[128,1152]{1,0:T(8,128)(2,1)S(1)}, bf16[128,1152]{1,0:T(8,128)(2,1)}, u32[]{:S(2)}) copy-start(bf16[128,1152]{1,0:T(8,128)(2,1)} %reduce-scatter.2.cloned.1.call-done) | copy-start | bytes 884740
  129.6 24.5 %all-to-all-start.3 = ((bf16[8,36,1152]{2,1,0:T(8,128)(2,1)}), bf16[8,36,1152]{2,1,0:T(8,128)(2,1)S(1)}, u32[]{:S(2)}, u32[]{:S(2)}) async-start(bf16[8,36,1152]{2,1,0:T(8,128)(2,1)} %broadcast_in_dim.13), calls=%async_computation.4 | async-start | bytes 1474560 | tf_op jit(solution)/shard_map/all_to_all | solution.py:29
  134.8 5.8 %collective-permute-start.6 = (bf16[128,576]{1,0:T(8,128)(2,1)S(1)}, bf16[128,576]{1,0:T(8,128)(2,1)S(1)}, u32[]{:S(2)}, u32[]{:S(2)}) collective-permute-start(bf16[128,576]{1,0:T(8,128)(2,1)S(1)} %broadcast_select_fusion), channel_id=1, source_target_pairs={{0,1},{1,0},{2,3},{3,2},{4,5},{5,4},{6,7},{7,6},{8,9},{9,8},{10,11... | collective-permute-start | bytes 442376 | tf_op jit(solution)/shard_map/ppermute | solution.py:170
  140.8 13.4 %collective-permute-start.7 = (f32[128]{0:T(128)S(1)}, f32[128]{0:T(128)S(1)}, u32[]{:S(2)}, u32[]{:S(2)}) collective-permute-start(f32[128]{0:T(128)S(1)} %multiply_reduce_fusion), channel_id=1, source_target_pairs={{0,1},{1,0},{2,3},{3,2},{4,5},{5,4},{6,7},{7,6},{8,9},{9,8},{10,11... | collective-permute-start | bytes 1544 | tf_op jit(solution)/shard_map/ppermute | solution.py:174
  155.1 13.5 %all-to-all-start.4 = ((bf16[8,36,1152]{2,1,0:T(8,128)(2,1)}), bf16[8,36,1152]{2,1,0:T(8,128)(2,1)S(1)}, u32[]{:S(2)}, u32[]{:S(2)}) async-start(bf16[8,36,1152]{2,1,0:T(8,128)(2,1)} %broadcast_in_dim.14), calls=%async_computation.5 | async-start | bytes 1474560 | tf_op jit(solution)/shard_map/all_to_all | solution.py:29
  168.7 6.9 %collective-permute-start.8 = (bf16[288,1152]{1,0:T(8,128)(2,1)S(1)}, bf16[288,1152]{1,0:T(8,128)(2,1)S(1)}, u32[]{:S(2)}, u32[]{:S(2)}) collective-permute-start(bf16[288,1152]{1,0:T(8,128)(2,1)S(1)} %reshape.34.mine), channel_id=1, source_target_pairs={{0,2},{2,0},{1,3},{3,1},{4,6},{6,4},{5,7},{7,5},{8,10},{10,8},{9,1... | collective-permute-start | bytes 1990664 | tf_op jit(solution)/shard_map/ppermute | solution.py:180
Sparse Core Ops, SparseCore 0:
  16.4 43.9 all-gather.1
  90.9 37.7 reduce-scatter.1

commit v5 on v4

--- a/solution.py
+++ b/solution.py
@@ -163,7 +163,6 @@
     mine = (jnp.where(first, top, bottom) + from_c.astype(F32)).astype(BF)
     mine = mine.reshape(near, half // 2 // near, width)
     mine = summed(lax.all_to_all(mine, NEAR, 0, 0)).astype(BF)
-    mine, sum_img = lax.optimization_barrier((mine, sum_img))
     mine = summed(spread(mine, "z", nz)).astype(BF)
 
     left, right = sum_img[:, :half], sum_img[:, half:]

time: 185 us -> 183 us (0.989)
  starting transfers between devices: 46.9 us -> 41.3 us
  other arithmetic: 5.87 us -> 7.85 us
    ppermute x1, starting transfers between devices: 5.12 us -> 1.89 us  [on_device(): theirs = lax.ppermute(mine, 'c', SWAP)]
    all_to_all x2, waiting for transfers between devices: 17.1 us -> 19.5 us  [spread(): return lax.all_to_all(copies, axes, 0, 0)]
  transfers between devices with their start and end apart: 14 -> 14, of which waited for: 13 -> 12; matrix products, arithmetic and copies ran while one was open for 4% -> 6% of each run, Pallas kernels for 2% -> 2%
where the time goes in v5:
time: 183 us; the launch traced here: 182 us
  waiting for transfers between devices  58.3 us (32%)
  starting transfers between devices  41.3 us (23%)
  blocking collectives  33.6 us (18%)
  between operations  14.3 us (8%)
  Pallas kernels  13.4 us (7%)
  local copies, waits for them, and re-layouts  10.5 us (6%)
  other arithmetic  7.85 us (4%)
  matrix products  3.07 us (2%)
    all_to_all x1, blocking collectives, spread(): return lax.all_to_all(copies, axes, 0, 0)  20 us
    all_to_all x2, waiting for transfers between devices, spread(): return lax.all_to_all(copies, axes, 0, 0)  19.5 us
    all_to_all x1, blocking collectives, on_device(): mine = summed(lax.all_to_all(mine, NEAR, 0, 0)).astype(BF)  13.6 us
    pallas_call x3, Pallas kernels, call(): pl.pallas_call(kernel, out_shape=[jax.ShapeDtypeStruct(*o) for o in outs]...  13.4 us
    all_gather x1, waiting for transfers between devices, on_device(): lax.all_gather(with_column(img_b, weight), 'z', axis=0, tiled=True)  10.6 us
    all_to_all x1, waiting for transfers between devices, on_device(): grad_utxt = summed(lax.all_to_all(part_txt, NEAR, 0, 0))  10.3 us
    all_to_all x2, starting transfers between devices, spread(): return lax.all_to_all(copies, axes, 0, 0)  8.82 us
    unnamed x18, local copies, waits for them, and re-layouts  8.08 us
  transfers between devices with their start and end apart: 14, of which 12 were waited for; matrix products, arithmetic and copies ran while one was open for 6% of the time, Pallas kernels for 2%

profile of v5, /device:TPU:1, one launch (start us, length us, event | category | flops | bytes accessed | tf_op | source)
XLA Modules:
  0.0 182.4 jit_solution(14325193929902311599)
XLA Ops:
  8.4 3.8 %collective-permute-start = (bf16[128,576]{1,0:T(8,128)(2,1)S(1)}, bf16[128,576]{1,0:T(8,128)(2,1)S(1)}, u32[]{:S(2)}, u32[]{:S(2)}) collective-permute-start(bf16[128,576]{1,0:T(8,128)(2,1)S(1)} %copy.29), channel_id=1, source_target_pairs={{0,1},{1,0},{2,3},{3,2},{4,5},{5,4},{6,7},{7,6},{8,9},{9,8},{10,11... | collective-permute-start | bytes 442376 | tf_op jit(solution)/shard_map/ppermute | solution.py:109
  12.2 1.4 fusion.11
  16.3 3.8 %collective-permute-start.1 = (bf16[64,1152]{1,0:T(8,128)(2,1)S(1)}, bf16[64,1152]{1,0:T(8,128)(2,1)S(1)}, u32[]{:S(2)}, u32[]{:S(2)}) collective-permute-start(bf16[64,1152]{1,0:T(8,128)(2,1)S(1)} %select_convert_fusion.1), channel_id=1, source_target_pairs={{0,1},{1,0},{2,3},{3,2},{4,5},{5,4},{6,7},{7,6},{8,9},{9,8},{10,11... | collective-permute-start | bytes 442376 | tf_op jit(solution)/shard_map/ppermute | solution.py:113
  20.2 2.3 %collective-permute-done.1 = bf16[64,1152]{1,0:T(8,128)(2,1)S(1)} collective-permute-done((bf16[64,1152]{1,0:T(8,128)(2,1)S(1)}, bf16[64,1152]{1,0:T(8,128)(2,1)S(1)}, u32[]{:S(2)}, u32[]{:S(2)}) %collective-permute-start.1) | collective-permute-done | bytes 147488 | tf_op jit(solution)/shard_map/ppermute | solution.py:113
  23.0 20.0 %all_to_all.25 = bf16[8,64,1280]{2,1,0:T(8,128)(2,1)S(1)} all-to-all(bf16[8,64,1280]{2,1,0:T(8,128)(2,1)S(1)} %broadcast_in_dim.12), channel_id=1, replica_groups=mesh['z'=8,'x'=4,'yl'=2,'c'=2,'yh'=2] {'x','yl'}, dimensions={0} | all-to-all | bytes 2621440 | tf_op jit(solution)/shard_map/all_to_all | solution.py:29
  43.0 4.0 %collective-permute-start.2 = (bf16[512,1280]{1,0:T(8,128)(2,1)S(1)}, bf16[512,1280]{1,0:T(8,128)(2,1)}, u32[]{:S(2)}, u32[]{:S(2)}) collective-permute-start(bf16[512,1280]{1,0:T(8,128)(2,1)S(1)} %bitcast.14), channel_id=1, source_target_pairs={{0,2},{2,0},{1,3},{3,1},{4,6},{6,4},{5,7},{7,5},{8,10},{10,8},{9,1... | collective-permute-start | bytes 3932168 | tf_op jit(solution)/shard_map/ppermute | solution.py:126
  47.0 2.7 %collective-permute-done.2.txt_theirs = bf16[512,1280]{1,0:T(8,128)(2,1)} collective-permute-done((bf16[512,1280]{1,0:T(8,128)(2,1)S(1)}, bf16[512,1280]{1,0:T(8,128)(2,1)}, u32[]{:S(2)}, u32[]{:S(2)}) %collective-permute-start.2) | collective-permute-done | bytes 1310752 | tf_op jit(solution)/shard_map/ppermute | solution.py:126
  49.8 10.6 %all-gather.2.cloned.1.call-done.img = bf16[1024,1280]{1,0:T(8,128)(2,1)} async-done(((bf16[128,1280]{1,0:T(8,128)(2,1)}), bf16[1024,1280]{1,0:T(8,128)(2,1)}) %all-gather.2.cloned.1.call-update) | async-done | bytes 2621456 | tf_op jit(solution)/shard_map/all_gather | solution.py:123
  60.4 1.7 copy-done.2
  62.1 7.5 %shard_map.67 = (bf16[1024,1024]{1,0:T(8,128)(2,1)S(1)}, bf16[8,64,1152]{2,1,0:T(8,128)(2,1)S(1)}, bf16[8,64,1152]{2,1,0:T(8,128)(2,1)S(1)}) custom-call(s32[2]{0:T(128)S(1)} %pad_add_fusion.where, bf16[1024,1280]{1,0:T(8,128)(2,1)S(1)} %copy-done.2, bf16[512,1280]{1,0:T(8,128)(2,1)} %collective-permute-done.2.txt_theirs, bf16[512,1280]{1,0:T(8,128)(2,1)S(1)} %bitcast.15), custom_call_target="tpu_custom_call" | custom-call | flops 4831838208 | bytes 8388608 | tf_op jit(solution)/shard_map/pallas_call | solution.py:82
  71.0 3.7 %collective-permute-start.3 = (bf16[8,64,1152]{2,1,0:T(8,128)(2,1)S(1)}, bf16[8,64,1152]{2,1,0:T(8,128)(2,1)S(1)}, u32[]{:S(2)}, u32[]{:S(2)}) collective-permute-start(bf16[8,64,1152]{2,1,0:T(8,128)(2,1)S(1)} %get-tuple-element.16), channel_id=1, source_target_pairs={{0,2},{2,0},{1,3},{3,1},{4,6},{6,4},{5,7},{7,5},{8,10},{10,8},{9,1... | collective-permute-start | bytes 3538952 | tf_op jit(solution)/shard_map/ppermute | solution.py:143
  74.7 2.5 %collective-permute-done.3 = bf16[8,64,1152]{2,1,0:T(8,128)(2,1)S(1)} collective-permute-done((bf16[8,64,1152]{2,1,0:T(8,128)(2,1)S(1)}, bf16[8,64,1152]{2,1,0:T(8,128)(2,1)S(1)}, u32[]{:S(2)}, u32[]{:S(2)}) %collective-permute-start.3) | collective-permute-done | bytes 1179680 | tf_op jit(solution)/shard_map/ppermute | solution.py:143
  78.5 4.8 %all-to-all-start.1 = ((bf16[8,64,1152]{2,1,0:T(8,128)(2,1)}), bf16[8,64,1152]{2,1,0:T(8,128)(2,1)}, u32[]{:S(2)}, u32[]{:S(2)}) async-start(bf16[8,64,1152]{2,1,0:T(8,128)(2,1)} %add_convert_fusion), calls=%async_computation.1 | async-start | bytes 2359296 | tf_op jit(solution)/shard_map/all_to_all | solution.py:145
  83.6 1.6 copy-done.4
  85.1 4.2 %shard_map.68 = bf16[1024,1152]{1,0:T(8,128)(2,1)S(1)} custom-call(bf16[1024,1024]{1,0:T(8,128)(2,1)S(1)} %copy-done.4, bf16[512,1280]{1,0:T(8,128)(2,1)} %collective-permute-done.2.txt_theirs, bf16[512,1280]{1,0:T(8,128)(2,1)S(1)} %bitcast.16), custom_call_target="tpu_custom_call" | custom-call | flops 2415919104 | bytes 8388608 | tf_op jit(solution)/shard_map/pallas_call | solution.py:82
  89.4 1.4 copy-done.1
  90.8 10.3 %all-to-all-done.1 = bf16[8,64,1152]{2,1,0:T(8,128)(2,1)} async-done(((bf16[8,64,1152]{2,1,0:T(8,128)(2,1)}), bf16[8,64,1152]{2,1,0:T(8,128)(2,1)}, u32[]{:S(2)}, u32[]{:S(2)}) %all-to-all-start.1) | async-done | bytes 1179680 | tf_op jit(solution)/shard_map/all_to_all | solution.py:145
  101.2 1.5 convert_reduce_fusion
  103.0 2.6 %collective-permute-start.4 = (bf16[64,1152]{1,0:T(8,128)(2,1)S(1)}, bf16[64,1152]{1,0:T(8,128)(2,1)S(1)}, u32[]{:S(2)}, u32[]{:S(2)}) collective-permute-start(bf16[64,1152]{1,0:T(8,128)(2,1)S(1)} %multiply_convert_fusion), channel_id=1, source_target_pairs={{0,1},{1,0},{2,3},{3,2},{4,5},{5,4},{6,7},{7,6},{8,9},{9,8},{10,11... | collective-permute-start | bytes 442376 | tf_op jit(solution)/shard_map/ppermute | solution.py:154
  105.5 3.0 %collective-permute-done.4 = bf16[64,1152]{1,0:T(8,128)(2,1)S(1)} collective-permute-done((bf16[64,1152]{1,0:T(8,128)(2,1)S(1)}, bf16[64,1152]{1,0:T(8,128)(2,1)S(1)}, u32[]{:S(2)}, u32[]{:S(2)}) %collective-permute-start.4) | collective-permute-done | bytes 147488 | tf_op jit(solution)/shard_map/ppermute | solution.py:154
  109.2 2.7 %collective-permute-start.5 = (bf16[288,1152]{1,0:T(8,128)(2,1)S(1)}, bf16[288,1152]{1,0:T(8,128)(2,1)S(1)}, u32[]{:S(2)}, u32[]{:S(2)}) collective-permute-start(bf16[288,1152]{1,0:T(8,128)(2,1)S(1)} %select_convert_fusion), channel_id=1, source_target_pairs={{0,2},{2,0},{1,3},{3,1},{4,6},{6,4},{5,7},{7,5},{8,10},{10,8},{9,1... | collective-permute-start | bytes 1990664 | tf_op jit(solution)/shard_map/ppermute | solution.py:162
  111.9 1.7 collective-permute-done.5
  113.9 13.6 %all_to_all.26 = bf16[8,36,1152]{2,1,0:T(8,128)(2,1)S(1)} all-to-all(bf16[8,36,1152]{2,1,0:T(8,128)(2,1)S(1)} %reshape.33), channel_id=1, replica_groups=mesh['z'=8,'x'=4,'yl'=2,'c'=2,'yh'=2] {'x','yl'}, dimensions={0} | all-to-all | bytes 1327104 | tf_op jit(solution)/shard_map/all_to_all | solution.py:165
  128.6 4.1 %all-to-all-start.3 = ((bf16[8,36,1152]{2,1,0:T(8,128)(2,1)}), bf16[8,36,1152]{2,1,0:T(8,128)(2,1)S(1)}, u32[]{:S(2)}, u32[]{:S(2)}) async-start(bf16[8,36,1152]{2,1,0:T(8,128)(2,1)} %broadcast_in_dim.13), calls=%async_computation.3 | async-start | bytes 1474560 | tf_op jit(solution)/shard_map/all_to_all | solution.py:29
  133.8 2.5 %collective-permute-start.6 = (bf16[128,576]{1,0:T(8,128)(2,1)S(1)}, bf16[128,576]{1,0:T(8,128)(2,1)S(1)}, u32[]{:S(2)}, u32[]{:S(2)}) collective-permute-start(bf16[128,576]{1,0:T(8,128)(2,1)S(1)} %broadcast_select_fusion), channel_id=1, source_target_pairs={{0,1},{1,0},{2,3},{3,2},{4,5},{5,4},{6,7},{7,6},{8,9},{9,8},{10,11... | collective-permute-start | bytes 442376 | tf_op jit(solution)/shard_map/ppermute | solution.py:169
  136.3 3.3 %collective-permute-done.6 = bf16[128,576]{1,0:T(8,128)(2,1)S(1)} collective-permute-done((bf16[128,576]{1,0:T(8,128)(2,1)S(1)}, bf16[128,576]{1,0:T(8,128)(2,1)S(1)}, u32[]{:S(2)}, u32[]{:S(2)}) %collective-permute-start.6) | collective-permute-done | bytes 147488 | tf_op jit(solution)/shard_map/ppermute | solution.py:169
  140.9 2.5 %collective-permute-start.7 = (f32[128]{0:T(128)S(1)}, f32[128]{0:T(128)S(1)}, u32[]{:S(2)}, u32[]{:S(2)}) collective-permute-start(f32[128]{0:T(128)S(1)} %multiply_reduce_fusion), channel_id=1, source_target_pairs={{0,1},{1,0},{2,3},{3,2},{4,5},{5,4},{6,7},{7,6},{8,9},{9,8},{10,11... | collective-permute-start | bytes 1544 | tf_op jit(solution)/shard_map/ppermute | solution.py:173
  143.4 10.1 %all-to-all-done.3 = bf16[8,36,1152]{2,1,0:T(8,128)(2,1)S(1)} async-done(((bf16[8,36,1152]{2,1,0:T(8,128)(2,1)}), bf16[8,36,1152]{2,1,0:T(8,128)(2,1)S(1)}, u32[]{:S(2)}, u32[]{:S(2)}) %all-to-all-start.3) | async-done | bytes 663584 | tf_op jit(solution)/shard_map/all_to_all | solution.py:29
  154.5 4.7 %all-to-all-start.4 = ((bf16[8,36,1152]{2,1,0:T(8,128)(2,1)}), bf16[8,36,1152]{2,1,0:T(8,128)(2,1)S(1)}, u32[]{:S(2)}, u32[]{:S(2)}) async-start(bf16[8,36,1152]{2,1,0:T(8,128)(2,1)} %broadcast_in_dim.14), calls=%async_computation.5 | async-start | bytes 1474560 | tf_op jit(solution)/shard_map/all_to_all | solution.py:29
  160.6 9.5 %all-to-all-done.4 = bf16[8,36,1152]{2,1,0:T(8,128)(2,1)S(1)} async-done(((bf16[8,36,1152]{2,1,0:T(8,128)(2,1)}), bf16[8,36,1152]{2,1,0:T(8,128)(2,1)S(1)}, u32[]{:S(2)}, u32[]{:S(2)}) %all-to-all-start.4) | async-done | bytes 663584 | tf_op jit(solution)/shard_map/all_to_all | solution.py:29
  170.2 1.9 %collective-permute-start.8 = (bf16[288,1152]{1,0:T(8,128)(2,1)S(1)}, bf16[288,1152]{1,0:T(8,128)(2,1)S(1)}, u32[]{:S(2)}, u32[]{:S(2)}) collective-permute-start(bf16[288,1152]{1,0:T(8,128)(2,1)S(1)} %reshape.34.mine), channel_id=1, source_target_pairs={{0,2},{2,0},{1,3},{3,1},{4,6},{6,4},{5,7},{7,5},{8,10},{10,8},{9,1... | collective-permute-start | bytes 1990664 | tf_op jit(solution)/shard_map/ppermute | solution.py:179
  173.9 1.7 shard_map.69
  (57 shorter events, 16.4 us)
Async XLA Ops:
  7.2 5.1 %copy-start = (bf16[576,1152]{1,0:T(8,128)(2,1)S(1)}, bf16[576,1152]{1,0:T(8,128)(2,1)}, u32[]{:S(2)}) copy-start(bf16[576,1152]{1,0:T(8,128)(2,1)} %param.6) | copy-start | bytes 3981316
  7.2 53.2 %all-gather.2.cloned.1.call-start = ((), (), s32[]{:S(2)}) async-start(), calls=%async_computation.6 | async-start | bytes 2949120 | tf_op jit(solution)/shard_map/all_gather | solution.py:123
  8.4 5.2 %copy-start.7 = (s32[128]{0:T(128)S(1)}, s32[128]{0:T(128)}, u32[]{:S(2)}) copy-start(s32[128]{0:T(128)} %param.7) | copy-start | bytes 1540
  8.4 6.7 %collective-permute-start = (bf16[128,576]{1,0:T(8,128)(2,1)S(1)}, bf16[128,576]{1,0:T(8,128)(2,1)S(1)}, u32[]{:S(2)}, u32[]{:S(2)}) collective-permute-start(bf16[128,576]{1,0:T(8,128)(2,1)S(1)} %copy.29), channel_id=1, source_target_pairs={{0,1},{1,0},{2,3},{3,2},{4,5},{5,4},{6,7},{7,6},{8,9},{9,8},{10,11... | collective-permute-start | bytes 442376 | tf_op jit(solution)/shard_map/ppermute | solution.py:109
  16.3 6.3 %collective-permute-start.1 = (bf16[64,1152]{1,0:T(8,128)(2,1)S(1)}, bf16[64,1152]{1,0:T(8,128)(2,1)S(1)}, u32[]{:S(2)}, u32[]{:S(2)}) collective-permute-start(bf16[64,1152]{1,0:T(8,128)(2,1)S(1)} %select_convert_fusion.1), channel_id=1, source_target_pairs={{0,1},{1,0},{2,3},{3,2},{4,5},{5,4},{6,7},{7,6},{8,9},{9,8},{10,11... | collective-permute-start | bytes 442376 | tf_op jit(solution)/shard_map/ppermute | solution.py:113
  43.0 6.8 %collective-permute-start.2 = (bf16[512,1280]{1,0:T(8,128)(2,1)S(1)}, bf16[512,1280]{1,0:T(8,128)(2,1)}, u32[]{:S(2)}, u32[]{:S(2)}) collective-permute-start(bf16[512,1280]{1,0:T(8,128)(2,1)S(1)} %bitcast.14), channel_id=1, source_target_pairs={{0,2},{2,0},{1,3},{3,1},{4,6},{6,4},{5,7},{7,5},{8,10},{10,8},{9,1... | collective-permute-start | bytes 3932168 | tf_op jit(solution)/shard_map/ppermute | solution.py:126
  60.4 1.7 copy-start.2
  69.7 1.3 copy-start.3
  71.0 6.1 %collective-permute-start.3 = (bf16[8,64,1152]{2,1,0:T(8,128)(2,1)S(1)}, bf16[8,64,1152]{2,1,0:T(8,128)(2,1)S(1)}, u32[]{:S(2)}, u32[]{:S(2)}) collective-permute-start(bf16[8,64,1152]{2,1,0:T(8,128)(2,1)S(1)} %get-tuple-element.16), channel_id=1, source_target_pairs={{0,2},{2,0},{1,3},{3,1},{4,6},{6,4},{5,7},{7,5},{8,10},{10,8},{9,1... | collective-permute-start | bytes 3538952 | tf_op jit(solution)/shard_map/ppermute | solution.py:143
  78.5 22.7 %all-to-all-start.1 = ((bf16[8,64,1152]{2,1,0:T(8,128)(2,1)}), bf16[8,64,1152]{2,1,0:T(8,128)(2,1)}, u32[]{:S(2)}, u32[]{:S(2)}) async-start(bf16[8,64,1152]{2,1,0:T(8,128)(2,1)} %add_convert_fusion), calls=%async_computation.1 | async-start | bytes 2359296 | tf_op jit(solution)/shard_map/all_to_all | solution.py:145
  83.3 49.4 %reduce-scatter.2.cloned.1.call-start = ((), (), s32[]{:S(2)}) async-start(), calls=%async_computation.7 | async-start | bytes 2654208 | tf_op jit(solution)/shard_map/reduce_scatter | solution.py:150
  83.5 1.6 copy-start.4
  89.4 1.4 copy-start.1
  102.6 6.0 %copy-start.6 = (bf16[128,576]{0,1:T(8,128)(2,1)S(1)}, bf16[128,576]{0,1:T(8,128)(2,1)}, u32[]{:S(2)}) copy-start(bf16[128,576]{0,1:T(8,128)(2,1)} %param.5) | copy-start | bytes 442372
  103.0 5.6 %collective-permute-start.4 = (bf16[64,1152]{1,0:T(8,128)(2,1)S(1)}, bf16[64,1152]{1,0:T(8,128)(2,1)S(1)}, u32[]{:S(2)}, u32[]{:S(2)}) collective-permute-start(bf16[64,1152]{1,0:T(8,128)(2,1)S(1)} %multiply_convert_fusion), channel_id=1, source_target_pairs={{0,1},{1,0},{2,3},{3,2},{4,5},{5,4},{6,7},{7,6},{8,9},{9,8},{10,11... | collective-permute-start | bytes 442376 | tf_op jit(solution)/shard_map/ppermute | solution.py:154
  109.2 4.4 %collective-permute-start.5 = (bf16[288,1152]{1,0:T(8,128)(2,1)S(1)}, bf16[288,1152]{1,0:T(8,128)(2,1)S(1)}, u32[]{:S(2)}, u32[]{:S(2)}) collective-permute-start(bf16[288,1152]{1,0:T(8,128)(2,1)S(1)} %select_convert_fusion), channel_id=1, source_target_pairs={{0,2},{2,0},{1,3},{3,1},{4,6},{6,4},{5,7},{7,5},{8,10},{10,8},{9,1... | collective-permute-start | bytes 1990664 | tf_op jit(solution)/shard_map/ppermute | solution.py:162
  128.6 24.8 %all-to-all-start.3 = ((bf16[8,36,1152]{2,1,0:T(8,128)(2,1)}), bf16[8,36,1152]{2,1,0:T(8,128)(2,1)S(1)}, u32[]{:S(2)}, u32[]{:S(2)}) async-start(bf16[8,36,1152]{2,1,0:T(8,128)(2,1)} %broadcast_in_dim.13), calls=%async_computation.3 | async-start | bytes 1474560 | tf_op jit(solution)/shard_map/all_to_all | solution.py:29
  133.8 5.8 %collective-permute-start.6 = (bf16[128,576]{1,0:T(8,128)(2,1)S(1)}, bf16[128,576]{1,0:T(8,128)(2,1)S(1)}, u32[]{:S(2)}, u32[]{:S(2)}) collective-permute-start(bf16[128,576]{1,0:T(8,128)(2,1)S(1)} %broadcast_select_fusion), channel_id=1, source_target_pairs={{0,1},{1,0},{2,3},{3,2},{4,5},{5,4},{6,7},{7,6},{8,9},{9,8},{10,11... | collective-permute-start | bytes 442376 | tf_op jit(solution)/shard_map/ppermute | solution.py:169
  140.9 12.7 %collective-permute-start.7 = (f32[128]{0:T(128)S(1)}, f32[128]{0:T(128)S(1)}, u32[]{:S(2)}, u32[]{:S(2)}) collective-permute-start(f32[128]{0:T(128)S(1)} %multiply_reduce_fusion), channel_id=1, source_target_pairs={{0,1},{1,0},{2,3},{3,2},{4,5},{5,4},{6,7},{7,6},{8,9},{9,8},{10,11... | collective-permute-start | bytes 1544 | tf_op jit(solution)/shard_map/ppermute | solution.py:173
  154.5 15.6 %all-to-all-start.4 = ((bf16[8,36,1152]{2,1,0:T(8,128)(2,1)}), bf16[8,36,1152]{2,1,0:T(8,128)(2,1)S(1)}, u32[]{:S(2)}, u32[]{:S(2)}) async-start(bf16[8,36,1152]{2,1,0:T(8,128)(2,1)} %broadcast_in_dim.14), calls=%async_computation.5 | async-start | bytes 1474560 | tf_op jit(solution)/shard_map/all_to_all | solution.py:29
  159.2 1.2 copy-start.5
  170.2 3.6 %collective-permute-start.8 = (bf16[288,1152]{1,0:T(8,128)(2,1)S(1)}, bf16[288,1152]{1,0:T(8,128)(2,1)S(1)}, u32[]{:S(2)}, u32[]{:S(2)}) collective-permute-start(bf16[288,1152]{1,0:T(8,128)(2,1)S(1)} %reshape.34.mine), channel_id=1, source_target_pairs={{0,2},{2,0},{1,3},{3,1},{4,6},{6,4},{5,7},{7,5},{8,10},{10,8},{9,1... | collective-permute-start | bytes 1990664 | tf_op jit(solution)/shard_map/ppermute | solution.py:179
Sparse Core Ops, SparseCore 0:
  16.4 43.9 all-gather.1
  90.9 37.7 reduce-scatter.1

commit v6 on v5

--- a/solution.py
+++ b/solution.py
@@ -37,27 +37,33 @@
     return jnp.concatenate([block, jnp.pad(weight[:, None], ((0, 0), (0, LANES - 1)))], axis=1)
 
 
-def pair_kernel(where, img, txt_theirs, txt_mine, coef, theirs, mine, w_img):
-    own, width = theirs.shape[1:]
+def pair_kernel(has_own, where, img, txt, coef, part, w_img):
+    own, width = part.shape[1:]
     pick = (lax.broadcasted_iota(jnp.int32, (8, LANES), 1) == 0).astype(BF)
     w_img[...] = contract(pick, img[:, width:], (1, 1)) * 10.0
-    half = txt_mine.shape[0]
-    for txt, out, at in ((txt_theirs, theirs, 0), (txt_mine, mine, half)):
-        for k in range(0, half, CHUNK):
-            dots = contract(txt[k : k + CHUNK, :width], img[:, :width], (1, 1))
-            sig = 1.0 / (1.0 + jnp.exp(2.0 - 10.0 * dots))
-            if at:
-                i = lax.broadcasted_iota(jnp.int32, (1, dots.shape[1]), 1) - where[0]
-                j = lax.broadcasted_iota(jnp.int32, (dots.shape[0], 1), 0) - (where[1] - k)
-                j = jnp.where((j >= 0) & (j < own), j, -1)
-                i = jnp.where(i >= 0, i, -2)
-                sig = jnp.where(j == i, sig - 1.0, sig)
-            w_txt = txt[k : k + CHUNK, width : width + 1].astype(F32)
-            c = (w_txt * w_img[:1] * sig).astype(BF)
-            coef[at + k : at + k + CHUNK] = c
-            got = jnp.dot(c, img[:, :width], preferred_element_type=F32).astype(BF)
-            for e in range(0, CHUNK, own):
-                out[(k + e) // own] = got[e : e + own]
+    for k in range(0, txt.shape[0], CHUNK):
+        dots = contract(txt[k : k + CHUNK, :width], img[:, :width], (1, 1))
+        sig = 1.0 / (1.0 + jnp.exp(2.0 - 10.0 * dots))
+        if has_own:
+            i = lax.broadcasted_iota(jnp.int32, (1, dots.shape[1]), 1) - where[0]
+            j = lax.broadcasted_iota(jnp.int32, (dots.shape[0], 1), 0) - (where[1] - k)
+            j = jnp.where((j >= 0) & (j < own), j, -1)
+            i = jnp.where(i >= 0, i, -2)
+            sig = jnp.where(j == i, sig - 1.0, sig)
+        w_txt = txt[k : k + CHUNK, width : width + 1].astype(F32)
+        c = (w_txt * w_img[:1] * sig).astype(BF)
+        coef[k : k + CHUNK] = c
+        got = jnp.dot(c, img[:, :width], preferred_element_type=F32).astype(BF)
+        for e in range(0, CHUNK, own):
+            part[(k + e) // own] = got[e : e + own]
+
+
+def ending_kernel(got, unit, inv, grad_out):
+    grad = got[0].astype(F32)
+    for k in range(1, got.shape[0]):
+        grad = grad + got[k].astype(F32)
+    dot = jnp.sum(unit[...] * grad, axis=1, keepdims=True)
+    grad_out[...] = ((grad - unit[...] * dot) * inv[...]).astype(BF)
 
 
 def join_kernel(where, mine, theirs, out):
@@ -66,14 +72,13 @@
     out[pl.ds(pl.multiple_of((1 - where[0]) * n, 8), n)] = theirs[...].astype(F32)
 
 
-def image_kernel(coef, txt_theirs, txt_mine, part):
+def image_kernel(coef_t, coef_m, txt_theirs, txt_mine, part):
     width = part.shape[1]
-    half = txt_mine.shape[0]
     for r in range(0, part.shape[0], CHUNK):
         cut = slice(r, r + CHUNK)
         part[cut] = (
-            contract(coef[:half, cut], txt_theirs[:, :width], (0, 0))
-            + contract(coef[half:, cut], txt_mine[:, :width], (0, 0))
+            contract(coef_t[:, cut], txt_theirs[:, :width], (0, 0))
+            + contract(coef_m[:, cut], txt_mine[:, :width], (0, 0))
         ).astype(BF)
 
 
@@ -127,30 +132,34 @@
 
     n_img, n_txt = nz * rows, near * own
     flops = 2 * n_img * 2 * n_txt * width
-    coef, part_t, part_m = call(
-        pair_kernel,
-        [((2 * n_txt, n_img), BF), ((near, own, width), BF), ((near, own, width), BF)],
-        [
-            lax.axis_index("z") * rows + yh * own,
-            (lax.axis_index("x") * 2 + lax.axis_index("yl")) * own,
-        ],
-        all_img,
-        txt_theirs,
-        txt_mine,
-        scratch=[pltpu.VMEM((8, n_img), F32)],
-        flops=2 * flops,
-    )
+    ids = [
+        lax.axis_index("z") * rows + yh * own,
+        (lax.axis_index("x") * 2 + lax.axis_index("yl")) * own,
+    ]
+
+    def pairs(txt, has_own):
+        return call(
+            functools.partial(pair_kernel, has_own),
+            [((n_txt, n_img), BF), ((near, own, width), BF)],
+            ids,
+            all_img,
+            txt,
+            scratch=[pltpu.VMEM((8, n_img), F32)],
+            flops=flops,
+        )
+
+    coef_t, part_t = pairs(txt_theirs, False)
     from_c = lax.ppermute(part_t, "c", SWAP)
+    coef_m, part_m = pairs(txt_mine, True)
     part_txt = (part_m.astype(F32) + from_c.astype(F32)).astype(BF)
-    grad_utxt = summed(lax.all_to_all(part_txt, NEAR, 0, 0))
+    got = lax.all_to_all(part_txt, NEAR, 0, 0)
 
     (part_img,) = call(
-        image_kernel, [((n_img, width), BF)], None, coef, txt_theirs, txt_mine, flops=flops
+        image_kernel, [((n_img, width), BF)], None, coef_t, coef_m, txt_theirs, txt_mine, flops=flops
     )
     sum_img = lax.psum_scatter(part_img, "z", scatter_dimension=0, tiled=True)
 
-    txt_dot = jnp.sum(unit_txt * grad_utxt, axis=1, keepdims=True)
-    grad_out = ((grad_utxt - unit_txt * txt_dot) * inv_txt).astype(BF)
+    (grad_out,) = call(ending_kernel, [((own, width), BF)], None, got, unit_txt, inv_txt)
     other = lax.ppermute(grad_out, "yh", SWAP)
     grad_full = jnp.concatenate(
         [jnp.where(low, grad_out, other), jnp.where(low, other, grad_out)], axis=0

time: 183 us -> 180 us (0.984)
  waiting for transfers between devices: 58.3 us -> 53 us
  local copies, waits for them, and re-layouts: 10.5 us -> 13.4 us
    unnamed x18 -> x24, local copies, waits for them, and re-layouts: 8.08 us -> 10.9 us
    ppermute x1, waiting for transfers between devices: 2.47 us -> 0.01 us  [on_device(): from_c = lax.ppermute(part_t, 'c', SWAP)]
    pallas_call x3 -> x5, Pallas kernels: 13.4 us -> 14.3 us  [call(): pl.pallas_call(kernel, out_shape=[jax.ShapeDtypeStruct(*o) for o in outs]...]
  transfers between devices with their start and end apart: 14 -> 14, of which waited for: 12 -> 11; matrix products, arithmetic and copies ran while one was open for 6% -> 6% of each run, Pallas kernels for 2% -> 5%
where the time goes in v6:
time: 180 us
  waiting for transfers between devices  53 us (29%)
  starting transfers between devices  41.2 us (23%)
  blocking collectives  33.6 us (19%)
  Pallas kernels  14.3 us (8%)
  between operations  14.3 us (8%)
  local copies, waits for them, and re-layouts  13.4 us (7%)
  other arithmetic  6.03 us (3%)
  matrix products  3.97 us (2%)
    all_to_all x1, blocking collectives, spread(): return lax.all_to_all(copies, axes, 0, 0)  20 us
    all_to_all x2, waiting for transfers between devices, spread(): return lax.all_to_all(copies, axes, 0, 0)  18.3 us
    pallas_call x5, Pallas kernels, call(): pl.pallas_call(kernel, out_shape=[jax.ShapeDtypeStruct(*o) for o in outs]...  14.3 us
    all_to_all x1, blocking collectives, on_device(): mine = summed(lax.all_to_all(mine, NEAR, 0, 0)).astype(BF)  13.6 us
    unnamed x24, local copies, waits for them, and re-layouts  10.9 us
    all_gather x1, waiting for transfers between devices, on_device(): lax.all_gather(with_column(img_b, weight), 'z', axis=0, tiled=True)  10.6 us
    all_to_all x1, waiting for transfers between devices, on_device(): got = lax.all_to_all(part_txt, NEAR, 0, 0)  8.76 us
    all_to_all x2, starting transfers between devices, spread(): return lax.all_to_all(copies, axes, 0, 0)  7.77 us
  transfers between devices with their start and end apart: 14, of which 11 were waited for; matrix products, arithmetic and copies ran while one was open for 6% of the time, Pallas kernels for 5%

profile of v6, /device:TPU:1, one launch (start us, length us, event | category | flops | bytes accessed | tf_op | source)
XLA Modules:
  0.0 179.8 jit_solution(10588280246327647677)
XLA Ops:
  8.4 3.8 %collective-permute-start = (bf16[128,576]{1,0:T(8,128)(2,1)S(1)}, bf16[128,576]{1,0:T(8,128)(2,1)S(1)}, u32[]{:S(2)}, u32[]{:S(2)}) collective-permute-start(bf16[128,576]{1,0:T(8,128)(2,1)S(1)} %copy.32), channel_id=1, source_target_pairs={{0,1},{1,0},{2,3},{3,2},{4,5},{5,4},{6,7},{7,6},{8,9},{9,8},{10,11... | collective-permute-start | bytes 442376 | tf_op jit(solution)/shard_map/ppermute | solution.py:114
  12.2 1.4 fusion.13
  16.3 3.8 %collective-permute-start.1 = (bf16[64,1152]{1,0:T(8,128)(2,1)S(1)}, bf16[64,1152]{1,0:T(8,128)(2,1)S(1)}, u32[]{:S(2)}, u32[]{:S(2)}) collective-permute-start(bf16[64,1152]{1,0:T(8,128)(2,1)S(1)} %select_convert_fusion.1), channel_id=1, source_target_pairs={{0,1},{1,0},{2,3},{3,2},{4,5},{5,4},{6,7},{7,6},{8,9},{9,8},{10,11... | collective-permute-start | bytes 442376 | tf_op jit(solution)/shard_map/ppermute | solution.py:118
  20.2 2.3 %collective-permute-done.1 = bf16[64,1152]{1,0:T(8,128)(2,1)S(1)} collective-permute-done((bf16[64,1152]{1,0:T(8,128)(2,1)S(1)}, bf16[64,1152]{1,0:T(8,128)(2,1)S(1)}, u32[]{:S(2)}, u32[]{:S(2)}) %collective-permute-start.1) | collective-permute-done | bytes 147488 | tf_op jit(solution)/shard_map/ppermute | solution.py:118
  23.0 20.0 %all_to_all.25 = bf16[8,64,1280]{2,1,0:T(8,128)(2,1)S(1)} all-to-all(bf16[8,64,1280]{2,1,0:T(8,128)(2,1)S(1)} %broadcast_in_dim.12), channel_id=1, replica_groups=mesh['z'=8,'x'=4,'yl'=2,'c'=2,'yh'=2] {'x','yl'}, dimensions={0} | all-to-all | bytes 2621440 | tf_op jit(solution)/shard_map/all_to_all | solution.py:29
  43.0 4.0 %collective-permute-start.2 = (bf16[512,1280]{1,0:T(8,128)(2,1)S(1)}, bf16[512,1280]{1,0:T(8,128)(2,1)}, u32[]{:S(2)}, u32[]{:S(2)}) collective-permute-start(bf16[512,1280]{1,0:T(8,128)(2,1)S(1)} %bitcast.16), channel_id=1, source_target_pairs={{0,2},{2,0},{1,3},{3,1},{4,6},{6,4},{5,7},{7,5},{8,10},{10,8},{9,1... | collective-permute-start | bytes 3932168 | tf_op jit(solution)/shard_map/ppermute | solution.py:131
  47.0 2.7 %collective-permute-done.2.txt.txt_theirs = bf16[512,1280]{1,0:T(8,128)(2,1)} collective-permute-done((bf16[512,1280]{1,0:T(8,128)(2,1)S(1)}, bf16[512,1280]{1,0:T(8,128)(2,1)}, u32[]{:S(2)}, u32[]{:S(2)}) %collective-permute-start.2) | collective-permute-done | bytes 1310752 | tf_op jit(solution)/shard_map/ppermute | solution.py:131
  49.8 10.6 %all-gather.2.cloned.1.call-done.img = bf16[1024,1280]{1,0:T(8,128)(2,1)} async-done(((bf16[128,1280]{1,0:T(8,128)(2,1)}), bf16[1024,1280]{1,0:T(8,128)(2,1)}) %all-gather.2.cloned.1.call-update) | async-done | bytes 2621456 | tf_op jit(solution)/shard_map/all_gather | solution.py:128
  60.4 1.7 copy-done.4
  62.1 4.4 %shard_map.68 = (bf16[512,1024]{1,0:T(8,128)(2,1)S(1)}, bf16[8,64,1152]{2,1,0:T(8,128)(2,1)S(1)}) custom-call(s32[2]{0:T(128)S(1)} %pad_add_fusion.where, bf16[1024,1280]{1,0:T(8,128)(2,1)S(1)} %copy-done.4, bf16[512,1280]{1,0:T(8,128)(2,1)} %collective-permute-done.2.txt.txt_theirs), custom_call_target="tpu_custom_call" | custom-call | flops 2415919104 | bytes 8388608 | tf_op jit(solution)/shard_map/pallas_call | solution.py:87
  67.5 3.7 %collective-permute-start.3 = (bf16[8,64,1152]{2,1,0:T(8,128)(2,1)S(1)}, bf16[8,64,1152]{2,1,0:T(8,128)(2,1)S(1)}, u32[]{:S(2)}, u32[]{:S(2)}) collective-permute-start(bf16[8,64,1152]{2,1,0:T(8,128)(2,1)S(1)} %get-tuple-element.17), channel_id=1, source_target_pairs={{0,2},{2,0},{1,3},{3,1},{4,6},{6,4},{5,7},{7,5},{8,10},{10,8},{9,1... | collective-permute-start | bytes 3538952 | tf_op jit(solution)/shard_map/ppermute | solution.py:152
  71.2 3.7 %shard_map.67 = (bf16[512,1024]{1,0:T(8,128)(2,1)S(1)}, bf16[8,64,1152]{2,1,0:T(8,128)(2,1)S(1)}) custom-call(s32[2]{0:T(128)S(1)} %pad_add_fusion.where, bf16[1024,1280]{1,0:T(8,128)(2,1)S(1)} %copy-done.4, bf16[512,1280]{1,0:T(8,128)(2,1)S(1)} %bitcast.17), custom_call_target="tpu_custom_call" | custom-call | flops 2415919104 | bytes 8388608 | tf_op jit(solution)/shard_map/pallas_call | solution.py:87
  77.3 4.8 %all-to-all-start.1 = ((bf16[8,64,1152]{2,1,0:T(8,128)(2,1)}), bf16[8,64,1152]{2,1,0:T(8,128)(2,1)S(1)}, u32[]{:S(2)}, u32[]{:S(2)}) async-start(bf16[8,64,1152]{2,1,0:T(8,128)(2,1)} %add_convert_fusion), calls=%async_computation.1 | async-start | bytes 2359296 | tf_op jit(solution)/shard_map/all_to_all | solution.py:155
  82.3 1.3 copy-done.3
  86.1 4.2 %shard_map.70 = bf16[1024,1152]{1,0:T(8,128)(2,1)S(1)} custom-call(bf16[512,1024]{1,0:T(8,128)(2,1)S(1)} %copy-done.6, bf16[512,1024]{1,0:T(8,128)(2,1)S(1)} %copy-done.8, bf16[512,1280]{1,0:T(8,128)(2,1)} %collective-permute-done.2.txt.txt_theirs, bf16[512,1280]{1,0:T(8,128)(2,1)S(1)} %bitcast.18), custom_call_target="tpu_custom_call" | custom-call | flops 2415919104 | bytes 8388608 | tf_op jit(solution)/shard_map/pallas_call | solution.py:87
  90.3 1.4 copy-done.1
  91.8 8.8 %all-to-all-done.1.got = bf16[8,64,1152]{2,1,0:T(8,128)(2,1)S(1)} async-done(((bf16[8,64,1152]{2,1,0:T(8,128)(2,1)}), bf16[8,64,1152]{2,1,0:T(8,128)(2,1)S(1)}, u32[]{:S(2)}, u32[]{:S(2)}) %all-to-all-start.1) | async-done | bytes 1179680 | tf_op jit(solution)/shard_map/all_to_all | solution.py:155
  100.9 2.5 %collective-permute-start.4 = (bf16[64,1152]{1,0:T(8,128)(2,1)S(1)}, bf16[64,1152]{1,0:T(8,128)(2,1)S(1)}, u32[]{:S(2)}, u32[]{:S(2)}) collective-permute-start(bf16[64,1152]{1,0:T(8,128)(2,1)S(1)} %shard_map.69), channel_id=1, source_target_pairs={{0,1},{1,0},{2,3},{3,2},{4,5},{5,4},{6,7},{7,6},{8,9},{9,8},{10,11... | collective-permute-start | bytes 442376 | tf_op jit(solution)/shard_map/ppermute | solution.py:163
  103.4 3.0 %collective-permute-done.4 = bf16[64,1152]{1,0:T(8,128)(2,1)S(1)} collective-permute-done((bf16[64,1152]{1,0:T(8,128)(2,1)S(1)}, bf16[64,1152]{1,0:T(8,128)(2,1)S(1)}, u32[]{:S(2)}, u32[]{:S(2)}) %collective-permute-start.4) | collective-permute-done | bytes 147488 | tf_op jit(solution)/shard_map/ppermute | solution.py:163
  106.5 1.4 convolution_bitcast_fusion
  108.0 2.4 %collective-permute-start.5 = (bf16[288,1152]{1,0:T(8,128)(2,1)S(1)}, bf16[288,1152]{1,0:T(8,128)(2,1)S(1)}, u32[]{:S(2)}, u32[]{:S(2)}) collective-permute-start(bf16[288,1152]{1,0:T(8,128)(2,1)S(1)} %select_convert_fusion), channel_id=1, source_target_pairs={{0,2},{2,0},{1,3},{3,1},{4,6},{6,4},{5,7},{7,5},{8,10},{10,8},{9,1... | collective-permute-start | bytes 1990664 | tf_op jit(solution)/shard_map/ppermute | solution.py:171
  110.4 1.7 collective-permute-done.5
  112.4 13.6 %all_to_all.26 = bf16[8,36,1152]{2,1,0:T(8,128)(2,1)S(1)} all-to-all(bf16[8,36,1152]{2,1,0:T(8,128)(2,1)S(1)} %reshape.41), channel_id=1, replica_groups=mesh['z'=8,'x'=4,'yl'=2,'c'=2,'yh'=2] {'x','yl'}, dimensions={0} | all-to-all | bytes 1327104 | tf_op jit(solution)/shard_map/all_to_all | solution.py:174
  127.1 4.1 %all-to-all-start.3 = ((bf16[8,36,1152]{2,1,0:T(8,128)(2,1)}), bf16[8,36,1152]{2,1,0:T(8,128)(2,1)S(1)}, u32[]{:S(2)}, u32[]{:S(2)}) async-start(bf16[8,36,1152]{2,1,0:T(8,128)(2,1)} %broadcast_in_dim.13), calls=%async_computation.3 | async-start | bytes 1474560 | tf_op jit(solution)/shard_map/all_to_all | solution.py:29
  132.3 2.5 %collective-permute-start.6 = (bf16[128,576]{1,0:T(8,128)(2,1)S(1)}, bf16[128,576]{1,0:T(8,128)(2,1)S(1)}, u32[]{:S(2)}, u32[]{:S(2)}) collective-permute-start(bf16[128,576]{1,0:T(8,128)(2,1)S(1)} %broadcast_select_fusion), channel_id=1, source_target_pairs={{0,1},{1,0},{2,3},{3,2},{4,5},{5,4},{6,7},{7,6},{8,9},{9,8},{10,11... | collective-permute-start | bytes 442376 | tf_op jit(solution)/shard_map/ppermute | solution.py:178
  134.8 3.3 %collective-permute-done.6 = bf16[128,576]{1,0:T(8,128)(2,1)S(1)} collective-permute-done((bf16[128,576]{1,0:T(8,128)(2,1)S(1)}, bf16[128,576]{1,0:T(8,128)(2,1)S(1)}, u32[]{:S(2)}, u32[]{:S(2)}) %collective-permute-start.6) | collective-permute-done | bytes 147488 | tf_op jit(solution)/shard_map/ppermute | solution.py:178
  139.3 2.5 %collective-permute-start.7 = (f32[128]{0:T(128)S(1)}, f32[128]{0:T(128)S(1)}, u32[]{:S(2)}, u32[]{:S(2)}) collective-permute-start(f32[128]{0:T(128)S(1)} %multiply_reduce_fusion), channel_id=1, source_target_pairs={{0,1},{1,0},{2,3},{3,2},{4,5},{5,4},{6,7},{7,6},{8,9},{9,8},{10,11... | collective-permute-start | bytes 1544 | tf_op jit(solution)/shard_map/ppermute | solution.py:182
  141.9 10.0 %all-to-all-done.3 = bf16[8,36,1152]{2,1,0:T(8,128)(2,1)S(1)} async-done(((bf16[8,36,1152]{2,1,0:T(8,128)(2,1)}), bf16[8,36,1152]{2,1,0:T(8,128)(2,1)S(1)}, u32[]{:S(2)}, u32[]{:S(2)}) %all-to-all-start.3) | async-done | bytes 663584 | tf_op jit(solution)/shard_map/all_to_all | solution.py:29
  152.9 3.7 %all-to-all-start.4 = ((bf16[8,36,1152]{2,1,0:T(8,128)(2,1)}), bf16[8,36,1152]{2,1,0:T(8,128)(2,1)S(1)}, u32[]{:S(2)}, u32[]{:S(2)}) async-start(bf16[8,36,1152]{2,1,0:T(8,128)(2,1)} %broadcast_in_dim.14), calls=%async_computation.5 | async-start | bytes 1474560 | tf_op jit(solution)/shard_map/all_to_all | solution.py:29
  158.1 8.2 %all-to-all-done.4 = bf16[8,36,1152]{2,1,0:T(8,128)(2,1)S(1)} async-done(((bf16[8,36,1152]{2,1,0:T(8,128)(2,1)}), bf16[8,36,1152]{2,1,0:T(8,128)(2,1)S(1)}, u32[]{:S(2)}, u32[]{:S(2)}) %all-to-all-start.4) | async-done | bytes 663584 | tf_op jit(solution)/shard_map/all_to_all | solution.py:29
  166.4 3.1 %collective-permute-start.8 = (bf16[288,1152]{1,0:T(8,128)(2,1)S(1)}, bf16[288,1152]{1,0:T(8,128)(2,1)S(1)}, u32[]{:S(2)}, u32[]{:S(2)}) collective-permute-start(bf16[288,1152]{1,0:T(8,128)(2,1)S(1)} %reshape.42.mine), channel_id=1, source_target_pairs={{0,2},{2,0},{1,3},{3,1},{4,6},{6,4},{5,7},{7,5},{8,10},{10,8},{9,1... | collective-permute-start | bytes 1990664 | tf_op jit(solution)/shard_map/ppermute | solution.py:188
  171.3 1.7 shard_map.71
  (63 shorter events, 19.0 us)
Async XLA Ops:
  7.2 5.1 %copy-start = (bf16[576,1152]{1,0:T(8,128)(2,1)S(1)}, bf16[576,1152]{1,0:T(8,128)(2,1)}, u32[]{:S(2)}) copy-start(bf16[576,1152]{1,0:T(8,128)(2,1)} %param.6) | copy-start | bytes 3981316
  7.2 53.2 %all-gather.2.cloned.1.call-start = ((), (), s32[]{:S(2)}) async-start(), calls=%async_computation.6 | async-start | bytes 2949120 | tf_op jit(solution)/shard_map/all_gather | solution.py:128
  8.4 5.2 %copy-start.10 = (s32[128]{0:T(128)S(1)}, s32[128]{0:T(128)}, u32[]{:S(2)}) copy-start(s32[128]{0:T(128)} %param.7) | copy-start | bytes 1540
  8.4 6.7 %collective-permute-start = (bf16[128,576]{1,0:T(8,128)(2,1)S(1)}, bf16[128,576]{1,0:T(8,128)(2,1)S(1)}, u32[]{:S(2)}, u32[]{:S(2)}) collective-permute-start(bf16[128,576]{1,0:T(8,128)(2,1)S(1)} %copy.32), channel_id=1, source_target_pairs={{0,1},{1,0},{2,3},{3,2},{4,5},{5,4},{6,7},{7,6},{8,9},{9,8},{10,11... | collective-permute-start | bytes 442376 | tf_op jit(solution)/shard_map/ppermute | solution.py:114
  16.3 6.3 %collective-permute-start.1 = (bf16[64,1152]{1,0:T(8,128)(2,1)S(1)}, bf16[64,1152]{1,0:T(8,128)(2,1)S(1)}, u32[]{:S(2)}, u32[]{:S(2)}) collective-permute-start(bf16[64,1152]{1,0:T(8,128)(2,1)S(1)} %select_convert_fusion.1), channel_id=1, source_target_pairs={{0,1},{1,0},{2,3},{3,2},{4,5},{5,4},{6,7},{7,6},{8,9},{9,8},{10,11... | collective-permute-start | bytes 442376 | tf_op jit(solution)/shard_map/ppermute | solution.py:118
  43.0 28.3 %copy-start.2 = (bf16[8,64,1280]{2,1,0:T(8,128)(2,1)}, bf16[8,64,1280]{2,1,0:T(8,128)(2,1)S(1)}, u32[]{:S(2)}) copy-start(bf16[8,64,1280]{2,1,0:T(8,128)(2,1)S(1)} %all_to_all.25) | copy-start | bytes 3932164
  43.0 6.8 %collective-permute-start.2 = (bf16[512,1280]{1,0:T(8,128)(2,1)S(1)}, bf16[512,1280]{1,0:T(8,128)(2,1)}, u32[]{:S(2)}, u32[]{:S(2)}) collective-permute-start(bf16[512,1280]{1,0:T(8,128)(2,1)S(1)} %bitcast.16), channel_id=1, source_target_pairs={{0,2},{2,0},{1,3},{3,1},{4,6},{6,4},{5,7},{7,5},{8,10},{10,8},{9,1... | collective-permute-start | bytes 3932168 | tf_op jit(solution)/shard_map/ppermute | solution.py:131
  60.4 1.7 copy-start.4
  66.6 1.0 copy-start.5
  67.5 8.4 %collective-permute-start.3 = (bf16[8,64,1152]{2,1,0:T(8,128)(2,1)S(1)}, bf16[8,64,1152]{2,1,0:T(8,128)(2,1)S(1)}, u32[]{:S(2)}, u32[]{:S(2)}) collective-permute-start(bf16[8,64,1152]{2,1,0:T(8,128)(2,1)S(1)} %get-tuple-element.17), channel_id=1, source_target_pairs={{0,2},{2,0},{1,3},{3,1},{4,6},{6,4},{5,7},{7,5},{8,10},{10,8},{9,1... | collective-permute-start | bytes 3538952 | tf_op jit(solution)/shard_map/ppermute | solution.py:152
  75.0 1.0 copy-start.7
  77.3 23.3 %all-to-all-start.1 = ((bf16[8,64,1152]{2,1,0:T(8,128)(2,1)}), bf16[8,64,1152]{2,1,0:T(8,128)(2,1)S(1)}, u32[]{:S(2)}, u32[]{:S(2)}) async-start(bf16[8,64,1152]{2,1,0:T(8,128)(2,1)} %add_convert_fusion), calls=%async_computation.1 | async-start | bytes 2359296 | tf_op jit(solution)/shard_map/all_to_all | solution.py:155
  82.1 49.1 %reduce-scatter.2.cloned.1.call-start = ((), (), s32[]{:S(2)}) async-start(), calls=%async_computation.7 | async-start | bytes 2654208 | tf_op jit(solution)/shard_map/reduce_scatter | solution.py:160
  82.3 1.3 copy-start.3
  83.6 1.2 copy-start.6
  84.8 1.2 copy-start.8
  90.3 1.4 copy-start.1
  100.9 5.6 %collective-permute-start.4 = (bf16[64,1152]{1,0:T(8,128)(2,1)S(1)}, bf16[64,1152]{1,0:T(8,128)(2,1)S(1)}, u32[]{:S(2)}, u32[]{:S(2)}) collective-permute-start(bf16[64,1152]{1,0:T(8,128)(2,1)S(1)} %shard_map.69), channel_id=1, source_target_pairs={{0,1},{1,0},{2,3},{3,2},{4,5},{5,4},{6,7},{7,6},{8,9},{9,8},{10,11... | collective-permute-start | bytes 442376 | tf_op jit(solution)/shard_map/ppermute | solution.py:163
  108.0 4.1 %collective-permute-start.5 = (bf16[288,1152]{1,0:T(8,128)(2,1)S(1)}, bf16[288,1152]{1,0:T(8,128)(2,1)S(1)}, u32[]{:S(2)}, u32[]{:S(2)}) collective-permute-start(bf16[288,1152]{1,0:T(8,128)(2,1)S(1)} %select_convert_fusion), channel_id=1, source_target_pairs={{0,2},{2,0},{1,3},{3,1},{4,6},{6,4},{5,7},{7,5},{8,10},{10,8},{9,1... | collective-permute-start | bytes 1990664 | tf_op jit(solution)/shard_map/ppermute | solution.py:171
  127.1 24.8 %all-to-all-start.3 = ((bf16[8,36,1152]{2,1,0:T(8,128)(2,1)}), bf16[8,36,1152]{2,1,0:T(8,128)(2,1)S(1)}, u32[]{:S(2)}, u32[]{:S(2)}) async-start(bf16[8,36,1152]{2,1,0:T(8,128)(2,1)} %broadcast_in_dim.13), calls=%async_computation.3 | async-start | bytes 1474560 | tf_op jit(solution)/shard_map/all_to_all | solution.py:29
  132.3 5.8 %collective-permute-start.6 = (bf16[128,576]{1,0:T(8,128)(2,1)S(1)}, bf16[128,576]{1,0:T(8,128)(2,1)S(1)}, u32[]{:S(2)}, u32[]{:S(2)}) collective-permute-start(bf16[128,576]{1,0:T(8,128)(2,1)S(1)} %broadcast_select_fusion), channel_id=1, source_target_pairs={{0,1},{1,0},{2,3},{3,2},{4,5},{5,4},{6,7},{7,6},{8,9},{9,8},{10,11... | collective-permute-start | bytes 442376 | tf_op jit(solution)/shard_map/ppermute | solution.py:178
  139.3 12.7 %collective-permute-start.7 = (f32[128]{0:T(128)S(1)}, f32[128]{0:T(128)S(1)}, u32[]{:S(2)}, u32[]{:S(2)}) collective-permute-start(f32[128]{0:T(128)S(1)} %multiply_reduce_fusion), channel_id=1, source_target_pairs={{0,1},{1,0},{2,3},{3,2},{4,5},{5,4},{6,7},{7,6},{8,9},{9,8},{10,11... | collective-permute-start | bytes 1544 | tf_op jit(solution)/shard_map/ppermute | solution.py:182
  152.9 13.3 %all-to-all-start.4 = ((bf16[8,36,1152]{2,1,0:T(8,128)(2,1)}), bf16[8,36,1152]{2,1,0:T(8,128)(2,1)S(1)}, u32[]{:S(2)}, u32[]{:S(2)}) async-start(bf16[8,36,1152]{2,1,0:T(8,128)(2,1)} %broadcast_in_dim.14), calls=%async_computation.5 | async-start | bytes 1474560 | tf_op jit(solution)/shard_map/all_to_all | solution.py:29
  156.6 1.2 copy-start.9
  166.4 4.9 %collective-permute-start.8 = (bf16[288,1152]{1,0:T(8,128)(2,1)S(1)}, bf16[288,1152]{1,0:T(8,128)(2,1)S(1)}, u32[]{:S(2)}, u32[]{:S(2)}) collective-permute-start(bf16[288,1152]{1,0:T(8,128)(2,1)S(1)} %reshape.42.mine), channel_id=1, source_target_pairs={{0,2},{2,0},{1,3},{3,1},{4,6},{6,4},{5,7},{7,5},{8,10},{10,8},{9,1... | collective-permute-start | bytes 1990664 | tf_op jit(solution)/shard_map/ppermute | solution.py:188
Sparse Core Ops, SparseCore 0:
  16.4 43.9 all-gather.1
  91.8 37.0 reduce-scatter.1

commit v7 on v6

--- a/solution.py
+++ b/solution.py
@@ -174,14 +174,12 @@
     mine = summed(lax.all_to_all(mine, NEAR, 0, 0)).astype(BF)
     mine = summed(spread(mine, "z", nz)).astype(BF)
 
-    left, right = sum_img[:, :half], sum_img[:, half:]
-    from_yh = lax.ppermute(jnp.where(low, right, left), "yh", SWAP)
-    grad_uimg = jnp.where(low, left, right).astype(F32) + from_yh.astype(F32)
-    unit_img = images.astype(F32) * inv_img
-    dot = jnp.sum(unit_img * grad_uimg, axis=1)
-    dot_other = lax.ppermute(dot, "yh", SWAP)
-    mine, dot_other = lax.optimization_barrier((mine, dot_other))
-    grad_image = (grad_uimg - unit_img * (dot + dot_other)[:, None]) * inv_img
+    from_yh = lax.ppermute(sum_img, "yh", SWAP)
+    mine, from_yh = lax.optimization_barrier((mine, from_yh))
+    grad_uimg = sum_img.astype(F32) + from_yh.astype(F32)
+    dot = jnp.sum(img32 * grad_uimg, axis=1, keepdims=True) * inv_img
+    grad_uimg = jnp.where(low, grad_uimg[:, :half], grad_uimg[:, half:])
+    grad_image = (grad_uimg - images.astype(F32) * inv_img * dot) * inv_img
 
     mine = spread(mine, NEAR, near).reshape(half // 2, width)
     mine, grad_image, grad_text = lax.optimization_barrier((mine, grad_image, grad_text))

time: 180 us -> 183 us (1.017)
  waiting for transfers between devices: 53 us -> 59 us
  starting transfers between devices: 41.2 us -> 38.4 us
  other arithmetic: 6.03 us -> 3.93 us
    all_to_all x2, waiting for transfers between devices: 18.3 us -> 27.5 us  [spread(): return lax.all_to_all(copies, axes, 0, 0)]
    ppermute x2 -> x1, waiting for transfers between devices: 3.25 us -> 0.01 us  [on_device(): from_yh = lax.ppermute(sum_img, 'yh', SWAP)]
    ppermute x2 -> x1, starting transfers between devices: 5.02 us -> 2.51 us  [on_device(): from_yh = lax.ppermute(sum_img, 'yh', SWAP)]
    unnamed x24 -> x32, local copies, waits for them, and re-layouts: 10.9 us -> 11.6 us
  transfers between devices with their start and end apart: 14 -> 13, of which waited for: 11 -> 10; matrix products, arithmetic and copies ran while one was open for 6% -> 4% of each run, Pallas kernels for 5% -> 5%
where the time goes in v7:
time: 183 us; the launch traced here: 182 us
  waiting for transfers between devices  59 us (32%)
  starting transfers between devices  38.4 us (21%)
  blocking collectives  33.6 us (18%)
  Pallas kernels  14.5 us (8%)
  between operations  14.3 us (8%)
  local copies, waits for them, and re-layouts  14.1 us (8%)
  matrix products  3.97 us (2%)
  other arithmetic  3.93 us (2%)
    all_to_all x2, waiting for transfers between devices, spread(): return lax.all_to_all(copies, axes, 0, 0)  27.5 us
    all_to_all x1, blocking collectives, spread(): return lax.all_to_all(copies, axes, 0, 0)  20 us
    pallas_call x5, Pallas kernels, call(): pl.pallas_call(kernel, out_shape=[jax.ShapeDtypeStruct(*o) for o in outs]...  14.5 us
    all_to_all x1, blocking collectives, on_device(): mine = summed(lax.all_to_all(mine, NEAR, 0, 0)).astype(BF)  13.6 us
    unnamed x32, local copies, waits for them, and re-layouts  11.6 us
    all_gather x1, waiting for transfers between devices, on_device(): lax.all_gather(with_column(img_b, weight), 'z', axis=0, tiled=True)  10.6 us
    all_to_all x2, starting transfers between devices, spread(): return lax.all_to_all(copies, axes, 0, 0)  8.91 us
    all_to_all x1, waiting for transfers between devices, on_device(): got = lax.all_to_all(part_txt, NEAR, 0, 0)  8.77 us
  transfers between devices with their start and end apart: 13, of which 10 were waited for; matrix products, arithmetic and copies ran while one was open for 4% of the time, Pallas kernels for 5%

profile of v7, /device:TPU:1, one launch (start us, length us, event | category | flops | bytes accessed | tf_op | source)
XLA Modules:
  0.0 181.9 jit_solution(3668722038937140096)
XLA Ops:
  8.4 3.8 %collective-permute-start = (bf16[128,576]{1,0:T(8,128)(2,1)S(1)}, bf16[128,576]{1,0:T(8,128)(2,1)S(1)}, u32[]{:S(2)}, u32[]{:S(2)}) collective-permute-start(bf16[128,576]{1,0:T(8,128)(2,1)S(1)} %copy.32), channel_id=1, source_target_pairs={{0,1},{1,0},{2,3},{3,2},{4,5},{5,4},{6,7},{7,6},{8,9},{9,8},{10,11... | collective-permute-start | bytes 442376 | tf_op jit(solution)/shard_map/ppermute | solution.py:114
  12.2 1.4 fusion.17
  13.8 1.3 collective-permute-done
  16.3 3.8 %collective-permute-start.1 = (bf16[64,1152]{1,0:T(8,128)(2,1)S(1)}, bf16[64,1152]{1,0:T(8,128)(2,1)S(1)}, u32[]{:S(2)}, u32[]{:S(2)}) collective-permute-start(bf16[64,1152]{1,0:T(8,128)(2,1)S(1)} %select_convert_fusion.1), channel_id=1, source_target_pairs={{0,1},{1,0},{2,3},{3,2},{4,5},{5,4},{6,7},{7,6},{8,9},{9,8},{10,11... | collective-permute-start | bytes 442376 | tf_op jit(solution)/shard_map/ppermute | solution.py:118
  20.2 2.3 %collective-permute-done.1 = bf16[64,1152]{1,0:T(8,128)(2,1)S(1)} collective-permute-done((bf16[64,1152]{1,0:T(8,128)(2,1)S(1)}, bf16[64,1152]{1,0:T(8,128)(2,1)S(1)}, u32[]{:S(2)}, u32[]{:S(2)}) %collective-permute-start.1) | collective-permute-done | bytes 147488 | tf_op jit(solution)/shard_map/ppermute | solution.py:118
  23.0 20.0 %all_to_all.25 = bf16[8,64,1280]{2,1,0:T(8,128)(2,1)S(1)} all-to-all(bf16[8,64,1280]{2,1,0:T(8,128)(2,1)S(1)} %broadcast_in_dim.12), channel_id=1, replica_groups=mesh['z'=8,'x'=4,'yl'=2,'c'=2,'yh'=2] {'x','yl'}, dimensions={0} | all-to-all | bytes 2621440 | tf_op jit(solution)/shard_map/all_to_all | solution.py:29
  43.0 4.0 %collective-permute-start.2 = (bf16[512,1280]{1,0:T(8,128)(2,1)S(1)}, bf16[512,1280]{1,0:T(8,128)(2,1)}, u32[]{:S(2)}, u32[]{:S(2)}) collective-permute-start(bf16[512,1280]{1,0:T(8,128)(2,1)S(1)} %bitcast.16), channel_id=1, source_target_pairs={{0,2},{2,0},{1,3},{3,1},{4,6},{6,4},{5,7},{7,5},{8,10},{10,8},{9,1... | collective-permute-start | bytes 3932168 | tf_op jit(solution)/shard_map/ppermute | solution.py:131
  47.0 2.7 %collective-permute-done.2.txt.txt_theirs = bf16[512,1280]{1,0:T(8,128)(2,1)} collective-permute-done((bf16[512,1280]{1,0:T(8,128)(2,1)S(1)}, bf16[512,1280]{1,0:T(8,128)(2,1)}, u32[]{:S(2)}, u32[]{:S(2)}) %collective-permute-start.2) | collective-permute-done | bytes 1310752 | tf_op jit(solution)/shard_map/ppermute | solution.py:131
  49.8 10.6 %all-gather.2.cloned.1.call-done.img = bf16[1024,1280]{1,0:T(8,128)(2,1)} async-done(((bf16[128,1280]{1,0:T(8,128)(2,1)}), bf16[1024,1280]{1,0:T(8,128)(2,1)}) %all-gather.2.cloned.1.call-update) | async-done | bytes 2621456 | tf_op jit(solution)/shard_map/all_gather | solution.py:128
  60.4 1.7 copy-done.4
  62.1 4.5 %shard_map.68 = (bf16[512,1024]{1,0:T(8,128)(2,1)S(1)}, bf16[8,64,1152]{2,1,0:T(8,128)(2,1)S(1)}) custom-call(s32[2]{0:T(128)S(1)} %pad_add_fusion.where, bf16[1024,1280]{1,0:T(8,128)(2,1)S(1)} %copy-done.4, bf16[512,1280]{1,0:T(8,128)(2,1)} %collective-permute-done.2.txt.txt_theirs), custom_call_target="tpu_custom_call" | custom-call | flops 2415919104 | bytes 8388608 | tf_op jit(solution)/shard_map/pallas_call | solution.py:87
  67.6 3.7 %collective-permute-start.3 = (bf16[8,64,1152]{2,1,0:T(8,128)(2,1)S(1)}, bf16[8,64,1152]{2,1,0:T(8,128)(2,1)S(1)}, u32[]{:S(2)}, u32[]{:S(2)}) collective-permute-start(bf16[8,64,1152]{2,1,0:T(8,128)(2,1)S(1)} %get-tuple-element.17), channel_id=1, source_target_pairs={{0,2},{2,0},{1,3},{3,1},{4,6},{6,4},{5,7},{7,5},{8,10},{10,8},{9,1... | collective-permute-start | bytes 3538952 | tf_op jit(solution)/shard_map/ppermute | solution.py:152
  71.3 3.8 %shard_map.67 = (bf16[512,1024]{1,0:T(8,128)(2,1)S(1)}, bf16[8,64,1152]{2,1,0:T(8,128)(2,1)S(1)}) custom-call(s32[2]{0:T(128)S(1)} %pad_add_fusion.where, bf16[1024,1280]{1,0:T(8,128)(2,1)S(1)} %copy-done.4, bf16[512,1280]{1,0:T(8,128)(2,1)S(1)} %bitcast.17), custom_call_target="tpu_custom_call" | custom-call | flops 2415919104 | bytes 8388608 | tf_op jit(solution)/shard_map/pallas_call | solution.py:87
  76.1 1.3 add_convert_fusion
  77.4 4.8 %all-to-all-start.1 = ((bf16[8,64,1152]{2,1,0:T(8,128)(2,1)}), bf16[8,64,1152]{2,1,0:T(8,128)(2,1)S(1)}, u32[]{:S(2)}, u32[]{:S(2)}) async-start(bf16[8,64,1152]{2,1,0:T(8,128)(2,1)} %add_convert_fusion), calls=%async_computation.1 | async-start | bytes 2359296 | tf_op jit(solution)/shard_map/all_to_all | solution.py:155
  82.5 1.3 copy-done.3
  86.2 4.2 %shard_map.70 = bf16[1024,1152]{1,0:T(8,128)(2,1)S(1)} custom-call(bf16[512,1024]{1,0:T(8,128)(2,1)S(1)} %copy-done.6, bf16[512,1024]{1,0:T(8,128)(2,1)S(1)} %copy-done.8, bf16[512,1280]{1,0:T(8,128)(2,1)} %collective-permute-done.2.txt.txt_theirs, bf16[512,1280]{1,0:T(8,128)(2,1)S(1)} %bitcast.18), custom_call_target="tpu_custom_call" | custom-call | flops 2415919104 | bytes 8388608 | tf_op jit(solution)/shard_map/pallas_call | solution.py:87
  90.5 1.4 copy-done.1
  92.0 8.8 %all-to-all-done.1.got = bf16[8,64,1152]{2,1,0:T(8,128)(2,1)S(1)} async-done(((bf16[8,64,1152]{2,1,0:T(8,128)(2,1)}), bf16[8,64,1152]{2,1,0:T(8,128)(2,1)S(1)}, u32[]{:S(2)}, u32[]{:S(2)}) %all-to-all-start.1) | async-done | bytes 1179680 | tf_op jit(solution)/shard_map/all_to_all | solution.py:155
  101.0 2.5 %collective-permute-start.4 = (bf16[64,1152]{1,0:T(8,128)(2,1)S(1)}, bf16[64,1152]{1,0:T(8,128)(2,1)S(1)}, u32[]{:S(2)}, u32[]{:S(2)}) collective-permute-start(bf16[64,1152]{1,0:T(8,128)(2,1)S(1)} %shard_map.69), channel_id=1, source_target_pairs={{0,1},{1,0},{2,3},{3,2},{4,5},{5,4},{6,7},{7,6},{8,9},{9,8},{10,11... | collective-permute-start | bytes 442376 | tf_op jit(solution)/shard_map/ppermute | solution.py:163
  103.6 3.1 %collective-permute-done.4 = bf16[64,1152]{1,0:T(8,128)(2,1)S(1)} collective-permute-done((bf16[64,1152]{1,0:T(8,128)(2,1)S(1)}, bf16[64,1152]{1,0:T(8,128)(2,1)S(1)}, u32[]{:S(2)}, u32[]{:S(2)}) %collective-permute-start.4) | collective-permute-done | bytes 147488 | tf_op jit(solution)/shard_map/ppermute | solution.py:163
  107.4 1.4 convolution_bitcast_fusion
  108.9 2.4 %collective-permute-start.5 = (bf16[288,1152]{1,0:T(8,128)(2,1)S(1)}, bf16[288,1152]{1,0:T(8,128)(2,1)S(1)}, u32[]{:S(2)}, u32[]{:S(2)}) collective-permute-start(bf16[288,1152]{1,0:T(8,128)(2,1)S(1)} %select_convert_fusion), channel_id=1, source_target_pairs={{0,2},{2,0},{1,3},{3,1},{4,6},{6,4},{5,7},{7,5},{8,10},{10,8},{9,1... | collective-permute-start | bytes 1990664 | tf_op jit(solution)/shard_map/ppermute | solution.py:171
  111.3 1.7 collective-permute-done.5
  113.3 13.6 %all_to_all.26 = bf16[8,36,1152]{2,1,0:T(8,128)(2,1)S(1)} all-to-all(bf16[8,36,1152]{2,1,0:T(8,128)(2,1)S(1)} %reshape.46), channel_id=1, replica_groups=mesh['z'=8,'x'=4,'yl'=2,'c'=2,'yh'=2] {'x','yl'}, dimensions={0} | all-to-all | bytes 1327104 | tf_op jit(solution)/shard_map/all_to_all | solution.py:174
  128.0 4.1 %all-to-all-start.3 = ((bf16[8,36,1152]{2,1,0:T(8,128)(2,1)}), bf16[8,36,1152]{2,1,0:T(8,128)(2,1)S(1)}, u32[]{:S(2)}, u32[]{:S(2)}) async-start(bf16[8,36,1152]{2,1,0:T(8,128)(2,1)} %broadcast_in_dim.13), calls=%async_computation.3 | async-start | bytes 1474560 | tf_op jit(solution)/shard_map/all_to_all | solution.py:29
  132.1 2.5 %collective-permute-start.6 = (bf16[128,1152]{1,0:T(8,128)(2,1)}, bf16[128,1152]{1,0:T(8,128)(2,1)S(1)}, u32[]{:S(2)}, u32[]{:S(2)}) collective-permute-start(bf16[128,1152]{1,0:T(8,128)(2,1)} %reduce-scatter.2.cloned.1.call-done), channel_id=1, source_target_pairs={{0,1},{1,0},{2,3},{3,2},{4,5},{5,4},{6,7},{7,6},{8,9},{9,8},{10,11... | collective-permute-start | bytes 884744 | tf_op jit(solution)/shard_map/ppermute | solution.py:177
  135.9 17.0 %all-to-all-done.3 = bf16[8,36,1152]{2,1,0:T(8,128)(2,1)S(1)} async-done(((bf16[8,36,1152]{2,1,0:T(8,128)(2,1)}), bf16[8,36,1152]{2,1,0:T(8,128)(2,1)S(1)}, u32[]{:S(2)}, u32[]{:S(2)}) %all-to-all-start.3) | async-done | bytes 663584 | tf_op jit(solution)/shard_map/all_to_all | solution.py:29
  153.9 4.8 %all-to-all-start.4 = ((bf16[8,36,1152]{2,1,0:T(8,128)(2,1)}), bf16[8,36,1152]{2,1,0:T(8,128)(2,1)S(1)}, u32[]{:S(2)}, u32[]{:S(2)}) async-start(bf16[8,36,1152]{2,1,0:T(8,128)(2,1)} %broadcast_in_dim.14), calls=%async_computation.5 | async-start | bytes 1474560 | tf_op jit(solution)/shard_map/all_to_all | solution.py:29
  159.1 10.6 %all-to-all-done.4 = bf16[8,36,1152]{2,1,0:T(8,128)(2,1)S(1)} async-done(((bf16[8,36,1152]{2,1,0:T(8,128)(2,1)}), bf16[8,36,1152]{2,1,0:T(8,128)(2,1)S(1)}, u32[]{:S(2)}, u32[]{:S(2)}) %all-to-all-start.4) | async-done | bytes 663584 | tf_op jit(solution)/shard_map/all_to_all | solution.py:29
  169.9 1.8 collective-permute-start.7
  173.4 1.7 shard_map.71
  (68 shorter events, 14.9 us)
Async XLA Ops:
  7.2 5.1 %copy-start = (bf16[576,1152]{1,0:T(8,128)(2,1)S(1)}, bf16[576,1152]{1,0:T(8,128)(2,1)}, u32[]{:S(2)}) copy-start(bf16[576,1152]{1,0:T(8,128)(2,1)} %param.6) | copy-start | bytes 3981316
  7.2 53.2 %all-gather.2.cloned.1.call-start = ((), (), s32[]{:S(2)}) async-start(), calls=%async_computation.6 | async-start | bytes 2949120 | tf_op jit(solution)/shard_map/all_gather | solution.py:128
  8.4 5.2 %copy-start.14 = (s32[128]{0:T(128)S(1)}, s32[128]{0:T(128)}, u32[]{:S(2)}) copy-start(s32[128]{0:T(128)} %param.7) | copy-start | bytes 1540
  8.4 6.7 %collective-permute-start = (bf16[128,576]{1,0:T(8,128)(2,1)S(1)}, bf16[128,576]{1,0:T(8,128)(2,1)S(1)}, u32[]{:S(2)}, u32[]{:S(2)}) collective-permute-start(bf16[128,576]{1,0:T(8,128)(2,1)S(1)} %copy.32), channel_id=1, source_target_pairs={{0,1},{1,0},{2,3},{3,2},{4,5},{5,4},{6,7},{7,6},{8,9},{9,8},{10,11... | collective-permute-start | bytes 442376 | tf_op jit(solution)/shard_map/ppermute | solution.py:114
  16.3 6.3 %collective-permute-start.1 = (bf16[64,1152]{1,0:T(8,128)(2,1)S(1)}, bf16[64,1152]{1,0:T(8,128)(2,1)S(1)}, u32[]{:S(2)}, u32[]{:S(2)}) collective-permute-start(bf16[64,1152]{1,0:T(8,128)(2,1)S(1)} %select_convert_fusion.1), channel_id=1, source_target_pairs={{0,1},{1,0},{2,3},{3,2},{4,5},{5,4},{6,7},{7,6},{8,9},{9,8},{10,11... | collective-permute-start | bytes 442376 | tf_op jit(solution)/shard_map/ppermute | solution.py:118
  43.0 28.3 %copy-start.2 = (bf16[8,64,1280]{2,1,0:T(8,128)(2,1)}, bf16[8,64,1280]{2,1,0:T(8,128)(2,1)S(1)}, u32[]{:S(2)}) copy-start(bf16[8,64,1280]{2,1,0:T(8,128)(2,1)S(1)} %all_to_all.25) | copy-start | bytes 3932164
  43.0 6.8 %collective-permute-start.2 = (bf16[512,1280]{1,0:T(8,128)(2,1)S(1)}, bf16[512,1280]{1,0:T(8,128)(2,1)}, u32[]{:S(2)}, u32[]{:S(2)}) collective-permute-start(bf16[512,1280]{1,0:T(8,128)(2,1)S(1)} %bitcast.16), channel_id=1, source_target_pairs={{0,2},{2,0},{1,3},{3,1},{4,6},{6,4},{5,7},{7,5},{8,10},{10,8},{9,1... | collective-permute-start | bytes 3932168 | tf_op jit(solution)/shard_map/ppermute | solution.py:131
  60.4 1.7 copy-start.4
  66.6 1.0 copy-start.5
  67.6 8.5 %collective-permute-start.3 = (bf16[8,64,1152]{2,1,0:T(8,128)(2,1)S(1)}, bf16[8,64,1152]{2,1,0:T(8,128)(2,1)S(1)}, u32[]{:S(2)}, u32[]{:S(2)}) collective-permute-start(bf16[8,64,1152]{2,1,0:T(8,128)(2,1)S(1)} %get-tuple-element.17), channel_id=1, source_target_pairs={{0,2},{2,0},{1,3},{3,1},{4,6},{6,4},{5,7},{7,5},{8,10},{10,8},{9,1... | collective-permute-start | bytes 3538952 | tf_op jit(solution)/shard_map/ppermute | solution.py:152
  75.1 1.0 copy-start.7
  77.4 23.3 %all-to-all-start.1 = ((bf16[8,64,1152]{2,1,0:T(8,128)(2,1)}), bf16[8,64,1152]{2,1,0:T(8,128)(2,1)S(1)}, u32[]{:S(2)}, u32[]{:S(2)}) async-start(bf16[8,64,1152]{2,1,0:T(8,128)(2,1)} %add_convert_fusion), calls=%async_computation.1 | async-start | bytes 2359296 | tf_op jit(solution)/shard_map/all_to_all | solution.py:155
  82.2 49.9 %reduce-scatter.2.cloned.1.call-start = ((), (), s32[]{:S(2)}) async-start(), calls=%async_computation.7 | async-start | bytes 2654208 | tf_op jit(solution)/shard_map/reduce_scatter | solution.py:160
  82.5 1.3 copy-start.3
  83.8 1.2 copy-start.6
  85.0 1.2 copy-start.8
  90.5 1.4 copy-start.1
  101.0 5.6 %collective-permute-start.4 = (bf16[64,1152]{1,0:T(8,128)(2,1)S(1)}, bf16[64,1152]{1,0:T(8,128)(2,1)S(1)}, u32[]{:S(2)}, u32[]{:S(2)}) collective-permute-start(bf16[64,1152]{1,0:T(8,128)(2,1)S(1)} %shard_map.69), channel_id=1, source_target_pairs={{0,1},{1,0},{2,3},{3,2},{4,5},{5,4},{6,7},{7,6},{8,9},{9,8},{10,11... | collective-permute-start | bytes 442376 | tf_op jit(solution)/shard_map/ppermute | solution.py:163
  106.7 0.7 copy-start.9
  106.7 0.7 copy-start.11
  108.9 4.1 %collective-permute-start.5 = (bf16[288,1152]{1,0:T(8,128)(2,1)S(1)}, bf16[288,1152]{1,0:T(8,128)(2,1)S(1)}, u32[]{:S(2)}, u32[]{:S(2)}) collective-permute-start(bf16[288,1152]{1,0:T(8,128)(2,1)S(1)} %select_convert_fusion), channel_id=1, source_target_pairs={{0,2},{2,0},{1,3},{3,1},{4,6},{6,4},{5,7},{7,5},{8,10},{10,8},{9,1... | collective-permute-start | bytes 1990664 | tf_op jit(solution)/shard_map/ppermute | solution.py:171
  127.1 7.6 %copy-start.10 = (bf16[64,1152]{1,0:T(8,128)(2,1)S(1)}, bf16[64,1152]{1,0:T(8,128)(2,1)}, u32[]{:S(2)}) copy-start(bf16[64,1152]{1,0:T(8,128)(2,1)} %copy-done.9) | copy-start | bytes 442372
  127.1 7.6 %copy-start.12 = (bf16[64,1152]{1,0:T(8,128)(2,1)S(1)}, bf16[64,1152]{1,0:T(8,128)(2,1)}, u32[]{:S(2)}) copy-start(bf16[64,1152]{1,0:T(8,128)(2,1)} %copy-done.11) | copy-start | bytes 442372
  128.0 24.8 %all-to-all-start.3 = ((bf16[8,36,1152]{2,1,0:T(8,128)(2,1)}), bf16[8,36,1152]{2,1,0:T(8,128)(2,1)S(1)}, u32[]{:S(2)}, u32[]{:S(2)}) async-start(bf16[8,36,1152]{2,1,0:T(8,128)(2,1)} %broadcast_in_dim.13), calls=%async_computation.3 | async-start | bytes 1474560 | tf_op jit(solution)/shard_map/all_to_all | solution.py:29
  132.1 20.8 %collective-permute-start.6 = (bf16[128,1152]{1,0:T(8,128)(2,1)}, bf16[128,1152]{1,0:T(8,128)(2,1)S(1)}, u32[]{:S(2)}, u32[]{:S(2)}) collective-permute-start(bf16[128,1152]{1,0:T(8,128)(2,1)} %reduce-scatter.2.cloned.1.call-done), channel_id=1, source_target_pairs={{0,1},{1,0},{2,3},{3,2},{4,5},{5,4},{6,7},{7,6},{8,9},{9,8},{10,11... | collective-permute-start | bytes 884744 | tf_op jit(solution)/shard_map/ppermute | solution.py:177
  152.9 5.8 %copy-start.13 = (bf16[128,1152]{1,0:T(8,128)(2,1)S(1)}, bf16[128,1152]{1,0:T(8,128)(2,1)}, u32[]{:S(2)}) copy-start(bf16[128,1152]{1,0:T(8,128)(2,1)} %reduce-scatter.2.cloned.1.call-done) | copy-start | bytes 884740
  153.9 15.9 %all-to-all-start.4 = ((bf16[8,36,1152]{2,1,0:T(8,128)(2,1)}), bf16[8,36,1152]{2,1,0:T(8,128)(2,1)S(1)}, u32[]{:S(2)}, u32[]{:S(2)}) async-start(bf16[8,36,1152]{2,1,0:T(8,128)(2,1)} %broadcast_in_dim.14), calls=%async_computation.5 | async-start | bytes 1474560 | tf_op jit(solution)/shard_map/all_to_all | solution.py:29
  169.9 3.5 %collective-permute-start.7 = (bf16[288,1152]{1,0:T(8,128)(2,1)S(1)}, bf16[288,1152]{1,0:T(8,128)(2,1)S(1)}, u32[]{:S(2)}, u32[]{:S(2)}) collective-permute-start(bf16[288,1152]{1,0:T(8,128)(2,1)S(1)} %reshape.47.mine), channel_id=1, source_target_pairs={{0,2},{2,0},{1,3},{3,1},{4,6},{6,4},{5,7},{7,5},{8,10},{10,8},{9,1... | collective-permute-start | bytes 1990664 | tf_op jit(solution)/shard_map/ppermute | solution.py:186
Sparse Core Ops, SparseCore 0:
  16.4 43.9 all-gather.1
  92.0 37.1 reduce-scatter.1

commit v8 on v6

--- a/solution.py
+++ b/solution.py
@@ -16,6 +16,7 @@
 SWAP = [(0, 1), (1, 0)]
 LANES = 128
 CHUNK = 256
+TEXTS = 512
 BF = jnp.bfloat16
 F32 = jnp.float32
 
@@ -41,8 +42,8 @@
     own, width = part.shape[1:]
     pick = (lax.broadcasted_iota(jnp.int32, (8, LANES), 1) == 0).astype(BF)
     w_img[...] = contract(pick, img[:, width:], (1, 1)) * 10.0
-    for k in range(0, txt.shape[0], CHUNK):
-        dots = contract(txt[k : k + CHUNK, :width], img[:, :width], (1, 1))
+    for k in range(0, txt.shape[0], TEXTS):
+        dots = contract(txt[k : k + TEXTS, :width], img[:, :width], (1, 1))
         sig = 1.0 / (1.0 + jnp.exp(2.0 - 10.0 * dots))
         if has_own:
             i = lax.broadcasted_iota(jnp.int32, (1, dots.shape[1]), 1) - where[0]
@@ -50,11 +51,11 @@
             j = jnp.where((j >= 0) & (j < own), j, -1)
             i = jnp.where(i >= 0, i, -2)
             sig = jnp.where(j == i, sig - 1.0, sig)
-        w_txt = txt[k : k + CHUNK, width : width + 1].astype(F32)
+        w_txt = txt[k : k + TEXTS, width : width + 1].astype(F32)
         c = (w_txt * w_img[:1] * sig).astype(BF)
-        coef[k : k + CHUNK] = c
+        coef[k : k + TEXTS] = c
         got = jnp.dot(c, img[:, :width], preferred_element_type=F32).astype(BF)
-        for e in range(0, CHUNK, own):
+        for e in range(0, TEXTS, own):
             part[(k + e) // own] = got[e : e + own]
 
 

time: 180 us -> 181 us (level)
  transfers between devices with their start and end apart: 14 -> 14, of which waited for: 11 -> 11; matrix products, arithmetic and copies ran while one was open for 6% -> 5% of each run, Pallas kernels for 5% -> 5%
where the time goes in v8:
time: 181 us
  waiting for transfers between devices  54.1 us (30%)
  starting transfers between devices  40.9 us (23%)
  blocking collectives  33.6 us (19%)
  Pallas kernels  14.4 us (8%)
  between operations  14.3 us (8%)
  local copies, waits for them, and re-layouts  13.4 us (7%)
  other arithmetic  6.03 us (3%)
  matrix products  3.97 us (2%)
    all_to_all x1, blocking collectives, spread(): return lax.all_to_all(copies, axes, 0, 0)  20 us
    all_to_all x2, waiting for transfers between devices, spread(): return lax.all_to_all(copies, axes, 0, 0)  19.4 us
    pallas_call x5, Pallas kernels, call(): pl.pallas_call(kernel, out_shape=[jax.ShapeDtypeStruct(*o) for o in outs]...  14.4 us
    all_to_all x1, blocking collectives, on_device(): mine = summed(lax.all_to_all(mine, NEAR, 0, 0)).astype(BF)  13.6 us
    unnamed x24, local copies, waits for them, and re-layouts  10.9 us
    all_gather x1, waiting for transfers between devices, on_device(): lax.all_gather(with_column(img_b, weight), 'z', axis=0, tiled=True)  10.6 us
    all_to_all x1, waiting for transfers between devices, on_device(): got = lax.all_to_all(part_txt, NEAR, 0, 0)  8.76 us
    all_to_all x2, starting transfers between devices, spread(): return lax.all_to_all(copies, axes, 0, 0)  8.68 us
  transfers between devices with their start and end apart: 14, of which 11 were waited for; matrix products, arithmetic and copies ran while one was open for 5% of the time, Pallas kernels for 5%

profile of v8, /device:TPU:1, one launch (start us, length us, event | category | flops | bytes accessed | tf_op | source)
XLA Modules:
  0.0 180.8 jit_solution(4323146979306405184)
XLA Ops:
  8.4 3.8 %collective-permute-start = (bf16[128,576]{1,0:T(8,128)(2,1)S(1)}, bf16[128,576]{1,0:T(8,128)(2,1)S(1)}, u32[]{:S(2)}, u32[]{:S(2)}) collective-permute-start(bf16[128,576]{1,0:T(8,128)(2,1)S(1)} %copy.32), channel_id=1, source_target_pairs={{0,1},{1,0},{2,3},{3,2},{4,5},{5,4},{6,7},{7,6},{8,9},{9,8},{10,11... | collective-permute-start | bytes 442376 | tf_op jit(solution)/shard_map/ppermute | solution.py:115
  12.2 1.4 fusion.13
  16.3 3.8 %collective-permute-start.1 = (bf16[64,1152]{1,0:T(8,128)(2,1)S(1)}, bf16[64,1152]{1,0:T(8,128)(2,1)S(1)}, u32[]{:S(2)}, u32[]{:S(2)}) collective-permute-start(bf16[64,1152]{1,0:T(8,128)(2,1)S(1)} %select_convert_fusion.1), channel_id=1, source_target_pairs={{0,1},{1,0},{2,3},{3,2},{4,5},{5,4},{6,7},{7,6},{8,9},{9,8},{10,11... | collective-permute-start | bytes 442376 | tf_op jit(solution)/shard_map/ppermute | solution.py:119
  20.2 2.3 %collective-permute-done.1 = bf16[64,1152]{1,0:T(8,128)(2,1)S(1)} collective-permute-done((bf16[64,1152]{1,0:T(8,128)(2,1)S(1)}, bf16[64,1152]{1,0:T(8,128)(2,1)S(1)}, u32[]{:S(2)}, u32[]{:S(2)}) %collective-permute-start.1) | collective-permute-done | bytes 147488 | tf_op jit(solution)/shard_map/ppermute | solution.py:119
  23.0 20.0 %all_to_all.25 = bf16[8,64,1280]{2,1,0:T(8,128)(2,1)S(1)} all-to-all(bf16[8,64,1280]{2,1,0:T(8,128)(2,1)S(1)} %broadcast_in_dim.12), channel_id=1, replica_groups=mesh['z'=8,'x'=4,'yl'=2,'c'=2,'yh'=2] {'x','yl'}, dimensions={0} | all-to-all | bytes 2621440 | tf_op jit(solution)/shard_map/all_to_all | solution.py:30
  43.0 4.0 %collective-permute-start.2 = (bf16[512,1280]{1,0:T(8,128)(2,1)S(1)}, bf16[512,1280]{1,0:T(8,128)(2,1)}, u32[]{:S(2)}, u32[]{:S(2)}) collective-permute-start(bf16[512,1280]{1,0:T(8,128)(2,1)S(1)} %bitcast.16), channel_id=1, source_target_pairs={{0,2},{2,0},{1,3},{3,1},{4,6},{6,4},{5,7},{7,5},{8,10},{10,8},{9,1... | collective-permute-start | bytes 3932168 | tf_op jit(solution)/shard_map/ppermute | solution.py:132
  47.0 2.7 %collective-permute-done.2.txt.txt_theirs = bf16[512,1280]{1,0:T(8,128)(2,1)} collective-permute-done((bf16[512,1280]{1,0:T(8,128)(2,1)S(1)}, bf16[512,1280]{1,0:T(8,128)(2,1)}, u32[]{:S(2)}, u32[]{:S(2)}) %collective-permute-start.2) | collective-permute-done | bytes 1310752 | tf_op jit(solution)/shard_map/ppermute | solution.py:132
  49.8 10.6 %all-gather.2.cloned.1.call-done.img = bf16[1024,1280]{1,0:T(8,128)(2,1)} async-done(((bf16[128,1280]{1,0:T(8,128)(2,1)}), bf16[1024,1280]{1,0:T(8,128)(2,1)}) %all-gather.2.cloned.1.call-update) | async-done | bytes 2621456 | tf_op jit(solution)/shard_map/all_gather | solution.py:129
  60.4 1.7 copy-done.4
  62.1 4.5 %shard_map.68 = (bf16[512,1024]{1,0:T(8,128)(2,1)S(1)}, bf16[8,64,1152]{2,1,0:T(8,128)(2,1)S(1)}) custom-call(s32[2]{0:T(128)S(1)} %pad_add_fusion.where, bf16[1024,1280]{1,0:T(8,128)(2,1)S(1)} %copy-done.4, bf16[512,1280]{1,0:T(8,128)(2,1)} %collective-permute-done.2.txt.txt_theirs), custom_call_target="tpu_custom_call" | custom-call | flops 2415919104 | bytes 8388608 | tf_op jit(solution)/shard_map/pallas_call | solution.py:88
  67.6 3.7 %collective-permute-start.3 = (bf16[8,64,1152]{2,1,0:T(8,128)(2,1)S(1)}, bf16[8,64,1152]{2,1,0:T(8,128)(2,1)S(1)}, u32[]{:S(2)}, u32[]{:S(2)}) collective-permute-start(bf16[8,64,1152]{2,1,0:T(8,128)(2,1)S(1)} %get-tuple-element.17), channel_id=1, source_target_pairs={{0,2},{2,0},{1,3},{3,1},{4,6},{6,4},{5,7},{7,5},{8,10},{10,8},{9,1... | collective-permute-start | bytes 3538952 | tf_op jit(solution)/shard_map/ppermute | solution.py:153
  71.3 3.8 %shard_map.67 = (bf16[512,1024]{1,0:T(8,128)(2,1)S(1)}, bf16[8,64,1152]{2,1,0:T(8,128)(2,1)S(1)}) custom-call(s32[2]{0:T(128)S(1)} %pad_add_fusion.where, bf16[1024,1280]{1,0:T(8,128)(2,1)S(1)} %copy-done.4, bf16[512,1280]{1,0:T(8,128)(2,1)S(1)} %bitcast.17), custom_call_target="tpu_custom_call" | custom-call | flops 2415919104 | bytes 8388608 | tf_op jit(solution)/shard_map/pallas_call | solution.py:88
  77.4 4.8 %all-to-all-start.1 = ((bf16[8,64,1152]{2,1,0:T(8,128)(2,1)}), bf16[8,64,1152]{2,1,0:T(8,128)(2,1)S(1)}, u32[]{:S(2)}, u32[]{:S(2)}) async-start(bf16[8,64,1152]{2,1,0:T(8,128)(2,1)} %add_convert_fusion), calls=%async_computation.1 | async-start | bytes 2359296 | tf_op jit(solution)/shard_map/all_to_all | solution.py:156
  82.4 1.3 copy-done.3
  86.2 4.2 %shard_map.70 = bf16[1024,1152]{1,0:T(8,128)(2,1)S(1)} custom-call(bf16[512,1024]{1,0:T(8,128)(2,1)S(1)} %copy-done.6, bf16[512,1024]{1,0:T(8,128)(2,1)S(1)} %copy-done.8, bf16[512,1280]{1,0:T(8,128)(2,1)} %collective-permute-done.2.txt.txt_theirs, bf16[512,1280]{1,0:T(8,128)(2,1)S(1)} %bitcast.18), custom_call_target="tpu_custom_call" | custom-call | flops 2415919104 | bytes 8388608 | tf_op jit(solution)/shard_map/pallas_call | solution.py:88
  90.4 1.4 copy-done.1
  91.9 8.8 %all-to-all-done.1.got = bf16[8,64,1152]{2,1,0:T(8,128)(2,1)S(1)} async-done(((bf16[8,64,1152]{2,1,0:T(8,128)(2,1)}), bf16[8,64,1152]{2,1,0:T(8,128)(2,1)S(1)}, u32[]{:S(2)}, u32[]{:S(2)}) %all-to-all-start.1) | async-done | bytes 1179680 | tf_op jit(solution)/shard_map/all_to_all | solution.py:156
  101.0 2.5 %collective-permute-start.4 = (bf16[64,1152]{1,0:T(8,128)(2,1)S(1)}, bf16[64,1152]{1,0:T(8,128)(2,1)S(1)}, u32[]{:S(2)}, u32[]{:S(2)}) collective-permute-start(bf16[64,1152]{1,0:T(8,128)(2,1)S(1)} %shard_map.69), channel_id=1, source_target_pairs={{0,1},{1,0},{2,3},{3,2},{4,5},{5,4},{6,7},{7,6},{8,9},{9,8},{10,11... | collective-permute-start | bytes 442376 | tf_op jit(solution)/shard_map/ppermute | solution.py:164
  103.5 3.0 %collective-permute-done.4 = bf16[64,1152]{1,0:T(8,128)(2,1)S(1)} collective-permute-done((bf16[64,1152]{1,0:T(8,128)(2,1)S(1)}, bf16[64,1152]{1,0:T(8,128)(2,1)S(1)}, u32[]{:S(2)}, u32[]{:S(2)}) %collective-permute-start.4) | collective-permute-done | bytes 147488 | tf_op jit(solution)/shard_map/ppermute | solution.py:164
  106.6 1.4 convolution_bitcast_fusion
  108.1 2.4 %collective-permute-start.5 = (bf16[288,1152]{1,0:T(8,128)(2,1)S(1)}, bf16[288,1152]{1,0:T(8,128)(2,1)S(1)}, u32[]{:S(2)}, u32[]{:S(2)}) collective-permute-start(bf16[288,1152]{1,0:T(8,128)(2,1)S(1)} %select_convert_fusion), channel_id=1, source_target_pairs={{0,2},{2,0},{1,3},{3,1},{4,6},{6,4},{5,7},{7,5},{8,10},{10,8},{9,1... | collective-permute-start | bytes 1990664 | tf_op jit(solution)/shard_map/ppermute | solution.py:172
  110.5 1.7 collective-permute-done.5
  112.5 13.6 %all_to_all.26 = bf16[8,36,1152]{2,1,0:T(8,128)(2,1)S(1)} all-to-all(bf16[8,36,1152]{2,1,0:T(8,128)(2,1)S(1)} %reshape.41), channel_id=1, replica_groups=mesh['z'=8,'x'=4,'yl'=2,'c'=2,'yh'=2] {'x','yl'}, dimensions={0} | all-to-all | bytes 1327104 | tf_op jit(solution)/shard_map/all_to_all | solution.py:175
  127.2 4.1 %all-to-all-start.3 = ((bf16[8,36,1152]{2,1,0:T(8,128)(2,1)}), bf16[8,36,1152]{2,1,0:T(8,128)(2,1)S(1)}, u32[]{:S(2)}, u32[]{:S(2)}) async-start(bf16[8,36,1152]{2,1,0:T(8,128)(2,1)} %broadcast_in_dim.13), calls=%async_computation.3 | async-start | bytes 1474560 | tf_op jit(solution)/shard_map/all_to_all | solution.py:30
  132.4 2.5 %collective-permute-start.6 = (bf16[128,576]{1,0:T(8,128)(2,1)S(1)}, bf16[128,576]{1,0:T(8,128)(2,1)S(1)}, u32[]{:S(2)}, u32[]{:S(2)}) collective-permute-start(bf16[128,576]{1,0:T(8,128)(2,1)S(1)} %broadcast_select_fusion), channel_id=1, source_target_pairs={{0,1},{1,0},{2,3},{3,2},{4,5},{5,4},{6,7},{7,6},{8,9},{9,8},{10,11... | collective-permute-start | bytes 442376 | tf_op jit(solution)/shard_map/ppermute | solution.py:179
  134.9 3.2 %collective-permute-done.6 = bf16[128,576]{1,0:T(8,128)(2,1)S(1)} collective-permute-done((bf16[128,576]{1,0:T(8,128)(2,1)S(1)}, bf16[128,576]{1,0:T(8,128)(2,1)S(1)}, u32[]{:S(2)}, u32[]{:S(2)}) %collective-permute-start.6) | collective-permute-done | bytes 147488 | tf_op jit(solution)/shard_map/ppermute | solution.py:179
  139.4 2.5 %collective-permute-start.7 = (f32[128]{0:T(128)S(1)}, f32[128]{0:T(128)S(1)}, u32[]{:S(2)}, u32[]{:S(2)}) collective-permute-start(f32[128]{0:T(128)S(1)} %multiply_reduce_fusion), channel_id=1, source_target_pairs={{0,1},{1,0},{2,3},{3,2},{4,5},{5,4},{6,7},{7,6},{8,9},{9,8},{10,11... | collective-permute-start | bytes 1544 | tf_op jit(solution)/shard_map/ppermute | solution.py:183
  141.9 10.0 %all-to-all-done.3 = bf16[8,36,1152]{2,1,0:T(8,128)(2,1)S(1)} async-done(((bf16[8,36,1152]{2,1,0:T(8,128)(2,1)}), bf16[8,36,1152]{2,1,0:T(8,128)(2,1)S(1)}, u32[]{:S(2)}, u32[]{:S(2)}) %all-to-all-start.3) | async-done | bytes 663584 | tf_op jit(solution)/shard_map/all_to_all | solution.py:30
  153.0 4.6 %all-to-all-start.4 = ((bf16[8,36,1152]{2,1,0:T(8,128)(2,1)}), bf16[8,36,1152]{2,1,0:T(8,128)(2,1)S(1)}, u32[]{:S(2)}, u32[]{:S(2)}) async-start(bf16[8,36,1152]{2,1,0:T(8,128)(2,1)} %broadcast_in_dim.14), calls=%async_computation.5 | async-start | bytes 1474560 | tf_op jit(solution)/shard_map/all_to_all | solution.py:30
  159.1 9.4 %all-to-all-done.4 = bf16[8,36,1152]{2,1,0:T(8,128)(2,1)S(1)} async-done(((bf16[8,36,1152]{2,1,0:T(8,128)(2,1)}), bf16[8,36,1152]{2,1,0:T(8,128)(2,1)S(1)}, u32[]{:S(2)}, u32[]{:S(2)}) %all-to-all-start.4) | async-done | bytes 663584 | tf_op jit(solution)/shard_map/all_to_all | solution.py:30
  168.6 2.0 %collective-permute-start.8 = (bf16[288,1152]{1,0:T(8,128)(2,1)S(1)}, bf16[288,1152]{1,0:T(8,128)(2,1)S(1)}, u32[]{:S(2)}, u32[]{:S(2)}) collective-permute-start(bf16[288,1152]{1,0:T(8,128)(2,1)S(1)} %reshape.42.mine), channel_id=1, source_target_pairs={{0,2},{2,0},{1,3},{3,1},{4,6},{6,4},{5,7},{7,5},{8,10},{10,8},{9,1... | collective-permute-start | bytes 1990664 | tf_op jit(solution)/shard_map/ppermute | solution.py:189
  172.3 1.7 shard_map.71
  (63 shorter events, 19.0 us)
Async XLA Ops:
  7.2 5.1 %copy-start = (bf16[576,1152]{1,0:T(8,128)(2,1)S(1)}, bf16[576,1152]{1,0:T(8,128)(2,1)}, u32[]{:S(2)}) copy-start(bf16[576,1152]{1,0:T(8,128)(2,1)} %param.6) | copy-start | bytes 3981316
  7.2 53.2 %all-gather.2.cloned.1.call-start = ((), (), s32[]{:S(2)}) async-start(), calls=%async_computation.6 | async-start | bytes 2949120 | tf_op jit(solution)/shard_map/all_gather | solution.py:129
  8.4 5.2 %copy-start.10 = (s32[128]{0:T(128)S(1)}, s32[128]{0:T(128)}, u32[]{:S(2)}) copy-start(s32[128]{0:T(128)} %param.7) | copy-start | bytes 1540
  8.4 6.7 %collective-permute-start = (bf16[128,576]{1,0:T(8,128)(2,1)S(1)}, bf16[128,576]{1,0:T(8,128)(2,1)S(1)}, u32[]{:S(2)}, u32[]{:S(2)}) collective-permute-start(bf16[128,576]{1,0:T(8,128)(2,1)S(1)} %copy.32), channel_id=1, source_target_pairs={{0,1},{1,0},{2,3},{3,2},{4,5},{5,4},{6,7},{7,6},{8,9},{9,8},{10,11... | collective-permute-start | bytes 442376 | tf_op jit(solution)/shard_map/ppermute | solution.py:115
  16.3 6.3 %collective-permute-start.1 = (bf16[64,1152]{1,0:T(8,128)(2,1)S(1)}, bf16[64,1152]{1,0:T(8,128)(2,1)S(1)}, u32[]{:S(2)}, u32[]{:S(2)}) collective-permute-start(bf16[64,1152]{1,0:T(8,128)(2,1)S(1)} %select_convert_fusion.1), channel_id=1, source_target_pairs={{0,1},{1,0},{2,3},{3,2},{4,5},{5,4},{6,7},{7,6},{8,9},{9,8},{10,11... | collective-permute-start | bytes 442376 | tf_op jit(solution)/shard_map/ppermute | solution.py:119
  43.0 28.3 %copy-start.2 = (bf16[8,64,1280]{2,1,0:T(8,128)(2,1)}, bf16[8,64,1280]{2,1,0:T(8,128)(2,1)S(1)}, u32[]{:S(2)}) copy-start(bf16[8,64,1280]{2,1,0:T(8,128)(2,1)S(1)} %all_to_all.25) | copy-start | bytes 3932164
  43.0 6.8 %collective-permute-start.2 = (bf16[512,1280]{1,0:T(8,128)(2,1)S(1)}, bf16[512,1280]{1,0:T(8,128)(2,1)}, u32[]{:S(2)}, u32[]{:S(2)}) collective-permute-start(bf16[512,1280]{1,0:T(8,128)(2,1)S(1)} %bitcast.16), channel_id=1, source_target_pairs={{0,2},{2,0},{1,3},{3,1},{4,6},{6,4},{5,7},{7,5},{8,10},{10,8},{9,1... | collective-permute-start | bytes 3932168 | tf_op jit(solution)/shard_map/ppermute | solution.py:132
  60.4 1.7 copy-start.4
  66.6 1.0 copy-start.5
  67.6 8.4 %collective-permute-start.3 = (bf16[8,64,1152]{2,1,0:T(8,128)(2,1)S(1)}, bf16[8,64,1152]{2,1,0:T(8,128)(2,1)S(1)}, u32[]{:S(2)}, u32[]{:S(2)}) collective-permute-start(bf16[8,64,1152]{2,1,0:T(8,128)(2,1)S(1)} %get-tuple-element.17), channel_id=1, source_target_pairs={{0,2},{2,0},{1,3},{3,1},{4,6},{6,4},{5,7},{7,5},{8,10},{10,8},{9,1... | collective-permute-start | bytes 3538952 | tf_op jit(solution)/shard_map/ppermute | solution.py:153
  75.1 1.0 copy-start.7
  77.4 23.3 %all-to-all-start.1 = ((bf16[8,64,1152]{2,1,0:T(8,128)(2,1)}), bf16[8,64,1152]{2,1,0:T(8,128)(2,1)S(1)}, u32[]{:S(2)}, u32[]{:S(2)}) async-start(bf16[8,64,1152]{2,1,0:T(8,128)(2,1)} %add_convert_fusion), calls=%async_computation.1 | async-start | bytes 2359296 | tf_op jit(solution)/shard_map/all_to_all | solution.py:156
  82.2 49.1 %reduce-scatter.2.cloned.1.call-start = ((), (), s32[]{:S(2)}) async-start(), calls=%async_computation.7 | async-start | bytes 2654208 | tf_op jit(solution)/shard_map/reduce_scatter | solution.py:161
  82.4 1.3 copy-start.3
  83.7 1.2 copy-start.6
  84.9 1.2 copy-start.8
  90.4 1.4 copy-start.1
  101.0 5.6 %collective-permute-start.4 = (bf16[64,1152]{1,0:T(8,128)(2,1)S(1)}, bf16[64,1152]{1,0:T(8,128)(2,1)S(1)}, u32[]{:S(2)}, u32[]{:S(2)}) collective-permute-start(bf16[64,1152]{1,0:T(8,128)(2,1)S(1)} %shard_map.69), channel_id=1, source_target_pairs={{0,1},{1,0},{2,3},{3,2},{4,5},{5,4},{6,7},{7,6},{8,9},{9,8},{10,11... | collective-permute-start | bytes 442376 | tf_op jit(solution)/shard_map/ppermute | solution.py:164
  108.1 4.1 %collective-permute-start.5 = (bf16[288,1152]{1,0:T(8,128)(2,1)S(1)}, bf16[288,1152]{1,0:T(8,128)(2,1)S(1)}, u32[]{:S(2)}, u32[]{:S(2)}) collective-permute-start(bf16[288,1152]{1,0:T(8,128)(2,1)S(1)} %select_convert_fusion), channel_id=1, source_target_pairs={{0,2},{2,0},{1,3},{3,1},{4,6},{6,4},{5,7},{7,5},{8,10},{10,8},{9,1... | collective-permute-start | bytes 1990664 | tf_op jit(solution)/shard_map/ppermute | solution.py:172
  127.2 24.8 %all-to-all-start.3 = ((bf16[8,36,1152]{2,1,0:T(8,128)(2,1)}), bf16[8,36,1152]{2,1,0:T(8,128)(2,1)S(1)}, u32[]{:S(2)}, u32[]{:S(2)}) async-start(bf16[8,36,1152]{2,1,0:T(8,128)(2,1)} %broadcast_in_dim.13), calls=%async_computation.3 | async-start | bytes 1474560 | tf_op jit(solution)/shard_map/all_to_all | solution.py:30
  132.4 5.8 %collective-permute-start.6 = (bf16[128,576]{1,0:T(8,128)(2,1)S(1)}, bf16[128,576]{1,0:T(8,128)(2,1)S(1)}, u32[]{:S(2)}, u32[]{:S(2)}) collective-permute-start(bf16[128,576]{1,0:T(8,128)(2,1)S(1)} %broadcast_select_fusion), channel_id=1, source_target_pairs={{0,1},{1,0},{2,3},{3,2},{4,5},{5,4},{6,7},{7,6},{8,9},{9,8},{10,11... | collective-permute-start | bytes 442376 | tf_op jit(solution)/shard_map/ppermute | solution.py:179
  139.4 12.7 %collective-permute-start.7 = (f32[128]{0:T(128)S(1)}, f32[128]{0:T(128)S(1)}, u32[]{:S(2)}, u32[]{:S(2)}) collective-permute-start(f32[128]{0:T(128)S(1)} %multiply_reduce_fusion), channel_id=1, source_target_pairs={{0,1},{1,0},{2,3},{3,2},{4,5},{5,4},{6,7},{7,6},{8,9},{9,8},{10,11... | collective-permute-start | bytes 1544 | tf_op jit(solution)/shard_map/ppermute | solution.py:183
  153.0 15.4 %all-to-all-start.4 = ((bf16[8,36,1152]{2,1,0:T(8,128)(2,1)}), bf16[8,36,1152]{2,1,0:T(8,128)(2,1)S(1)}, u32[]{:S(2)}, u32[]{:S(2)}) async-start(bf16[8,36,1152]{2,1,0:T(8,128)(2,1)} %broadcast_in_dim.14), calls=%async_computation.5 | async-start | bytes 1474560 | tf_op jit(solution)/shard_map/all_to_all | solution.py:30
  157.6 1.2 copy-start.9
  168.6 3.7 %collective-permute-start.8 = (bf16[288,1152]{1,0:T(8,128)(2,1)S(1)}, bf16[288,1152]{1,0:T(8,128)(2,1)S(1)}, u32[]{:S(2)}, u32[]{:S(2)}) collective-permute-start(bf16[288,1152]{1,0:T(8,128)(2,1)S(1)} %reshape.42.mine), channel_id=1, source_target_pairs={{0,2},{2,0},{1,3},{3,1},{4,6},{6,4},{5,7},{7,5},{8,10},{10,8},{9,1... | collective-permute-start | bytes 1990664 | tf_op jit(solution)/shard_map/ppermute | solution.py:189
Sparse Core Ops, SparseCore 0:
  16.4 43.9 all-gather.1
  92.0 36.9 reduce-scatter.1
